TPU v7x, 128 devices: a whole 4x4x4 slice. The times are simulated.
128 devices in a mesh: tm: 16 (over x, z), batch: 8 (over y, core).
Axes of the slice: x: 4, y: 4, z: 4, core: 2. Of those that a mesh axis runs over, the one named last changes fastest.
Arguments:
- state: float32 [16, 8, 256, 1152], P('tm', 'batch'), may hold values from -6 to 6
- noise_draws: bfloat16 [2, 16, 8, 256, 1152], P(None, 'tm', 'batch'), may hold values from -6 to 6
- class_vec: float32 [8, 1152], P('batch'), may hold values from -6 to 6
- window_start: int32 [8], P('batch'), may hold values from 0 to 977
- advance: int32 [8], P('batch'), may hold values from 1 to 7
- step_dt: float32 [1000], replicated, may hold values from 0.05 to 0.2
- step_sigma: float32 [1000], replicated, may hold values from 0.05 to 0.2
- w_ada: bfloat16 [1152, 3456], replicated, may hold values from -0.1875 to 0.1875
- w_up: bfloat16 [4608, 1152], P(('tm', 'batch')), may hold values from -0.1875 to 0.1875
- w_down: bfloat16 [4608, 1152], P(('tm', 'batch')), may hold values from -0.09375 to 0.09375
Outputs:
- window_out: float32 [16, 8, 256, 1152], P('tm', 'batch')
All inputs are finite; a program needn't handle non-finite values.
Results may differ from a plain program's by a relative error of at most 0.0037.
Values may be sent and summed in bfloat16 or wider, within the bound.
No kernel may reach another device: no remote copies, remote signals or barrier semaphores. Data moves between devices by JAX's collectives and lax.ppermute only.
A program may use at most 128 MiB of HBM per device.

v0:
```python
import math

import jax
import jax.numpy as jnp
from jax import lax
from jax.sharding import PartitionSpec as P

SLIDE_BITS = 3


EPSILON = 1e-06


def spread_2(shard, axis, root):
    mine = lax.axis_index(axis) == root
    return lax.psum(jnp.where(mine, shard, jnp.zeros_like(shard)), axis)


def carried_in(part, axis, combine, identity):
    place = lax.axis_index(axis)
    gathered = lax.all_gather(part, axis)
    state = jnp.zeros_like(part) + jnp.asarray(identity, part.dtype)

    def one(turn, state):
        return combine(state, lax.dynamic_index_in_dim(gathered, turn, 0, False))

    return lax.fori_loop(0, place, one, state)


def from_behind(shard, axis, by):
    peers = lax.axis_size(axis)
    pairs = [(i, i + by) for i in range(peers) if 0 <= i + by < peers]
    return lax.ppermute(shard, axis, pairs)


def time_embed(steps_now, half_width):
    frequency = jnp.exp(-math.log(10000.0) * jnp.arange(half_width, dtype=jnp.float32) / half_width)
    angles = steps_now.astype(jnp.float32)[:, None] * frequency[None, :]
    return jnp.concatenate([jnp.cos(angles), jnp.sin(angles)], axis=1)


def dense_pair(hidden_rows, up_rows, down_rows):
    before = lax.dot_general(
        hidden_rows, up_rows, (((1,), (1,)), ((), ())), preferred_element_type=jnp.float32
    )
    activated = jax.nn.gelu(before, approximate=True).astype(jnp.bfloat16)
    return jnp.dot(activated, down_rows, preferred_element_type=jnp.float32)


def combine_sum(earlier, later):
    return earlier + later


def increment(current, noise_now, steps_now, class_vec, step_dt, step_sigma, w_ada, mlp_apply):
    images, tokens, channels = current.shape
    step_table = lax.iota(jnp.int32, step_dt.shape[0])
    onehot = (steps_now[:, None] == step_table[None, :]).astype(jnp.float32)
    step_size = jnp.sum(onehot * step_dt[None, :], axis=1)
    spread = jnp.sum(onehot * step_sigma[None, :], axis=1)
    condition = jax.nn.silu(time_embed(steps_now, channels // 2) + class_vec).astype(jnp.bfloat16)
    modulation = jnp.dot(condition, w_ada, preferred_element_type=jnp.float32)
    shift_by = modulation[:, :channels]
    scale_by = modulation[:, channels : 2 * channels]
    gate_by = modulation[:, 2 * channels :]
    mean_val = jnp.mean(current, axis=2, keepdims=True)
    centred = current - mean_val
    var_val = jnp.mean(centred * centred, axis=2, keepdims=True)
    normed = centred * lax.rsqrt(var_val + EPSILON)
    hidden_in = (normed * (1.0 + scale_by[:, None, :]) + shift_by[:, None, :]).astype(jnp.bfloat16)
    mlp_out = mlp_apply(hidden_in.reshape(images * tokens, channels)).reshape(
        images, tokens, channels
    )
    drift = gate_by[:, None, :] * mlp_out - current
    return step_size[:, None, None] * drift + spread[:, None, None] * noise_now.astype(jnp.float32)


def per_device(
    state, noise_draws, class_vec, window_start, advance, step_dt, step_sigma, w_ada, w_up, w_down
):
    window_size = lax.axis_size("tm")
    position = lax.axis_index("tm")
    up_whole, down_whole = (
        lax.all_gather(w_up, ("tm", "batch"), axis=0, tiled=True),
        lax.all_gather(w_down, ("tm", "batch"), axis=0, tiled=True),
    )

    def mlp_apply(hidden_rows):
        return dense_pair(hidden_rows, up_whole, down_whole)

    def sweep(current, noise_now, starts):
        steps_now = starts + position
        step_inc = increment(
            current, noise_now, steps_now, class_vec, step_dt, step_sigma, w_ada, mlp_apply
        )
        base_rows = spread_2(current, "tm", 0)
        prefix = carried_in(step_inc, "tm", combine_sum, jnp.zeros_like(step_inc))
        updated = base_rows + prefix
        return (updated, step_inc)

    updated, step_inc = sweep(state[0], noise_draws[0, 0], window_start)
    end_rows = updated + step_inc
    tail_rows = jnp.where(position == window_size - 1, end_rows, jnp.zeros_like(end_rows))
    moved = updated
    for section_bit in range(SLIDE_BITS):
        distance = 1 << section_bit
        arrived, arrived_tail = from_behind((moved, tail_rows), "tm", -distance)
        taken = advance >> section_bit & 1 == 1
        outside = position + distance >= window_size
        incoming = jnp.where(outside, tail_rows, arrived)
        moved = jnp.where(taken[:, None, None], incoming, moved)
        tail_rows = jnp.where(position >= window_size - distance, tail_rows, arrived_tail)
    final_rows, leftover = sweep(moved, noise_draws[1, 0], window_start + advance)
    return final_rows[None]


def solution(mesh):
    in_specs = (
        P("tm", "batch", None, None),
        P(None, "tm", "batch", None, None),
        P("batch", None),
        P("batch"),
        P("batch"),
        P(),
        P(),
        P(),
        P(("tm", "batch"), None),
        P(("tm", "batch"), None),
    )
    out_specs = P("tm", "batch", None, None)
    return jax.shard_map(
        per_device, mesh=mesh, in_specs=in_specs, out_specs=out_specs, check_vma=False
    )
```

profile of v0, /device:TPU:0, one launch (start us, length us, event | category | flops | bytes accessed | tf_op | source)
XLA Modules:
  0.0 791.6 jit_solution(7158159004411722302)
XLA Ops:
  6.5 0.0 copy-start.9
  6.5 0.0 copy-start.6
  6.5 0.0 all-gather.15.cloned.1.call-start
  6.5 0.7 all-gather.15.cloned.1.call-update
  7.3 0.0 all-gather.13.cloned.1.call-start
  7.3 0.7 all-gather.13.cloned.1.call-update
  8.0 0.0 all-gather.9.cloned.1.call-start
  9.4 1.4 reduce_sum.73
  10.8 0.1 fusion.87
  10.9 0.0 copy-done.8
  10.9 0.0 copy-done.9
  10.9 0.7 select_reduce_fusion
  11.6 0.0 copy-done.6
  11.6 4.5 fusion.73
  16.2 0.0 copy-done.1
  16.2 1.2 fusion.39
  17.4 68.0 %all-gather.15.cloned.1.call-done = bf16[128,36,1152]{2,1,0:T(8,128)(2,1)} async-done(((bf16[1,36,1152]{2,1,0:T(8,128)(2,1)}), bf16[128,36,1152]{2,1,0:T(8,128)(2,1)}) %all-gather.15.cloned.1.call-update) | async-done | bytes 10616848 | tf_op jit(solution)/shard_map/all_gather | solution.py:84
  85.3 16.3 %reshape.304 = bf16[4608,1152]{1,0:T(8,128)(2,1)} reshape(bf16[128,36,1152]{2,1,0:T(8,128)(2,1)} %all-gather.15.cloned.1.call-done) | data formatting | bytes 21233664
  101.6 58.2 %all-gather.13.cloned.1.call-done = bf16[128,36,1152]{2,1,0:T(8,128)(2,1)} async-done(((bf16[1,36,1152]{2,1,0:T(8,128)(2,1)}), bf16[128,36,1152]{2,1,0:T(8,128)(2,1)}) %all-gather.13.cloned.1.call-update) | async-done | bytes 10616848 | tf_op jit(solution)/shard_map/all_gather | solution.py:83
  159.9 16.3 %reshape.302 = bf16[4608,1152]{1,0:T(8,128)(2,1)} reshape(bf16[128,36,1152]{2,1,0:T(8,128)(2,1)} %all-gather.13.cloned.1.call-done) | data formatting | bytes 21233664
  176.2 0.0 copy-done.10
  176.2 15.8 %fusion.18 = f32[256,1152]{1,0:T(8,128)} fusion(bf16[4608,1152]{1,0:T(8,128)(2,1)} %reshape.304, f32[1,1,256,1152]{3,2,1,0:T(8,128)S(1)} %copy-done.1, bf16[4608,1152]{1,0:T(8,128)(2,1)} %reshape.302, bf16[2,1,1,256,1152]{4,3,2,1,0:T(8,128)(2,1)S(1)} %copy-done.10, f32[]{:T(128)} %get-tuple-element.86, f32[1152]{0:T(1024)S(1)} %get-tuple-element.82, ...), kind=kOutput, calls=%fused_computation.24 | convolution fusion | flops 5449678848 | bytes 25389064 | tf_op jit(solution)/shard_map/dot_general | solution.py:47
  192.0 0.0 all-gather.9.cloned.1.call-update
  192.0 0.0 all-reduce.3.cloned.1.call-start
  192.1 0.5 all-reduce.3.cloned.1.call-update
  192.6 0.0 all-gather.11.cloned.1.call-start
  192.6 120.7 %all-gather.9.cloned.1.call-done = f32[4096,1152]{1,0:T(8,128)} async-done(((f32[256,1152]{1,0:T(8,128)}), f32[4096,1152]{1,0:T(8,128)}) %all-gather.9.cloned.1.call-update) | async-done | bytes 18874384 | tf_op jit(solution)/shard_map/all_gather | solution.py:21
  313.3 0.1 broadcast.231.clone
  313.4 89.8 %all-reduce.3.cloned.1.call-done = f32[1,256,1152]{2,1,0:T(8,128)} async-done(((f32[1,256,1152]{2,1,0:T(8,128)}), f32[1,256,1152]{2,1,0:T(8,128)}) %all-reduce.3.cloned.1.call-update) | async-done | bytes 1179664 | tf_op jit(solution)/shard_map/psum | solution.py:16
  403.2 1.5 add.160
  404.7 1.3 collective-permute-start.2
  406.0 26.8 %collective-permute-done.2 = f32[1,256,1152]{2,1,0:T(8,128)S(1)} collective-permute-done((f32[1,256,1152]{2,1,0:T(8,128)S(1)}, f32[1,256,1152]{2,1,0:T(8,128)S(1)}, u32[]{:S(2)}, u32[]{:S(2)}) %collective-permute-start.2) | collective-permute-done | bytes 1179680 | tf_op jit(solution)/shard_map/ppermute | solution.py:33
  432.8 1.0 copy-done.2
  433.8 0.0 copy-done
  433.9 2.5 select_select_fusion.2
  436.3 1.3 collective-permute-start.3
  437.6 1.3 collective-permute-start
  438.9 26.1 %collective-permute-done.3 = f32[1,256,1152]{2,1,0:T(8,128)S(1)} collective-permute-done((f32[1,256,1152]{2,1,0:T(8,128)S(1)}, f32[1,256,1152]{2,1,0:T(8,128)S(1)}, u32[]{:S(2)}, u32[]{:S(2)}) %collective-permute-start.3) | collective-permute-done | bytes 1179680 | tf_op jit(solution)/shard_map/ppermute | solution.py:33
  465.0 25.3 %collective-permute-done = f32[1,256,1152]{2,1,0:T(8,128)S(1)} collective-permute-done((f32[1,256,1152]{2,1,0:T(8,128)}, f32[1,256,1152]{2,1,0:T(8,128)S(1)}, u32[]{:S(2)}, u32[]{:S(2)}) %collective-permute-start) | collective-permute-done | bytes 1179680 | tf_op jit(solution)/shard_map/ppermute | solution.py:33
  490.3 0.0 copy-done.4
  490.3 1.0 copy-done.5
  491.4 1.9 select_select_fusion.1
  493.2 1.3 collective-permute-start.4
  494.5 1.5 collective-permute-start.1
  496.0 0.1 fusion.85
  496.1 4.4 fusion.71
  500.5 0.6 slice_reduce_fusion.1
  501.2 22.9 %collective-permute-done.4 = f32[1,256,1152]{2,1,0:T(8,128)S(1)} collective-permute-done((f32[1,256,1152]{2,1,0:T(8,128)S(1)}, f32[1,256,1152]{2,1,0:T(8,128)S(1)}, u32[]{:S(2)}, u32[]{:S(2)}) %collective-permute-start.4) | collective-permute-done | bytes 1179680 | tf_op jit(solution)/shard_map/ppermute | solution.py:33
  524.1 0.7 collective-permute-done.1
  524.8 0.3 copy-done.3
  525.1 1.9 fusion.101
  527.0 0.0 copy-start.7
  527.0 0.0 copy-start.11
  527.0 1.2 multiply_reduce_fusion
  528.2 0.0 copy-done.7
  528.2 0.4 copy-done.11
  528.6 15.9 %fusion.22 = f32[1,256,1152]{2,1,0:T(8,128)} fusion(f32[1,256,1152]{2,1,0:T(8,128)S(1)} %get-tuple-element.104, bf16[4608,1152]{1,0:T(8,128)(2,1)} %reshape.304, bf16[4608,1152]{1,0:T(8,128)(2,1)} %reshape.302, bf16[2,1,1,256,1152]{4,3,2,1,0:T(8,128)(2,1)S(1)} %copy-done.11, f32[]{:T(128)} %get-tuple-element.85, f32[1152]{0:T(1024)S(1)} %copy-done.7, ...), kind=kOutput, calls=%fused_computation.28 | convolution fusion | flops 5449678848 | bytes 25389064 | tf_op jit(solution)/shard_map/dot_general | solution.py:47
  544.5 0.0 all-gather.11.cloned.1.call-update
  544.5 0.0 all-reduce.5.cloned.1.call-start
  544.6 0.5 all-reduce.5.cloned.1.call-update
  545.1 147.3 %all-gather.11.cloned.1.call-done = f32[16,256,1152]{2,1,0:T(8,128)} async-done(((f32[1,256,1152]{2,1,0:T(8,128)}), f32[16,256,1152]{2,1,0:T(8,128)}) %all-gather.11.cloned.1.call-update) | async-done | bytes 18874384 | tf_op jit(solution)/shard_map/all_gather | solution.py:21
  692.4 0.1 broadcast.231
  692.5 89.8 %all-reduce.5.cloned.1.call-done = f32[1,256,1152]{2,1,0:T(8,128)} async-done(((f32[1,256,1152]{2,1,0:T(8,128)}), f32[1,256,1152]{2,1,0:T(8,128)}) %all-reduce.5.cloned.1.call-update) | async-done | bytes 1179664 | tf_op jit(solution)/shard_map/psum | solution.py:16
  782.3 2.4 add_bitcast_fusion
  (15 shorter events, 0.1 us)
Async XLA Ops:
  6.5 4.3 copy-start.8
  6.5 4.3 copy-start.9
  6.5 5.0 copy-start.6
  6.5 78.8 %all-gather.15.cloned.1.call-start = ((), (), s32[]{:S(2)}) async-start(), calls=%async_computation.5 | async-start | bytes 11888640 | tf_op jit(solution)/shard_map/all_gather | solution.py:84
  7.3 152.6 %all-gather.13.cloned.1.call-start = ((), (), s32[]{:S(2)}) async-start(), calls=%async_computation.4 | async-start | bytes 11888640 | tf_op jit(solution)/shard_map/all_gather | solution.py:83
  8.0 305.3 %all-gather.9.cloned.1.call-start = ((), (), s32[]{:S(2)}) async-start(), calls=%async_computation.2 | async-start | bytes 20054016 | tf_op jit(solution)/shard_map/all_gather | solution.py:21
  11.6 4.6 copy-start.1
  101.6 74.6 %copy-start.10 = (bf16[2,1,1,256,1152]{4,3,2,1,0:T(8,128)(2,1)S(1)}, bf16[2,1,1,256,1152]{4,3,2,1,0:T(8,128)(2,1)}, u32[]{:S(2)}) copy-start(bf16[2,1,1,256,1152]{4,3,2,1,0:T(8,128)(2,1)} %param.15) | copy-start | bytes 3538948
  192.0 211.2 %all-reduce.3.cloned.1.call-start = ((), (), s32[]{:S(2)}) async-start(), calls=%async_computation | async-start | bytes 2359296 | tf_op jit(solution)/shard_map/psum | solution.py:16
  192.6 499.8 %all-gather.11.cloned.1.call-start = ((), (), s32[]{:S(2)}) async-start(), calls=%async_computation.3 | async-start | bytes 20054016 | tf_op jit(solution)/shard_map/all_gather | solution.py:21
  403.2 30.6 %copy-start = (f32[256,1152]{1,0:T(8,128)S(1)}, f32[256,1152]{1,0:T(8,128)}, u32[]{:S(2)}) copy-start(f32[256,1152]{1,0:T(8,128)} %fusion.18) | copy-start | bytes 3538948
  404.7 28.1 %collective-permute-start.2 = (f32[1,256,1152]{2,1,0:T(8,128)S(1)}, f32[1,256,1152]{2,1,0:T(8,128)S(1)}, u32[]{:S(2)}, u32[]{:S(2)}) collective-permute-start(f32[1,256,1152]{2,1,0:T(8,128)S(1)} %add.160), channel_id=1, source_target_pairs={{8,0},{16,8},{24,16},{32,24},{40,32},{48,40},{56,48},{64,56},{72,6... | collective-permute-start | bytes 3538952 | tf_op jit(solution)/shard_map/ppermute | solution.py:33
  432.8 1.0 copy-start.2
  436.3 28.7 %collective-permute-start.3 = (f32[1,256,1152]{2,1,0:T(8,128)S(1)}, f32[1,256,1152]{2,1,0:T(8,128)S(1)}, u32[]{:S(2)}, u32[]{:S(2)}) collective-permute-start(f32[1,256,1152]{2,1,0:T(8,128)S(1)} %get-tuple-element.107), channel_id=1, source_target_pairs={{16,0},{24,8},{32,16},{40,24},{48,32},{56,40},{64,48},{72,56},{80,... | collective-permute-start | bytes 3538952 | tf_op jit(solution)/shard_map/ppermute | solution.py:33
  437.6 52.7 %collective-permute-start = (f32[1,256,1152]{2,1,0:T(8,128)}, f32[1,256,1152]{2,1,0:T(8,128)S(1)}, u32[]{:S(2)}, u32[]{:S(2)}) collective-permute-start(f32[1,256,1152]{2,1,0:T(8,128)} %get-tuple-element.108), channel_id=1, source_target_pairs={{8,0},{16,8},{24,16},{32,24},{40,32},{48,40},{56,48},{64,56},{72,6... | collective-permute-start | bytes 3538952 | tf_op jit(solution)/shard_map/ppermute | solution.py:33
  465.0 25.3 %copy-start.4 = (f32[1,256,1152]{2,1,0:T(8,128)}, f32[1,256,1152]{2,1,0:T(8,128)S(1)}, u32[]{:S(2)}) copy-start(f32[1,256,1152]{2,1,0:T(8,128)S(1)} %collective-permute-done.3) | copy-start | bytes 3538948
  490.3 1.1 copy-start.5
  493.2 30.8 %collective-permute-start.4 = (f32[1,256,1152]{2,1,0:T(8,128)S(1)}, f32[1,256,1152]{2,1,0:T(8,128)S(1)}, u32[]{:S(2)}, u32[]{:S(2)}) collective-permute-start(f32[1,256,1152]{2,1,0:T(8,128)S(1)} %get-tuple-element.105), channel_id=1, source_target_pairs={{32,0},{40,8},{48,16},{56,24},{64,32},{72,40},{80,48},{88,56},{96,... | collective-permute-start | bytes 3538952 | tf_op jit(solution)/shard_map/ppermute | solution.py:33
  494.5 30.3 %collective-permute-start.1 = (f32[1,256,1152]{2,1,0:T(8,128)S(1)}, f32[1,256,1152]{2,1,0:T(8,128)}, u32[]{:S(2)}, u32[]{:S(2)}) collective-permute-start(f32[1,256,1152]{2,1,0:T(8,128)S(1)} %get-tuple-element.106), channel_id=1, source_target_pairs={{16,0},{24,8},{32,16},{40,24},{48,32},{56,40},{64,48},{72,56},{80,... | collective-permute-start | bytes 3538952 | tf_op jit(solution)/shard_map/ppermute | solution.py:33
  524.1 1.0 copy-start.3
  527.0 1.2 copy-start.7
  527.0 1.6 copy-start.11
  544.5 237.8 %all-reduce.5.cloned.1.call-start = ((), (), s32[]{:S(2)}) async-start(), calls=%async_computation.1 | async-start | bytes 2359296 | tf_op jit(solution)/shard_map/psum | solution.py:16
Sparse Core Ops, SparseCore 0:
  10.3 74.9 all-gather.14
  88.3 71.5 all-gather.12
  192.1 121.1 all-gather.8
  316.5 86.6 all-reduce.2
  544.6 147.7 all-gather.10
  695.6 86.6 all-reduce.4
where the time goes:
time: 794 us; the launch traced here: 792 us
  waiting for transfers between devices  678 us (85%)
  matrix products  40.6 us (5%)
  local copies, waits for them, and re-layouts  35.5 us (4%)
  other arithmetic  15.6 us (2%)
  between operations  15 us (2%)
    all_gather x2, waiting for transfers between devices, carried_in(): gathered = lax.all_gather(part, axis)  268 us
    psum x2, waiting for transfers between devices, spread_2(): return lax.psum(jnp.where(mine, shard, jnp.zeros_like(shard)), axis)  180 us
    ppermute x5, waiting for transfers between devices, from_behind(): return lax.ppermute(shard, axis, pairs)  102 us
    all_gather x1, waiting for transfers between devices, per_device(): lax.all_gather(w_down, ('tm', 'batch'), axis=0, tiled=True)  68 us
    all_gather x1, waiting for transfers between devices, per_device(): lax.all_gather(w_up, ('tm', 'batch'), axis=0, tiled=True)  58.2 us
    unnamed x26, local copies, waits for them, and re-layouts  35.3 us
    dot_general x2, matrix products, dense_pair(): return jnp.dot(activated, down_rows, preferred_element_type=jnp.float32)  31.7 us
  transfers between devices with their start and end apart: 11, of which 11 were waited for; matrix products, arithmetic and copies ran while one was open for 4% of the time, Pallas kernels for 0%

commit v1 on v0

v1 whole, which is shorter than its diff:
```python
import functools
import math

import jax
import jax.numpy as jnp
from jax import lax
from jax.experimental import pallas as pl
from jax.experimental.pallas import tpu as pltpu
from jax.sharding import PartitionSpec as P

EPSILON = 1e-06
ALL = ("tm", "batch")
SIDE = 4
CORES = 2
THIRDS = 3
SLIDE = 7
f32, bf16 = jnp.float32, jnp.bfloat16


def device_pairs(move):
    pairs = []
    for x in range(SIDE):
        for z in range(SIDE):
            for y in range(SIDE):
                for core in range(CORES):
                    here, there = (x, z, y, core), move((x, z, y, core))
                    flat = [((p[0] * SIDE + p[1]) * SIDE + p[2]) * CORES + p[3] for p in (here, there)]
                    pairs.append(tuple(flat))
    return pairs


def neighbour(axis, first):
    def move(place):
        place = list(place)
        odd = (place[3] == 0) == first
        place[axis] = place[axis] ^ 1 if odd else SIDE - 1 - place[axis]
        return tuple(place)

    return device_pairs(move)


def send(rows, axis, first):
    return lax.ppermute(rows, ALL, neighbour(axis, first))


def swap_cores(rows):
    return lax.ppermute(rows, ALL, device_pairs(lambda p: (p[0], p[1], p[2], 1 - p[3])))


def grow(rows, axis, core):
    near = send(rows, axis, True)
    both = send(jnp.concatenate([rows, near]), axis, False)
    count = rows.shape[0]
    second, far = both[:count], both[count:]
    low = jnp.where(core == 0, near, second)
    high = jnp.where(core == 0, second, near)
    return jnp.concatenate([rows, low, high, far])


def gelu(before):
    inner = math.sqrt(2.0 / math.pi) * (before + 0.044715 * (before * before * before))
    return 0.5 * before * (1.0 + jnp.tanh(inner))


def copies(side, pairs, up_buf, down_buf, sems, slot):
    made = []
    size = pairs[0][0].shape[0]
    for part, pair in enumerate(pairs):
        place = pl.ds(part * size, size)
        made.append(pltpu.make_async_copy(pair[side], up_buf.at[slot, place], sems.at[slot, 0, part]))
        made.append(
            pltpu.make_async_copy(pair[1 - side], down_buf.at[slot, place], sems.at[slot, 1, part])
        )
    return made


def start_set(core_ref, *where):
    for side in (0, 1):

        @pl.when(core_ref[0] == side)
        def _():
            for copy in copies(side, *where):
                copy.start()


def wait_set(*where):
    for copy in copies(0, *where):
        copy.wait()


def mlp_sets(core_ref, sets, hidden_ref, acc_ref, fresh, up_buf, down_buf, sems):
    for index, pairs in enumerate(sets):
        slot = index % 2
        if index + 1 < len(sets):
            start_set(core_ref, sets[index + 1], up_buf, down_buf, sems, 1 - slot)
        wait_set(pairs, up_buf, down_buf, sems, slot)
        before = lax.dot_general(
            hidden_ref[...], up_buf[slot], (((1,), (1,)), ((), ())), preferred_element_type=f32
        )
        part = jnp.dot(gelu(before).astype(bf16), down_buf[slot], preferred_element_type=f32)
        if fresh and index == 0:
            acc_ref[...] = part
        else:
            acc_ref[...] += part


def as_sets(refs):
    pairs = [(refs[i], refs[i + 1]) for i in range(0, len(refs), 2)]
    return [pairs[i : i + THIRDS] for i in range(0, len(pairs), THIRDS)]


def weight_scratch(units, width, slots):
    return [
        pltpu.VMEM((slots, units, width), bf16),
        pltpu.VMEM((slots, units, width), bf16),
        pltpu.SemaphoreType.DMA((slots, 2, THIRDS)),
    ]


def flat_sets(sets):
    return [array for pairs in sets for pair in pairs for array in pair]


SMEM = pl.BlockSpec(memory_space=pltpu.SMEM)
VMEM = pl.BlockSpec(memory_space=pltpu.VMEM)
ANY = pl.BlockSpec(memory_space=pl.ANY)
PARAMS = pltpu.CompilerParams(vmem_limit_bytes=36 * 2**20)


def piece_kernel(count, fresh, core_ref, hidden_ref, *refs):
    acc_in = None if fresh else refs[0]
    refs = refs if fresh else refs[1:]
    sets = as_sets(refs[:count])
    acc_ref, up_buf, down_buf, sems = refs[count:]
    start_set(core_ref, sets[0], up_buf, down_buf, sems, 0)
    if not fresh:
        acc_ref[...] = acc_in[...]
    mlp_sets(core_ref, sets, hidden_ref, acc_ref, fresh, up_buf, down_buf, sems)


def mlp_piece(core, hidden, acc, sets):
    weights = flat_sets(sets)
    units = THIRDS * weights[0].shape[0]
    fresh = acc is None
    given = [] if fresh else [acc]
    return pl.pallas_call(
        functools.partial(piece_kernel, len(weights), fresh),
        out_shape=jax.ShapeDtypeStruct(hidden.shape, f32),
        in_specs=[SMEM, VMEM] + [VMEM] * len(given) + [ANY] * len(weights),
        out_specs=VMEM,
        scratch_shapes=weight_scratch(units, hidden.shape[1], min(2, len(sets))),
        compiler_params=PARAMS,
        name="mlp_piece",
    )(core, hidden, *given, *weights)


def finish_kernel(
    count, core_ref, first_ref, step_ref, hidden_ref, acc_in, state_ref, noise_ref, later_ref, gate_ref, *refs
):
    sets = as_sets(refs[:count])
    out_ref, acc_ref, up_buf, down_buf, sems = refs[count:]
    start_set(core_ref, sets[0], up_buf, down_buf, sems, 0)
    acc_ref[...] = acc_in[...]
    mlp_sets(core_ref, sets, hidden_ref, acc_ref, False, up_buf, down_buf, sems)
    peers, rows, _ = out_ref.shape
    rows = rows // 3
    gate = gate_ref[...]

    def one(peer, carry):
        place = pl.ds(pl.multiple_of(peer * rows, rows), rows)
        state = state_ref[place, :]
        drift = gate * acc_ref[place, :] - state
        inc = step_ref[0] * drift + step_ref[1] * noise_ref[place, :].astype(f32)
        inc = inc + first_ref[0] * state
        high = inc.astype(bf16)
        out_ref[peer, 0:rows, :] = high
        out_ref[peer, rows : 2 * rows, :] = (inc - high.astype(f32)).astype(bf16)
        out_ref[peer, 2 * rows : 3 * rows, :] = later_ref[place, :]
        return carry

    lax.fori_loop(0, peers, one, 0)


def finish_first(core, is_first, step, hidden, acc, state, noise, later, gate, sets, peers):
    weights = flat_sets(sets)
    units = THIRDS * weights[0].shape[0]
    tokens, width = hidden.shape
    return pl.pallas_call(
        functools.partial(finish_kernel, len(weights)),
        out_shape=jax.ShapeDtypeStruct((peers, 3 * (tokens // peers), width), bf16),
        in_specs=[SMEM] * 3 + [VMEM] * 6 + [ANY] * len(weights),
        out_specs=VMEM,
        scratch_shapes=[pltpu.VMEM((tokens, width), f32)] + weight_scratch(units, width, 1),
        compiler_params=PARAMS,
        name="finish_first",
    )(core, is_first, step, hidden, acc, state, noise, later, gate, *weights)


def second_kernel(count, core_ref, advance_ref, dt_ref, sigma_ref, got_ref, shift_ref, scale_ref, gate_ref, *refs):
    sets = as_sets(refs[:count])
    out_ref, prefix_ref, hidden_ref, acc_ref, up_buf, down_buf, sems = refs[count:]
    start_set(core_ref, sets[0], up_buf, down_buf, sems, 0)
    window, rows, width = out_ref.shape
    advance = advance_ref[0]

    total = jnp.zeros((rows, width), f32)
    for place in range(window):
        inc = got_ref[place, 0:rows, :].astype(f32) + got_ref[place, rows : 2 * rows, :].astype(f32)
        total = total + inc
        prefix_ref[place + 1] = total
    for place in range(window + 1, window + SLIDE):
        prefix_ref[place] = total

    def modulate(place, carry):
        state = prefix_ref[place + advance]
        mean = jnp.mean(state, axis=1, keepdims=True)
        centred = state - mean
        var = jnp.mean(centred * centred, axis=1, keepdims=True)
        normed = centred * lax.rsqrt(var + EPSILON)
        hidden = normed * (1.0 + scale_ref[pl.ds(place, 1), :]) + shift_ref[pl.ds(place, 1), :]
        hidden_ref[pl.ds(pl.multiple_of(place * rows, rows), rows), :] = hidden.astype(bf16)
        return carry

    lax.fori_loop(0, window, modulate, 0)
    mlp_sets(core_ref, sets, hidden_ref, acc_ref, True, up_buf, down_buf, sems)

    def advance_one(place, updated):
        out_ref[place] = updated.astype(bf16)
        state = prefix_ref[place + advance]
        mlp_out = acc_ref[pl.ds(pl.multiple_of(place * rows, rows), rows), :]
        drift = gate_ref[pl.ds(place, 1), :] * mlp_out - state
        noise = got_ref[place, 2 * rows : 3 * rows, :].astype(f32)
        return updated + (dt_ref[place] * drift + sigma_ref[place] * noise)

    lax.fori_loop(0, window, advance_one, prefix_ref[advance])


def second_sweep(core, advance, dt, sigma, got, shift, scale, gate, sets):
    weights = flat_sets(sets)
    units = THIRDS * weights[0].shape[0]
    window, rows, width = got.shape
    rows = rows // 3
    return pl.pallas_call(
        functools.partial(second_kernel, len(weights)),
        out_shape=jax.ShapeDtypeStruct((window, rows, width), bf16),
        in_specs=[SMEM] * 4 + [VMEM] * 4 + [ANY] * len(weights),
        out_specs=VMEM,
        scratch_shapes=[
            pltpu.VMEM((window + SLIDE + 1, rows, width), f32),
            pltpu.VMEM((window * rows, width), bf16),
            pltpu.VMEM((window * rows, width), f32),
        ]
        + weight_scratch(units, width, 2),
        compiler_params=PARAMS,
        name="second_sweep",
    )(core, advance, dt, sigma, got, shift, scale, gate, *weights)


def time_embed(steps_now, half_width):
    frequency = jnp.exp(-math.log(10000.0) * jnp.arange(half_width, dtype=f32) / half_width)
    angles = steps_now.astype(f32)[:, None] * frequency[None, :]
    return jnp.concatenate([jnp.cos(angles), jnp.sin(angles)], axis=1)


def per_device(
    state, noise_draws, class_vec, window_start, advance, step_dt, step_sigma, w_ada, w_up, w_down
):
    window = lax.axis_size("tm")
    position = lax.axis_index("tm")
    core = lax.axis_index("batch") % CORES
    core_arg = core.astype(jnp.int32)[None]
    state, noise_now, noise_later = state[0, 0], noise_draws[0, 0, 0], noise_draws[1, 0, 0]
    tokens, width = state.shape

    other = swap_cores(jnp.where(core == 0, w_down, w_up))
    rows = jnp.where(
        core == 0, jnp.concatenate([w_up, other]), jnp.concatenate([other, w_down])
    )
    third = rows.shape[0] // THIRDS
    parts = [rows[i * third : (i + 1) * third] for i in range(THIRDS)]
    orders = [(0, 1, 2), (1, 2, 0), (2, 0, 1)]
    for phase in range(2):
        parts = [grow(part, order[phase], core) for part, order in zip(parts, orders)]

    last = [order[2] for order in orders]
    first = [send(part, axis, True) for part, axis in zip(parts, last)]
    second = [send(part, axis, False) for part, axis in zip(parts, last)]
    own_swapped = [swap_cores(part) for part in parts]
    far = [send(part, axis, False) for part, axis in zip(first, last)]
    first_swapped = [swap_cores(part) for part in first]
    second_swapped = [swap_cores(part) for part in second]
    far_swapped = [swap_cores(part) for part in far]
    set_own = list(zip(parts, own_swapped))
    set_low = list(zip(first, second_swapped))
    set_high = list(zip(second, first_swapped))
    set_far = list(zip(far, far_swapped))

    begin, ahead = window_start[0], advance[0]
    steps = jnp.concatenate(
        [
            begin + ahead + jnp.arange(window, dtype=jnp.int32),
            jnp.full((8,), begin + position, jnp.int32),
        ]
    )
    condition = jax.nn.silu(time_embed(steps, width // 2) + class_vec).astype(bf16)
    modulation = jnp.dot(condition, w_ada, preferred_element_type=f32)
    shift_by, scale_by, gate_by = (modulation[:, i * width : (i + 1) * width] for i in range(3))
    own = slice(window, window + 1)

    mean = jnp.mean(state, axis=1, keepdims=True)
    centred = state - mean
    var = jnp.mean(centred * centred, axis=1, keepdims=True)
    normed = centred * lax.rsqrt(var + EPSILON)
    hidden = (normed * (1.0 + scale_by[own]) + shift_by[own]).astype(bf16)

    step_now = jnp.stack(
        [
            lax.dynamic_index_in_dim(step_dt, begin + position, 0, False),
            lax.dynamic_index_in_dim(step_sigma, begin + position, 0, False),
        ]
    )
    dt_later = lax.dynamic_slice(step_dt, (begin + ahead,), (window,))
    sigma_later = lax.dynamic_slice(step_sigma, (begin + ahead,), (window,))
    is_first = (position == 0).astype(f32)[None]

    acc = mlp_piece(core_arg, hidden, None, [set_own])
    acc = mlp_piece(core_arg, hidden, acc, [set_low, set_high])
    sent = finish_first(
        core_arg, is_first, step_now, hidden, acc, state, noise_now, noise_later, gate_by[own], [set_far], window
    )
    got = lax.all_to_all(sent, "tm", 0, 0, tiled=True)
    updated = second_sweep(
        core_arg,
        advance,
        dt_later,
        sigma_later,
        got,
        shift_by[:window],
        scale_by[:window],
        gate_by[:window],
        [set_own, set_low, set_high, set_far],
    )
    final = lax.all_to_all(updated, "tm", 0, 0, tiled=True)
    return final.reshape(1, 1, tokens, width).astype(f32)


def solution(mesh):
    in_specs = (
        P("tm", "batch", None, None),
        P(None, "tm", "batch", None, None),
        P("batch", None),
        P("batch"),
        P("batch"),
        P(),
        P(),
        P(),
        P(("tm", "batch"), None),
        P(("tm", "batch"), None),
    )
    out_specs = P("tm", "batch", None, None)
    return jax.shard_map(
        per_device, mesh=mesh, in_specs=in_specs, out_specs=out_specs, check_vma=False
    )
```

time: 794 us -> 198 us (0.25)
  waiting for transfers between devices: 678 us -> 72.5 us
  matrix products: 40.6 us -> 5.29 us
  Pallas kernels: 0 us -> 32.5 us
  starting transfers between devices: 6.83 us -> 35.6 us
  blocking collectives: 0 us -> 17.1 us
  between operations: 15 us -> 1.79 us
  local copies, waits for them, and re-layouts: 35.5 us -> 23.9 us
    all_gather x4 -> x0, waiting for transfers between devices: 394 us -> none  [the longest x2 268 us: carried_in(): gathered = lax.all_gather(part, axis)]
    psum x2 -> x0, waiting for transfers between devices: 180 us -> none  [spread_2(): return lax.psum(jnp.where(mine, shard, jnp.zeros_like(shard)), axis)]
    ppermute x5 -> x34, waiting for transfers between devices: 102 us -> 48.6 us  [the longest x21 47.2 us: send(): return lax.ppermute(rows, ALL, neighbour(axis, first))]
    dot_general x4 -> x1, matrix products: 40.6 us -> 5.29 us  [per_device(): modulation = jnp.dot(condition, w_ada, preferred_element_type=f32)]
    pallas_call x0 -> x4, Pallas kernels: none -> 32.5 us  [the longest x1 15.2 us: second_sweep(): pl.pallas_call(functools.partial(second_kernel, len(weights)), out_shape=...]
    ppermute x5 -> x34, starting transfers between devices: 6.63 us -> 31.1 us  [the longest x21 28.8 us: send(): return lax.ppermute(rows, ALL, neighbour(axis, first))]
    all_to_all x0 -> x1, waiting for transfers between devices: none -> 23.9 us  [per_device(): got = lax.all_to_all(sent, 'tm', 0, 0, tiled=True)]
    unnamed x26 -> x67, local copies, waits for them, and re-layouts: 35.3 us -> 15.6 us
  transfers between devices with their start and end apart: 11 -> 35, of which waited for: 11 -> 11; matrix products, arithmetic and copies ran while one was open for 4% -> 10% of each run, Pallas kernels for 0% -> 5%
where the time goes in v1:
time: 198 us; the launch traced here: 197 us
  waiting for transfers between devices  72.5 us (37%)
  starting transfers between devices  35.6 us (18%)
  Pallas kernels  32.5 us (16%)
  local copies, waits for them, and re-layouts  23.9 us (12%)
  blocking collectives  17.1 us (9%)
  other arithmetic  8.11 us (4%)
  matrix products  5.29 us (3%)
    ppermute x21, waiting for transfers between devices, send(): return lax.ppermute(rows, ALL, neighbour(axis, first))  47.2 us
    ppermute x21, starting transfers between devices, send(): return lax.ppermute(rows, ALL, neighbour(axis, first))  28.8 us
    all_to_all x1, waiting for transfers between devices, per_device(): got = lax.all_to_all(sent, 'tm', 0, 0, tiled=True)  23.9 us
    all_to_all x1, blocking collectives, per_device(): final = lax.all_to_all(updated, 'tm', 0, 0, tiled=True)  17.1 us
    unnamed x67, local copies, waits for them, and re-layouts  15.6 us
    pallas_call x1, Pallas kernels, second_sweep(): pl.pallas_call(functools.partial(second_kernel, len(weights)), out_shape=...  15.2 us
    pallas_call x2, Pallas kernels, mlp_piece(): pl.pallas_call(functools.partial(piece_kernel, len(weights), fresh), out_...  10.5 us
    pallas_call x1, Pallas kernels, finish_first(): pl.pallas_call(functools.partial(finish_kernel, len(weights)), out_shape=...  6.85 us
  transfers between devices with their start and end apart: 35, of which 11 were waited for; matrix products, arithmetic and copies ran while one was open for 10% of the time, Pallas kernels for 5%

profile of v1, /device:TPU:0, one launch (start us, length us, event | category | flops | bytes accessed | tf_op | source)
XLA Modules:
  0.0 196.8 jit_solution(3774708113807371689)
XLA Ops:
  0.0 0.9 broadcast_select_fusion
  1.0 1.3 collective-permute-done
  2.3 1.0 maximum_select_fusion
  3.3 0.7 fusion.7
  4.0 1.7 collective-permute-start.11
  6.9 2.0 %collective-permute-start.6 = (bf16[24,1152]{1,0:T(8,128)(2,1)S(1)}, bf16[24,1152]{1,0:T(8,128)(2,1)S(1)}, u32[]{:S(2)}, u32[]{:S(2)}) collective-permute-start(bf16[24,1152]{1,0:T(8,128)(2,1)S(1)} %get-tuple-element.32), channel_id=1, source_target_pairs={{0,8},{1,25},{2,10},{3,27},{4,12},{5,29},{6,14},{7,31},{8,0},{9,17... | collective-permute-start | bytes 165896 | tf_op jit(solution)/shard_map/ppermute | solution.py:43
  8.9 1.5 collective-permute-start.1
  10.4 2.3 %collective-permute-start.12 = (bf16[48,1152]{1,0:T(8,128)(2,1)S(1)}, bf16[48,1152]{1,0:T(8,128)(2,1)S(1)}, u32[]{:S(2)}, u32[]{:S(2)}) collective-permute-start(bf16[48,1152]{1,0:T(8,128)(2,1)S(1)} %pad_maximum_fusion.5), channel_id=1, source_target_pairs={{0,6},{1,3},{2,4},{3,1},{4,2},{5,7},{6,0},{7,5},{8,14},{9,11},{10,... | collective-permute-start | bytes 331784 | tf_op jit(solution)/shard_map/ppermute | solution.py:43
  12.7 2.7 %collective-permute-start.7 = (bf16[48,1152]{1,0:T(8,128)(2,1)S(1)}, bf16[48,1152]{1,0:T(8,128)(2,1)S(1)}, u32[]{:S(2)}, u32[]{:S(2)}) collective-permute-start(bf16[48,1152]{1,0:T(8,128)(2,1)S(1)} %pad_maximum_fusion.4), channel_id=1, source_target_pairs={{0,24},{1,9},{2,26},{3,11},{4,28},{5,13},{6,30},{7,15},{8,16},{9,1... | collective-permute-start | bytes 331784 | tf_op jit(solution)/shard_map/ppermute | solution.py:43
  15.5 2.8 %collective-permute-start.2 = (bf16[48,1152]{1,0:T(8,128)(2,1)S(1)}, bf16[48,1152]{1,0:T(8,128)(2,1)S(1)}, u32[]{:S(2)}, u32[]{:S(2)}) collective-permute-start(bf16[48,1152]{1,0:T(8,128)(2,1)S(1)} %pad_maximum_fusion.3), channel_id=1, source_target_pairs={{0,96},{1,33},{2,98},{3,35},{4,100},{5,37},{6,102},{7,39},{8,104},... | collective-permute-start | bytes 331784 | tf_op jit(solution)/shard_map/ppermute | solution.py:43
  18.8 0.6 constant_dynamic-update-slice_fusion.16
  19.4 0.6 constant_dynamic-update-slice_fusion.15
  20.1 0.6 constant_dynamic-update-slice_fusion.10
  20.7 0.8 collective-permute-done.2
  21.6 1.0 collective-permute-start.3
  22.6 0.7 collective-permute-start.8
  23.5 4.1 %collective-permute-done.3 = bf16[96,1152]{1,0:T(8,128)(2,1)S(1)} collective-permute-done((bf16[96,1152]{1,0:T(8,128)(2,1)S(1)}, bf16[96,1152]{1,0:T(8,128)(2,1)S(1)}, u32[]{:S(2)}, u32[]{:S(2)}) %collective-permute-start.3) | collective-permute-done | bytes 221216 | tf_op jit(solution)/shard_map/ppermute | solution.py:43
  27.7 2.0 collective-permute-start.4
  29.7 2.8 %collective-permute-start.14 = (bf16[192,1152]{1,0:T(8,128)(2,1)S(1)}, bf16[192,1152]{1,0:T(8,128)(2,1)S(1)}, u32[]{:S(2)}, u32[]{:S(2)}) collective-permute-start(bf16[192,1152]{1,0:T(8,128)(2,1)S(1)} %constant_dynamic-update-slice_fusion.18), channel_id=1, source_target_pairs={{0,96},{1,33},{2,98},{3,35},{4,100},{5,37},{6,102},{7,39},{8,104},... | collective-permute-start | bytes 1327112 | tf_op jit(solution)/shard_map/ppermute | solution.py:43
  32.6 2.1 %collective-permute-start.9 = (bf16[192,1152]{1,0:T(8,128)(2,1)S(1)}, bf16[192,1152]{1,0:T(8,128)(2,1)S(1)}, u32[]{:S(2)}, u32[]{:S(2)}) collective-permute-start(bf16[192,1152]{1,0:T(8,128)(2,1)S(1)} %constant_dynamic-update-slice_fusion.9), channel_id=1, source_target_pairs={{0,6},{1,3},{2,4},{3,1},{4,2},{5,7},{6,0},{7,5},{8,14},{9,11},{10,... | collective-permute-start | bytes 1327112 | tf_op jit(solution)/shard_map/ppermute | solution.py:43
  34.7 2.6 %collective-permute-done.4 = bf16[192,1152]{1,0:T(8,128)(2,1)S(1)} collective-permute-done((bf16[192,1152]{1,0:T(8,128)(2,1)S(1)}, bf16[192,1152]{1,0:T(8,128)(2,1)S(1)}, u32[]{:S(2)}, u32[]{:S(2)}) %collective-permute-start.4) | collective-permute-done | bytes 442400 | tf_op jit(solution)/shard_map/ppermute | solution.py:43
  37.5 2.1 %collective-permute-start.17 = (bf16[384,1152]{1,0:T(8,128)(2,1)S(1)}, bf16[384,1152]{1,0:T(8,128)(2,1)}, u32[]{:S(2)}, u32[]{:S(2)}) collective-permute-start(bf16[384,1152]{1,0:T(8,128)(2,1)S(1)} %slice_dynamic-update-slice_fusion.2.refs_0_), channel_id=1, source_target_pairs={{0,6},{1,3},{2,4},{3,1},{4,2},{5,7},{6,0},{7,5},{8,14},{9,11},{10,... | collective-permute-start | bytes 2654216 | tf_op jit(solution)/shard_map/ppermute | solution.py:43
  39.6 0.7 collective-permute-start.16
  40.2 4.3 %collective-permute-done.9 = bf16[192,1152]{1,0:T(8,128)(2,1)S(1)} collective-permute-done((bf16[192,1152]{1,0:T(8,128)(2,1)S(1)}, bf16[192,1152]{1,0:T(8,128)(2,1)S(1)}, u32[]{:S(2)}, u32[]{:S(2)}) %collective-permute-start.9) | collective-permute-done | bytes 442400 | tf_op jit(solution)/shard_map/ppermute | solution.py:43
  44.6 0.7 select_dynamic-update-slice_fusion.3
  45.3 0.7 select_dynamic-update-slice_fusion.2
  46.1 0.7 slice_dynamic-update-slice_fusion.1.refs_2_
  47.3 13.9 %collective-permute-done.17.refs_7_.refs_12_ = bf16[384,1152]{1,0:T(8,128)(2,1)} collective-permute-done((bf16[384,1152]{1,0:T(8,128)(2,1)S(1)}, bf16[384,1152]{1,0:T(8,128)(2,1)}, u32[]{:S(2)}, u32[]{:S(2)}) %collective-permute-start.17) | collective-permute-done | bytes 884768 | tf_op jit(solution)/shard_map/ppermute | solution.py:43
  61.3 1.4 collective-permute-start.23
  62.8 0.9 copy-done.1
  64.2 2.1 %collective-permute-done.20.refs_9_.refs_14_ = bf16[384,1152]{1,0:T(8,128)(2,1)S(1)} collective-permute-done((bf16[384,1152]{1,0:T(8,128)(2,1)}, bf16[384,1152]{1,0:T(8,128)(2,1)S(1)}, u32[]{:S(2)}, u32[]{:S(2)}) %collective-permute-start.20) | collective-permute-done | bytes 884768 | tf_op jit(solution)/shard_map/ppermute | solution.py:43
  67.2 0.9 copy-done.4
  68.1 0.7 collective-permute-start.28
  69.6 14.9 %collective-permute-done.23.refs_11_.refs_16_ = bf16[384,1152]{1,0:T(8,128)(2,1)} collective-permute-done((bf16[384,1152]{1,0:T(8,128)(2,1)S(1)}, bf16[384,1152]{1,0:T(8,128)(2,1)}, u32[]{:S(2)}, u32[]{:S(2)}) %collective-permute-start.23) | collective-permute-done | bytes 884768 | tf_op jit(solution)/shard_map/ppermute | solution.py:43
  85.4 1.2 collective-permute-start.32
  86.5 5.3 %fusion = f32[24,3456]{1,0:T(8,128)} fusion(bf16[1152,3456]{1,0:T(8,128)(2,1)} %param.17, f32[24,576]{1,0:T(8,128)S(1)} %get-tuple-element.44, f32[24,576]{1,0:T(8,128)S(1)} %get-tuple-element.43, f32[1152]{0:T(1024)S(1)} %reduce.1), kind=kOutput, calls=%fused_computation.52 | convolution fusion | flops 191296512 | bytes 8409600 | tf_op jit(solution)/shard_map/dot_general | solution.py:306
  91.8 0.9 slice_bitcast_fusion
  92.8 0.9 copy-done.14
  93.7 0.9 copy-done.20
  95.1 4.0 %collective-permute-done.30.refs_2_.refs_20_ = bf16[384,1152]{1,0:T(8,128)(2,1)} collective-permute-done((bf16[384,1152]{1,0:T(8,128)(2,1)}, bf16[384,1152]{1,0:T(8,128)(2,1)}, u32[]{:S(2)}, u32[]{:S(2)}) %collective-permute-start.30) | collective-permute-done | bytes 884768 | tf_op jit(solution)/shard_map/ppermute | solution.py:43
  99.1 0.9 copy-done.17
  100.6 1.4 dynamic_slice.16
  102.0 1.3 dynamic_slice.15
  103.3 1.3 pad_maximum_fusion.6.step_ref
  104.6 0.8 fusion.3
  105.7 4.3 %mlp_piece.2.refs_0_ = f32[256,1152]{1,0:T(8,128)S(1)} custom-call(s32[1]{0:T(128)} %bitcast.core_ref, bf16[256,1152]{1,0:T(8,128)(2,1)S(1)} %add_convert_fusion.hidden_ref, bf16[384,1152]{1,0:T(8,128)(2,1)S(1)} %slice_dynamic-update-slice_fusion.2.refs_0_, bf16[384,1152]{1,0:T(8,128)(2,1)S(1)} %copy-done.2, ...), custom_call_target="tpu_custom_call" | custom-call | tf_op jit(solution)/shard_map/mlp_piece/pallas_call | solution.py:146
  110.1 6.1 %mlp_piece.3.acc_in = f32[256,1152]{1,0:T(8,128)S(1)} custom-call(s32[1]{0:T(128)} %bitcast.core_ref, bf16[256,1152]{1,0:T(8,128)(2,1)S(1)} %add_convert_fusion.hidden_ref, f32[256,1152]{1,0:T(8,128)S(1)} %mlp_piece.2.refs_0_, bf16[384,1152]{1,0:T(8,128)(2,1)} %collective-permute-done.16.refs_1_.refs_6_, ...), custom_call_target="tpu_custom_call" | custom-call | tf_op jit(solution)/shard_map/mlp_piece/pallas_call | solution.py:146
  116.3 6.9 %finish_first.1 = bf16[16,48,1152]{2,1,0:T(8,128)(2,1)} custom-call(s32[1]{0:T(128)} %bitcast.core_ref, f32[1]{0:T(128)} %bitcast.3.first_ref, f32[2]{0:T(128)S(1)} %pad_maximum_fusion.6.step_ref, bf16[256,1152]{1,0:T(8,128)(2,1)S(1)} %add_convert_fusion.hidden_ref, f32[256,1152]{1,0:T(8,128)S(1)} %mlp_piece.3.acc_in, f32[256,1152]{1,0:T(8,128)S(1)} %bitcast.17, ...), custom_call_target="tpu_custom_call" | custom-call | tf_op jit(solution)/shard_map/finish_first/pallas_call | solution.py:188
  123.2 4.6 %all-to-all-start = ((bf16[16,48,1152]{2,1,0:T(8,128)(2,1)}), bf16[16,48,1152]{2,1,0:T(8,128)(2,1)}, u32[]{:S(2)}, u32[]{:S(2)}) async-start(bf16[16,48,1152]{2,1,0:T(8,128)(2,1)} %finish_first.1), calls=%async_computation | async-start | bytes 3538944 | tf_op jit(solution)/shard_map/all_to_all | solution.py:331
  127.8 0.8 dynamic_slice.13.dt_ref
  128.6 0.8 dynamic_slice.14.sigma_ref
  129.3 1.6 fusion.6
  131.0 23.9 %all-to-all-done.got_ref = bf16[16,48,1152]{2,1,0:T(8,128)(2,1)} async-done(((bf16[16,48,1152]{2,1,0:T(8,128)(2,1)}), bf16[16,48,1152]{2,1,0:T(8,128)(2,1)}, u32[]{:S(2)}, u32[]{:S(2)}) %all-to-all-start) | async-done | bytes 1769504 | tf_op jit(solution)/shard_map/all_to_all | solution.py:331
  154.9 1.2 copy-done.6
  156.0 1.2 copy-done.10
  157.2 1.2 copy-done.16
  158.4 1.2 copy-done.19
  159.5 1.2 copy-done.22
  160.7 0.9 copy-done.24
  161.6 0.9 copy-done.25
  162.5 0.9 copy-done.26
  163.4 15.2 %second_sweep.1 = bf16[16,16,1152]{2,1,0:T(8,128)(2,1)S(1)} custom-call(s32[1]{0:T(128)} %bitcast.core_ref, s32[1]{0:T(128)} %copy.42.advance_ref, f32[16]{0:T(128)S(1)} %dynamic_slice.13.dt_ref, f32[16]{0:T(128)S(1)} %dynamic_slice.14.sigma_ref, bf16[16,48,1152]{2,1,0:T(8,128)(2,1)} %all-to-all-done.got_ref, f32[16,1152]{1,0:T(8,128)S(1)} %copy-done.26, ...), custom_call_target="tpu_custom_call" | custom-call | tf_op jit(solution)/shard_map/second_sweep/pallas_call | solution.py:243
  178.6 17.1 %all_to_all.10 = bf16[16,16,1152]{2,1,0:T(8,128)(2,1)S(1)} all-to-all(bf16[16,16,1152]{2,1,0:T(8,128)(2,1)S(1)} %second_sweep.1), channel_id=1, replica_groups=mesh['tm'=16,'batch'=8] {'tm'}, dimensions={0} | all-to-all | bytes 1179648 | tf_op jit(solution)/shard_map/all_to_all | solution.py:343
  195.7 1.1 convert.2
  (125 shorter events, 6.2 us)
Async XLA Ops:
  0.9 1.4 collective-permute-start
  4.0 6.5 %collective-permute-start.11 = (bf16[24,1152]{1,0:T(8,128)(2,1)S(1)}, bf16[24,1152]{1,0:T(8,128)(2,1)S(1)}, u32[]{:S(2)}, u32[]{:S(2)}) collective-permute-start(bf16[24,1152]{1,0:T(8,128)(2,1)S(1)} %get-tuple-element.25), channel_id=1, source_target_pairs={{0,2},{1,7},{2,0},{3,5},{4,6},{5,3},{6,4},{7,1},{8,10},{9,15},{10,... | collective-permute-start | bytes 165896 | tf_op jit(solution)/shard_map/ppermute | solution.py:43
  6.9 5.8 %collective-permute-start.6 = (bf16[24,1152]{1,0:T(8,128)(2,1)S(1)}, bf16[24,1152]{1,0:T(8,128)(2,1)S(1)}, u32[]{:S(2)}, u32[]{:S(2)}) collective-permute-start(bf16[24,1152]{1,0:T(8,128)(2,1)S(1)} %get-tuple-element.32), channel_id=1, source_target_pairs={{0,8},{1,25},{2,10},{3,27},{4,12},{5,29},{6,14},{7,31},{8,0},{9,17... | collective-permute-start | bytes 165896 | tf_op jit(solution)/shard_map/ppermute | solution.py:43
  8.9 6.5 %collective-permute-start.1 = (bf16[24,1152]{1,0:T(8,128)(2,1)S(1)}, bf16[24,1152]{1,0:T(8,128)(2,1)S(1)}, u32[]{:S(2)}, u32[]{:S(2)}) collective-permute-start(bf16[24,1152]{1,0:T(8,128)(2,1)S(1)} %get-tuple-element.33), channel_id=1, source_target_pairs={{0,32},{1,97},{2,34},{3,99},{4,36},{5,101},{6,38},{7,103},{8,40},{... | collective-permute-start | bytes 165896 | tf_op jit(solution)/shard_map/ppermute | solution.py:43
  10.4 12.9 %collective-permute-start.12 = (bf16[48,1152]{1,0:T(8,128)(2,1)S(1)}, bf16[48,1152]{1,0:T(8,128)(2,1)S(1)}, u32[]{:S(2)}, u32[]{:S(2)}) collective-permute-start(bf16[48,1152]{1,0:T(8,128)(2,1)S(1)} %pad_maximum_fusion.5), channel_id=1, source_target_pairs={{0,6},{1,3},{2,4},{3,1},{4,2},{5,7},{6,0},{7,5},{8,14},{9,11},{10,... | collective-permute-start | bytes 331784 | tf_op jit(solution)/shard_map/ppermute | solution.py:43
  12.7 6.0 %collective-permute-start.7 = (bf16[48,1152]{1,0:T(8,128)(2,1)S(1)}, bf16[48,1152]{1,0:T(8,128)(2,1)S(1)}, u32[]{:S(2)}, u32[]{:S(2)}) collective-permute-start(bf16[48,1152]{1,0:T(8,128)(2,1)S(1)} %pad_maximum_fusion.4), channel_id=1, source_target_pairs={{0,24},{1,9},{2,26},{3,11},{4,28},{5,13},{6,30},{7,15},{8,16},{9,1... | collective-permute-start | bytes 331784 | tf_op jit(solution)/shard_map/ppermute | solution.py:43
  15.5 6.0 %collective-permute-start.2 = (bf16[48,1152]{1,0:T(8,128)(2,1)S(1)}, bf16[48,1152]{1,0:T(8,128)(2,1)S(1)}, u32[]{:S(2)}, u32[]{:S(2)}) collective-permute-start(bf16[48,1152]{1,0:T(8,128)(2,1)S(1)} %pad_maximum_fusion.3), channel_id=1, source_target_pairs={{0,96},{1,33},{2,98},{3,35},{4,100},{5,37},{6,102},{7,39},{8,104},... | collective-permute-start | bytes 331784 | tf_op jit(solution)/shard_map/ppermute | solution.py:43
  21.6 6.0 %collective-permute-start.3 = (bf16[96,1152]{1,0:T(8,128)(2,1)S(1)}, bf16[96,1152]{1,0:T(8,128)(2,1)S(1)}, u32[]{:S(2)}, u32[]{:S(2)}) collective-permute-start(bf16[96,1152]{1,0:T(8,128)(2,1)S(1)} %pad_maximum_fusion), channel_id=1, source_target_pairs={{0,8},{1,25},{2,10},{3,27},{4,12},{5,29},{6,14},{7,31},{8,0},{9,17... | collective-permute-start | bytes 663560 | tf_op jit(solution)/shard_map/ppermute | solution.py:43
  22.6 9.9 %collective-permute-start.8 = (bf16[96,1152]{1,0:T(8,128)(2,1)S(1)}, bf16[96,1152]{1,0:T(8,128)(2,1)S(1)}, u32[]{:S(2)}, u32[]{:S(2)}) collective-permute-start(bf16[96,1152]{1,0:T(8,128)(2,1)S(1)} %pad_maximum_fusion.1), channel_id=1, source_target_pairs={{0,2},{1,7},{2,0},{3,5},{4,6},{5,3},{6,4},{7,1},{8,10},{9,15},{10,... | collective-permute-start | bytes 663560 | tf_op jit(solution)/shard_map/ppermute | solution.py:43
  23.4 6.2 %collective-permute-start.13 = (bf16[96,1152]{1,0:T(8,128)(2,1)S(1)}, bf16[96,1152]{1,0:T(8,128)(2,1)S(1)}, u32[]{:S(2)}, u32[]{:S(2)}) collective-permute-start(bf16[96,1152]{1,0:T(8,128)(2,1)S(1)} %pad_maximum_fusion.2), channel_id=1, source_target_pairs={{0,32},{1,97},{2,34},{3,99},{4,36},{5,101},{6,38},{7,103},{8,40},{... | collective-permute-start | bytes 663560 | tf_op jit(solution)/shard_map/ppermute | solution.py:43
  27.7 9.6 %collective-permute-start.4 = (bf16[192,1152]{1,0:T(8,128)(2,1)S(1)}, bf16[192,1152]{1,0:T(8,128)(2,1)S(1)}, u32[]{:S(2)}, u32[]{:S(2)}) collective-permute-start(bf16[192,1152]{1,0:T(8,128)(2,1)S(1)} %constant_dynamic-update-slice_fusion), channel_id=1, source_target_pairs={{0,24},{1,9},{2,26},{3,11},{4,28},{5,13},{6,30},{7,15},{8,16},{9,1... | collective-permute-start | bytes 1327112 | tf_op jit(solution)/shard_map/ppermute | solution.py:43
  29.7 17.1 %collective-permute-start.14 = (bf16[192,1152]{1,0:T(8,128)(2,1)S(1)}, bf16[192,1152]{1,0:T(8,128)(2,1)S(1)}, u32[]{:S(2)}, u32[]{:S(2)}) collective-permute-start(bf16[192,1152]{1,0:T(8,128)(2,1)S(1)} %constant_dynamic-update-slice_fusion.18), channel_id=1, source_target_pairs={{0,96},{1,33},{2,98},{3,35},{4,100},{5,37},{6,102},{7,39},{8,104},... | collective-permute-start | bytes 1327112 | tf_op jit(solution)/shard_map/ppermute | solution.py:43
  32.6 12.0 %collective-permute-start.9 = (bf16[192,1152]{1,0:T(8,128)(2,1)S(1)}, bf16[192,1152]{1,0:T(8,128)(2,1)S(1)}, u32[]{:S(2)}, u32[]{:S(2)}) collective-permute-start(bf16[192,1152]{1,0:T(8,128)(2,1)S(1)} %constant_dynamic-update-slice_fusion.9), channel_id=1, source_target_pairs={{0,6},{1,3},{2,4},{3,1},{4,2},{5,7},{6,0},{7,5},{8,14},{9,11},{10,... | collective-permute-start | bytes 1327112 | tf_op jit(solution)/shard_map/ppermute | solution.py:43
  37.5 23.8 %collective-permute-start.17 = (bf16[384,1152]{1,0:T(8,128)(2,1)S(1)}, bf16[384,1152]{1,0:T(8,128)(2,1)}, u32[]{:S(2)}, u32[]{:S(2)}) collective-permute-start(bf16[384,1152]{1,0:T(8,128)(2,1)S(1)} %slice_dynamic-update-slice_fusion.2.refs_0_), channel_id=1, source_target_pairs={{0,6},{1,3},{2,4},{3,1},{4,2},{5,7},{6,0},{7,5},{8,14},{9,11},{10,... | collective-permute-start | bytes 2654216 | tf_op jit(solution)/shard_map/ppermute | solution.py:43
  39.6 21.8 %collective-permute-start.16 = (bf16[384,1152]{1,0:T(8,128)(2,1)S(1)}, bf16[384,1152]{1,0:T(8,128)(2,1)}, u32[]{:S(2)}, u32[]{:S(2)}) collective-permute-start(bf16[384,1152]{1,0:T(8,128)(2,1)S(1)} %slice_dynamic-update-slice_fusion.2.refs_0_), channel_id=1, source_target_pairs={{0,2},{1,7},{2,0},{3,5},{4,6},{5,3},{6,4},{7,1},{8,10},{9,15},{10,... | collective-permute-start | bytes 2654216 | tf_op jit(solution)/shard_map/ppermute | solution.py:43
  40.2 22.5 %collective-permute-start.5 = (bf16[384,1152]{1,0:T(8,128)(2,1)S(1)}, bf16[384,1152]{1,0:T(8,128)(2,1)S(1)}, u32[]{:S(2)}, u32[]{:S(2)}) collective-permute-start(bf16[384,1152]{1,0:T(8,128)(2,1)S(1)} %slice_dynamic-update-slice_fusion.2.refs_0_), channel_id=1, source_target_pairs={{0,1},{1,0},{2,3},{3,2},{4,5},{5,4},{6,7},{7,6},{8,9},{9,8},{10,11... | collective-permute-start | bytes 2654216 | tf_op jit(solution)/shard_map/ppermute | solution.py:47
  46.1 22.7 %copy-start = (f32[1,1,256,1152]{3,2,1,0:T(8,128)S(1)}, f32[1,1,256,1152]{3,2,1,0:T(8,128)}, u32[]{:S(2)}) copy-start(f32[1,1,256,1152]{3,2,1,0:T(8,128)} %param.10) | copy-start | bytes 3538948
  46.8 19.5 %collective-permute-start.20 = (bf16[384,1152]{1,0:T(8,128)(2,1)}, bf16[384,1152]{1,0:T(8,128)(2,1)S(1)}, u32[]{:S(2)}, u32[]{:S(2)}) collective-permute-start(bf16[384,1152]{1,0:T(8,128)(2,1)} %slice_dynamic-update-slice_fusion.1.refs_2_), channel_id=1, source_target_pairs={{0,96},{1,33},{2,98},{3,35},{4,100},{5,37},{6,102},{7,39},{8,104},... | collective-permute-start | bytes 2654216 | tf_op jit(solution)/shard_map/ppermute | solution.py:43
  46.8 19.5 %collective-permute-start.19 = (bf16[384,1152]{1,0:T(8,128)(2,1)}, bf16[384,1152]{1,0:T(8,128)(2,1)S(1)}, u32[]{:S(2)}, u32[]{:S(2)}) collective-permute-start(bf16[384,1152]{1,0:T(8,128)(2,1)} %slice_dynamic-update-slice_fusion.1.refs_2_), channel_id=1, source_target_pairs={{0,32},{1,97},{2,34},{3,99},{4,36},{5,101},{6,38},{7,103},{8,40},{... | collective-permute-start | bytes 2654216 | tf_op jit(solution)/shard_map/ppermute | solution.py:43
  47.3 21.6 %copy-start.28 = (f32[1,1152]{1,0:T(1,128)S(1)}, f32[1,1152]{1,0:T(1,128)}, u32[]{:S(2)}) copy-start(f32[1,1152]{1,0:T(1,128)} %param.12) | copy-start | bytes 13828
  61.2 5.6 %collective-permute-start.10 = (bf16[384,1152]{1,0:T(8,128)(2,1)}, bf16[384,1152]{1,0:T(8,128)(2,1)S(1)}, u32[]{:S(2)}, u32[]{:S(2)}) collective-permute-start(bf16[384,1152]{1,0:T(8,128)(2,1)} %slice_dynamic-update-slice_fusion.1.refs_2_), channel_id=1, source_target_pairs={{0,1},{1,0},{2,3},{3,2},{4,5},{5,4},{6,7},{7,6},{8,9},{9,8},{10,11... | collective-permute-start | bytes 2654216 | tf_op jit(solution)/shard_map/ppermute | solution.py:47
  61.3 23.2 %collective-permute-start.23 = (bf16[384,1152]{1,0:T(8,128)(2,1)S(1)}, bf16[384,1152]{1,0:T(8,128)(2,1)}, u32[]{:S(2)}, u32[]{:S(2)}) collective-permute-start(bf16[384,1152]{1,0:T(8,128)(2,1)S(1)} %slice_dynamic-update-slice_fusion.refs_4_), channel_id=1, source_target_pairs={{0,24},{1,9},{2,26},{3,11},{4,28},{5,13},{6,30},{7,15},{8,16},{9,1... | collective-permute-start | bytes 2654216 | tf_op jit(solution)/shard_map/ppermute | solution.py:43
  62.8 0.9 copy-start.1
  63.7 20.8 %collective-permute-start.22 = (bf16[384,1152]{1,0:T(8,128)(2,1)S(1)}, bf16[384,1152]{1,0:T(8,128)(2,1)}, u32[]{:S(2)}, u32[]{:S(2)}) collective-permute-start(bf16[384,1152]{1,0:T(8,128)(2,1)S(1)} %slice_dynamic-update-slice_fusion.refs_4_), channel_id=1, source_target_pairs={{0,8},{1,25},{2,10},{3,27},{4,12},{5,29},{6,14},{7,31},{8,0},{9,17... | collective-permute-start | bytes 2654216 | tf_op jit(solution)/shard_map/ppermute | solution.py:43
  66.3 0.9 copy-start.7
  66.3 18.4 %collective-permute-start.15 = (bf16[384,1152]{1,0:T(8,128)(2,1)S(1)}, bf16[384,1152]{1,0:T(8,128)(2,1)}, u32[]{:S(2)}, u32[]{:S(2)}) collective-permute-start(bf16[384,1152]{1,0:T(8,128)(2,1)S(1)} %slice_dynamic-update-slice_fusion.refs_4_), channel_id=1, source_target_pairs={{0,1},{1,0},{2,3},{3,2},{4,5},{5,4},{6,7},{7,6},{8,9},{9,8},{10,11... | collective-permute-start | bytes 2654216 | tf_op jit(solution)/shard_map/ppermute | solution.py:47
  66.3 2.5 %copy-start.11 = (bf16[384,1152]{1,0:T(8,128)(2,1)}, bf16[384,1152]{1,0:T(8,128)(2,1)S(1)}, u32[]{:S(2)}) copy-start(bf16[384,1152]{1,0:T(8,128)(2,1)S(1)} %collective-permute-done.19.refs_3_.refs_8_) | copy-start | bytes 2654212
  66.3 19.0 %collective-permute-start.18 = (bf16[384,1152]{1,0:T(8,128)(2,1)}, bf16[384,1152]{1,0:T(8,128)(2,1)}, u32[]{:S(2)}, u32[]{:S(2)}) collective-permute-start(bf16[384,1152]{1,0:T(8,128)(2,1)} %collective-permute-done.17.refs_7_.refs_12_), channel_id=1, source_target_pairs={{0,1},{1,0},{2,3},{3,2},{4,5},{5,4},{6,7},{7,6},{8,9},{9,8},{10,11... | collective-permute-start | bytes 2654216 | tf_op jit(solution)/shard_map/ppermute | solution.py:47
  67.2 0.9 copy-start.4
  68.1 17.3 %collective-permute-start.28 = (bf16[384,1152]{1,0:T(8,128)(2,1)}, bf16[384,1152]{1,0:T(8,128)(2,1)}, u32[]{:S(2)}, u32[]{:S(2)}) collective-permute-start(bf16[384,1152]{1,0:T(8,128)(2,1)} %collective-permute-done.16.refs_1_.refs_6_), channel_id=1, source_target_pairs={{0,6},{1,3},{2,4},{3,1},{4,2},{5,7},{6,0},{7,5},{8,14},{9,11},{10,... | collective-permute-start | bytes 2654216 | tf_op jit(solution)/shard_map/ppermute | solution.py:43
  69.0 16.3 %copy-start.8 = (bf16[384,1152]{1,0:T(8,128)(2,1)S(1)}, bf16[384,1152]{1,0:T(8,128)(2,1)}, u32[]{:S(2)}) copy-start(bf16[384,1152]{1,0:T(8,128)(2,1)} %copy-done.7) | copy-start | bytes 2654212
  84.5 8.2 %collective-permute-start.25 = (bf16[384,1152]{1,0:T(8,128)(2,1)}, bf16[384,1152]{1,0:T(8,128)(2,1)S(1)}, u32[]{:S(2)}, u32[]{:S(2)}) collective-permute-start(bf16[384,1152]{1,0:T(8,128)(2,1)} %collective-permute-done.16.refs_1_.refs_6_), channel_id=1, source_target_pairs={{0,1},{1,0},{2,3},{3,2},{4,5},{5,4},{6,7},{7,6},{8,9},{9,8},{10,11... | collective-permute-start | bytes 2654216 | tf_op jit(solution)/shard_map/ppermute | solution.py:47
  84.5 14.6 %collective-permute-start.30 = (bf16[384,1152]{1,0:T(8,128)(2,1)}, bf16[384,1152]{1,0:T(8,128)(2,1)}, u32[]{:S(2)}, u32[]{:S(2)}) collective-permute-start(bf16[384,1152]{1,0:T(8,128)(2,1)} %copy-done.11), channel_id=1, source_target_pairs={{0,96},{1,33},{2,98},{3,35},{4,100},{5,37},{6,102},{7,39},{8,104},... | collective-permute-start | bytes 2654216 | tf_op jit(solution)/shard_map/ppermute | solution.py:43
  84.7 14.4 %collective-permute-start.26 = (bf16[384,1152]{1,0:T(8,128)(2,1)}, bf16[384,1152]{1,0:T(8,128)(2,1)S(1)}, u32[]{:S(2)}, u32[]{:S(2)}) collective-permute-start(bf16[384,1152]{1,0:T(8,128)(2,1)} %copy-done.11), channel_id=1, source_target_pairs={{0,1},{1,0},{2,3},{3,2},{4,5},{5,4},{6,7},{7,6},{8,9},{9,8},{10,11... | collective-permute-start | bytes 2654216 | tf_op jit(solution)/shard_map/ppermute | solution.py:47
  85.3 8.4 %collective-permute-start.21 = (bf16[384,1152]{1,0:T(8,128)(2,1)S(1)}, bf16[384,1152]{1,0:T(8,128)(2,1)S(1)}, u32[]{:S(2)}, u32[]{:S(2)}) collective-permute-start(bf16[384,1152]{1,0:T(8,128)(2,1)S(1)} %copy-done.8), channel_id=1, source_target_pairs={{0,1},{1,0},{2,3},{3,2},{4,5},{5,4},{6,7},{7,6},{8,9},{9,8},{10,11... | collective-permute-start | bytes 2654216 | tf_op jit(solution)/shard_map/ppermute | solution.py:47
  85.4 15.2 %collective-permute-start.32 = (bf16[384,1152]{1,0:T(8,128)(2,1)}, bf16[384,1152]{1,0:T(8,128)(2,1)}, u32[]{:S(2)}, u32[]{:S(2)}) collective-permute-start(bf16[384,1152]{1,0:T(8,128)(2,1)} %collective-permute-done.22.refs_5_.refs_10_), channel_id=1, source_target_pairs={{0,24},{1,9},{2,26},{3,11},{4,28},{5,13},{6,30},{7,15},{8,16},{9,1... | collective-permute-start | bytes 2654216 | tf_op jit(solution)/shard_map/ppermute | solution.py:43
  86.5 5.3 %copy-start.27 = (bf16[2,1,1,256,1152]{4,3,2,1,0:T(8,128)(2,1)S(1)}, bf16[2,1,1,256,1152]{4,3,2,1,0:T(8,128)(2,1)}, u32[]{:S(2)}) copy-start(bf16[2,1,1,256,1152]{4,3,2,1,0:T(8,128)(2,1)} %param.11) | copy-start | bytes 3538948
  92.8 0.9 copy-start.14
  93.7 16.4 %collective-permute-start.27 = (bf16[384,1152]{1,0:T(8,128)(2,1)}, bf16[384,1152]{1,0:T(8,128)(2,1)}, u32[]{:S(2)}, u32[]{:S(2)}) collective-permute-start(bf16[384,1152]{1,0:T(8,128)(2,1)} %collective-permute-done.22.refs_5_.refs_10_), channel_id=1, source_target_pairs={{0,1},{1,0},{2,3},{3,2},{4,5},{5,4},{6,7},{7,6},{8,9},{9,8},{10,11... | collective-permute-start | bytes 2654216 | tf_op jit(solution)/shard_map/ppermute | solution.py:47
  93.7 0.9 copy-start.20
  94.6 15.5 %collective-permute-start.24 = (bf16[384,1152]{1,0:T(8,128)(2,1)}, bf16[384,1152]{1,0:T(8,128)(2,1)}, u32[]{:S(2)}, u32[]{:S(2)}) collective-permute-start(bf16[384,1152]{1,0:T(8,128)(2,1)} %collective-permute-done.23.refs_11_.refs_16_), channel_id=1, source_target_pairs={{0,1},{1,0},{2,3},{3,2},{4,5},{5,4},{6,7},{7,6},{8,9},{9,8},{10,11... | collective-permute-start | bytes 2654216 | tf_op jit(solution)/shard_map/ppermute | solution.py:47
  99.1 17.2 %collective-permute-start.29 = (bf16[384,1152]{1,0:T(8,128)(2,1)}, bf16[384,1152]{1,0:T(8,128)(2,1)}, u32[]{:S(2)}, u32[]{:S(2)}) collective-permute-start(bf16[384,1152]{1,0:T(8,128)(2,1)} %collective-permute-done.28.refs_0_.refs_18_), channel_id=1, source_target_pairs={{0,1},{1,0},{2,3},{3,2},{4,5},{5,4},{6,7},{7,6},{8,9},{9,8},{10,11... | collective-permute-start | bytes 2654216 | tf_op jit(solution)/shard_map/ppermute | solution.py:47
  99.1 1.0 copy-start.17
  100.1 16.3 %collective-permute-start.31 = (bf16[384,1152]{1,0:T(8,128)(2,1)}, bf16[384,1152]{1,0:T(8,128)(2,1)}, u32[]{:S(2)}, u32[]{:S(2)}) collective-permute-start(bf16[384,1152]{1,0:T(8,128)(2,1)} %collective-permute-done.30.refs_2_.refs_20_), channel_id=1, source_target_pairs={{0,1},{1,0},{2,3},{3,2},{4,5},{5,4},{6,7},{7,6},{8,9},{9,8},{10,11... | collective-permute-start | bytes 2654216 | tf_op jit(solution)/shard_map/ppermute | solution.py:47
  100.6 15.8 %collective-permute-start.33 = (bf16[384,1152]{1,0:T(8,128)(2,1)}, bf16[384,1152]{1,0:T(8,128)(2,1)}, u32[]{:S(2)}, u32[]{:S(2)}) collective-permute-start(bf16[384,1152]{1,0:T(8,128)(2,1)} %collective-permute-done.32.refs_4_.refs_22_), channel_id=1, source_target_pairs={{0,1},{1,0},{2,3},{3,2},{4,5},{5,4},{6,7},{7,6},{8,9},{9,8},{10,11... | collective-permute-start | bytes 2654216 | tf_op jit(solution)/shard_map/ppermute | solution.py:47
  100.6 5.1 %copy-start.2 = (bf16[384,1152]{1,0:T(8,128)(2,1)S(1)}, bf16[384,1152]{1,0:T(8,128)(2,1)}, u32[]{:S(2)}) copy-start(bf16[384,1152]{1,0:T(8,128)(2,1)} %copy-done.1) | copy-start | bytes 2654212
  100.6 5.1 %copy-start.5 = (bf16[384,1152]{1,0:T(8,128)(2,1)S(1)}, bf16[384,1152]{1,0:T(8,128)(2,1)}, u32[]{:S(2)}) copy-start(bf16[384,1152]{1,0:T(8,128)(2,1)} %copy-done.4) | copy-start | bytes 2654212
  105.7 4.4 %copy-start.9 = (bf16[384,1152]{1,0:T(8,128)(2,1)S(1)}, bf16[384,1152]{1,0:T(8,128)(2,1)}, u32[]{:S(2)}) copy-start(bf16[384,1152]{1,0:T(8,128)(2,1)} %copy-done.7) | copy-start | bytes 2654212
  105.7 4.4 %copy-start.12 = (bf16[384,1152]{1,0:T(8,128)(2,1)S(1)}, bf16[384,1152]{1,0:T(8,128)(2,1)}, u32[]{:S(2)}) copy-start(bf16[384,1152]{1,0:T(8,128)(2,1)} %copy-done.11) | copy-start | bytes 2654212
  105.7 4.4 %copy-start.15 = (bf16[384,1152]{1,0:T(8,128)(2,1)S(1)}, bf16[384,1152]{1,0:T(8,128)(2,1)}, u32[]{:S(2)}) copy-start(bf16[384,1152]{1,0:T(8,128)(2,1)} %copy-done.14) | copy-start | bytes 2654212
  105.7 4.4 %copy-start.18 = (bf16[384,1152]{1,0:T(8,128)(2,1)S(1)}, bf16[384,1152]{1,0:T(8,128)(2,1)}, u32[]{:S(2)}) copy-start(bf16[384,1152]{1,0:T(8,128)(2,1)} %copy-done.17) | copy-start | bytes 2654212
  105.7 4.4 %copy-start.21 = (bf16[384,1152]{1,0:T(8,128)(2,1)S(1)}, bf16[384,1152]{1,0:T(8,128)(2,1)}, u32[]{:S(2)}) copy-start(bf16[384,1152]{1,0:T(8,128)(2,1)} %copy-done.20) | copy-start | bytes 2654212
  110.1 6.3 %copy-start.23 = (bf16[256,1152]{1,0:T(8,128)(2,1)S(1)}, bf16[256,1152]{1,0:T(8,128)(2,1)}, u32[]{:S(2)}) copy-start(bf16[256,1152]{1,0:T(8,128)(2,1)} %get-tuple-element.20.noise_ref) | copy-start | bytes 1769476
  123.2 31.7 %copy-start.3 = (bf16[384,1152]{1,0:T(8,128)(2,1)S(1)}, bf16[384,1152]{1,0:T(8,128)(2,1)}, u32[]{:S(2)}) copy-start(bf16[384,1152]{1,0:T(8,128)(2,1)} %copy-done.1) | copy-start | bytes 2654212
  123.2 31.7 %copy-start.13 = (bf16[384,1152]{1,0:T(8,128)(2,1)S(1)}, bf16[384,1152]{1,0:T(8,128)(2,1)}, u32[]{:S(2)}) copy-start(bf16[384,1152]{1,0:T(8,128)(2,1)} %copy-done.11) | copy-start | bytes 2654212
  123.2 31.6 %all-to-all-start = ((bf16[16,48,1152]{2,1,0:T(8,128)(2,1)}), bf16[16,48,1152]{2,1,0:T(8,128)(2,1)}, u32[]{:S(2)}, u32[]{:S(2)}) async-start(bf16[16,48,1152]{2,1,0:T(8,128)(2,1)} %finish_first.1), calls=%async_computation | async-start | bytes 3538944 | tf_op jit(solution)/shard_map/all_to_all | solution.py:331
  154.9 1.2 copy-start.6
  156.0 1.2 copy-start.10
  157.2 1.2 copy-start.16
  158.4 1.2 copy-start.19
  159.5 1.2 copy-start.22
  160.7 0.9 copy-start.24
  161.6 0.9 copy-start.25
  162.5 0.9 copy-start.26

commit v2 on v1

v2 whole, which is shorter than its diff:
```python
import functools
import math

import jax
import jax.numpy as jnp
from jax import lax
from jax.experimental import pallas as pl
from jax.experimental.pallas import tpu as pltpu
from jax.sharding import PartitionSpec as P

EPSILON = 1e-06
ALL = ("tm", "batch")
SIDE = 4
CORES = 2
THIRDS = 3
SLIDE = 7
ROWS = 16
OWN_ROW = slice(16, 17)
f32, bf16 = jnp.float32, jnp.bfloat16


def device_pairs(move):
    pairs = []
    for x in range(SIDE):
        for z in range(SIDE):
            for y in range(SIDE):
                for core in range(CORES):
                    here, there = (x, z, y, core), move((x, z, y, core))
                    flat = [((p[0] * SIDE + p[1]) * SIDE + p[2]) * CORES + p[3] for p in (here, there)]
                    pairs.append(tuple(flat))
    return pairs


def neighbour(axis, first):
    def move(place):
        place = list(place)
        odd = (place[3] == 0) == first
        place[axis] = place[axis] ^ 1 if odd else SIDE - 1 - place[axis]
        return tuple(place)

    return device_pairs(move)


def send(rows, axis, first):
    return lax.ppermute(rows, ALL, neighbour(axis, first))


def swap_cores(rows):
    return lax.ppermute(rows, ALL, device_pairs(lambda p: (p[0], p[1], p[2], 1 - p[3])))


def grow(rows, axis, core):
    near = send(rows, axis, True)
    both = send(jnp.concatenate([rows, near]), axis, False)
    count = rows.shape[0]
    second, far = both[:count], both[count:]
    low = jnp.where(core == 0, near, second)
    high = jnp.where(core == 0, second, near)
    return jnp.concatenate([rows, low, high, far])


def gelu(before):
    inner = math.sqrt(2.0 / math.pi) * (before + 0.044715 * (before * before * before))
    return 0.5 * before * (1.0 + jnp.tanh(inner))


def copies(side, pairs, up_buf, down_buf, sems, slot):
    made = []
    size = pairs[0][0].shape[0]
    for part, pair in enumerate(pairs):
        place = pl.ds(part * size, size)
        made.append(pltpu.make_async_copy(pair[side], up_buf.at[slot, place], sems.at[slot, 0, part]))
        made.append(
            pltpu.make_async_copy(pair[1 - side], down_buf.at[slot, place], sems.at[slot, 1, part])
        )
    return made


def start_set(core_ref, *where):
    for side in (0, 1):

        @pl.when(core_ref[0] == side)
        def _():
            for copy in copies(side, *where):
                copy.start()


def wait_set(*where):
    for copy in copies(0, *where):
        copy.wait()


def mlp_part(hidden, up_rows, down_rows):
    before = lax.dot_general(hidden, up_rows, (((1,), (1,)), ((), ())), preferred_element_type=f32)
    return jnp.dot(gelu(before).astype(bf16), down_rows, preferred_element_type=f32)


def mlp_sets(core_ref, sets, kept_refs, hidden_ref, acc_ref, given, up_buf, down_buf, sems, kept_sems):
    kept = []
    for index, pairs in enumerate(sets):
        slot = index % 2
        if index + 1 < len(sets):
            start_set(core_ref, sets[index + 1], up_buf, down_buf, sems, 1 - slot)
        wait_set(pairs, up_buf, down_buf, sems, slot)
        for kind, buf in enumerate((up_buf, down_buf)):
            place = 2 * index + kind
            kept.append(pltpu.make_async_copy(buf.at[slot], kept_refs[place], kept_sems.at[place]))
            kept[-1].start()
        part = mlp_part(hidden_ref[...], up_buf[slot], down_buf[slot])
        if index > 0:
            acc_ref[...] += part
        elif given is None:
            acc_ref[...] = part
        else:
            acc_ref[...] = given[...] + part
    for copy in kept:
        copy.wait()


def as_sets(refs):
    pairs = [(refs[i], refs[i + 1]) for i in range(0, len(refs), 2)]
    return [pairs[i : i + THIRDS] for i in range(0, len(pairs), THIRDS)]


def weight_scratch(units, width, slots):
    return [
        pltpu.VMEM((slots, units, width), bf16),
        pltpu.VMEM((slots, units, width), bf16),
        pltpu.SemaphoreType.DMA((slots, 2, THIRDS)),
        pltpu.SemaphoreType.DMA((2 * slots,)),
    ]


def kept_shapes(units, width, slots):
    return [jax.ShapeDtypeStruct((units, width), bf16)] * (2 * slots)


def flat_sets(sets):
    return [array for pairs in sets for pair in pairs for array in pair]


SMEM = pl.BlockSpec(memory_space=pltpu.SMEM)
VMEM = pl.BlockSpec(memory_space=pltpu.VMEM)
ANY = pl.BlockSpec(memory_space=pl.ANY)
HBM = pl.BlockSpec(memory_space=pltpu.HBM)
MIB = 2**20


def room(mebibytes):
    return pltpu.CompilerParams(vmem_limit_bytes=mebibytes * MIB)


def modulated(state, shift_row, scale_row):
    mean = jnp.mean(state, axis=1, keepdims=True)
    centred = state - mean
    var = jnp.mean(centred * centred, axis=1, keepdims=True)
    normed = centred * lax.rsqrt(var + EPSILON)
    return (normed * (1.0 + scale_row) + shift_row).astype(bf16)


def block_of(place, rows):
    return pl.ds(pl.multiple_of(place * rows, rows), rows)


def own_kernel(count, core_ref, state_ref, mod_ref, *refs):
    sets = as_sets(refs[:count])
    hidden_ref, acc_ref, *weights = refs[count:]
    kept, weights = weights[:2], weights[2:]
    start_set(core_ref, sets[0], *weights[:3], 0)
    tokens, width = state_ref.shape

    def one(place, carry):
        rows = block_of(place, ROWS)
        hidden_ref[rows, :] = modulated(
            state_ref[rows, :], mod_ref[OWN_ROW, 0:width], mod_ref[OWN_ROW, width : 2 * width]
        )
        return carry

    lax.fori_loop(0, tokens // ROWS, one, 0)
    mlp_sets(core_ref, sets, kept, hidden_ref, acc_ref, None, *weights)


def own_piece(core, state, mod, sets):
    weights = flat_sets(sets)
    units = THIRDS * weights[0].shape[0]
    tokens, width = state.shape
    return pl.pallas_call(
        functools.partial(own_kernel, len(weights)),
        out_shape=[jax.ShapeDtypeStruct((tokens, width), bf16), jax.ShapeDtypeStruct((tokens, width), f32)]
        + kept_shapes(units, width, 1),
        in_specs=[SMEM, VMEM, VMEM] + [ANY] * len(weights),
        out_specs=[VMEM, VMEM, HBM, HBM],
        scratch_shapes=weight_scratch(units, width, 1),
        compiler_params=room(56),
        name="own_piece",
    )(core, state, mod, *weights)


def next_kernel(count, core_ref, hidden_ref, acc_in, *refs):
    sets = as_sets(refs[:count])
    acc_ref, *weights = refs[count:]
    kept, weights = weights[:4], weights[4:]
    start_set(core_ref, sets[0], *weights[:3], 0)
    mlp_sets(core_ref, sets, kept, hidden_ref, acc_ref, acc_in, *weights)


def next_piece(core, hidden, acc, sets):
    weights = flat_sets(sets)
    units = THIRDS * weights[0].shape[0]
    tokens, width = hidden.shape
    return pl.pallas_call(
        functools.partial(next_kernel, len(weights)),
        out_shape=[jax.ShapeDtypeStruct((tokens, width), f32)] + kept_shapes(units, width, 2),
        in_specs=[SMEM, VMEM, VMEM] + [ANY] * len(weights),
        out_specs=[VMEM] + [HBM] * 4,
        scratch_shapes=weight_scratch(units, width, 2),
        compiler_params=room(56),
        name="next_piece",
    )(core, hidden, acc, *weights)


def far_kernel(
    count, core_ref, first_ref, begin_ref, dt_ref, sigma_ref, hidden_ref, acc_in, state_ref, noise_ref, mod_ref, *refs
):
    sets = as_sets(refs[:count])
    out_ref, up_kept, down_kept, acc_ref, state_buf, noise_buf, own_sems, *weights = refs[count:]
    start_set(core_ref, sets[0], *weights[:3], 0)
    own = [
        pltpu.make_async_copy(state_ref, state_buf, own_sems.at[0]),
        pltpu.make_async_copy(noise_ref, noise_buf, own_sems.at[1]),
    ]
    for copy in own:
        copy.start()
    mlp_sets(core_ref, sets, [up_kept, down_kept], hidden_ref, acc_ref, acc_in, *weights)
    for copy in own:
        copy.wait()
    peers, rows, width = out_ref.shape
    rows = rows // 2
    step = begin_ref[0]

    def one(peer, carry):
        place = block_of(peer, rows)
        state = state_buf[place, :]
        drift = mod_ref[OWN_ROW, 2 * width : 3 * width] * acc_ref[place, :] - state
        inc = dt_ref[step] * drift + sigma_ref[step] * noise_buf[0, place, :].astype(f32)
        out_ref[peer, 0:rows, :] = (inc + first_ref[0] * state).astype(bf16)
        out_ref[peer, rows : 2 * rows, :] = noise_buf[1, place, :]
        return carry

    lax.fori_loop(0, peers, one, 0)


def far_piece(core, is_first, step, dt, sigma, hidden, acc, state, noise, mod, sets, peers):
    weights = flat_sets(sets)
    units = THIRDS * weights[0].shape[0]
    tokens, width = hidden.shape
    return pl.pallas_call(
        functools.partial(far_kernel, len(weights)),
        out_shape=[jax.ShapeDtypeStruct((peers, 2 * (tokens // peers), width), bf16)]
        + kept_shapes(units, width, 1),
        in_specs=[SMEM] * 5 + [VMEM] * 2 + [ANY] * 2 + [VMEM] + [ANY] * len(weights),
        out_specs=[VMEM, HBM, HBM],
        scratch_shapes=[
            pltpu.VMEM((tokens, width), f32),
            pltpu.VMEM(state.shape, f32),
            pltpu.VMEM(noise.shape, bf16),
            pltpu.SemaphoreType.DMA((2,)),
        ]
        + weight_scratch(units, width, 1),
        compiler_params=room(56),
        name="far_piece",
    )(core, is_first, step, dt, sigma, hidden, acc, state, noise, mod, *weights)


def second_kernel(count, begin_ref, advance_ref, dt_ref, sigma_ref, got_ref, mod_ref, *refs):
    sets = [(refs[i], refs[i + 1]) for i in range(0, count, 2)]
    out_ref, prefix_ref, hidden_ref, acc_ref, up_buf, down_buf, sems = refs[count:]

    def copies(index):
        slot = index % 2
        return [
            pltpu.make_async_copy(sets[index][kind], buf.at[slot], sems.at[slot, kind, 0])
            for kind, buf in enumerate((up_buf, down_buf))
        ]

    for copy in copies(0):
        copy.start()
    window, rows, width = out_ref.shape
    advance = advance_ref[0]
    begin = begin_ref[0] + advance

    total = got_ref[0, 0:rows, :].astype(f32)
    for place in range(1, window + SLIDE):
        prefix_ref[place] = total
        if place < window:
            total = total + got_ref[place, 0:rows, :].astype(f32)

    def modulate(place, carry):
        row = pl.ds(place, 1)
        hidden_ref[block_of(place, rows), :] = modulated(
            prefix_ref[place + advance], mod_ref[row, 0:width], mod_ref[row, width : 2 * width]
        )
        return carry

    lax.fori_loop(0, window, modulate, 0)
    for index in range(len(sets)):
        if index + 1 < len(sets):
            for copy in copies(index + 1):
                copy.start()
        for copy in copies(index):
            copy.wait()
        part = mlp_part(hidden_ref[...], up_buf[index % 2], down_buf[index % 2])
        acc_ref[...] = part if index == 0 else acc_ref[...] + part

    def update(place, updated):
        out_ref[place] = updated.astype(bf16)
        gate = mod_ref[pl.ds(place, 1), 2 * width : 3 * width]
        drift = gate * acc_ref[block_of(place, rows), :] - prefix_ref[place + advance]
        noise = got_ref[place, rows : 2 * rows, :].astype(f32)
        return updated + (dt_ref[begin + place] * drift + sigma_ref[begin + place] * noise)

    lax.fori_loop(0, window, update, prefix_ref[advance])


def second_sweep(begin, advance, dt, sigma, got, mod, weights):
    units = weights[0].shape[0]
    window, rows, width = got.shape
    rows = rows // 2
    return pl.pallas_call(
        functools.partial(second_kernel, len(weights)),
        out_shape=jax.ShapeDtypeStruct((window, rows, width), bf16),
        in_specs=[SMEM] * 4 + [VMEM] * 2 + [HBM] * len(weights),
        out_specs=VMEM,
        scratch_shapes=[
            pltpu.VMEM((window + SLIDE, rows, width), f32),
            pltpu.VMEM((window * rows, width), bf16),
            pltpu.VMEM((window * rows, width), f32),
        ]
        + weight_scratch(units, width, 2)[:3],
        compiler_params=room(56),
        name="second_sweep",
    )(begin, advance, dt, sigma, got, mod, *weights)


def time_embed(steps_now, half_width):
    frequency = jnp.exp(-math.log(10000.0) * jnp.arange(half_width, dtype=f32) / half_width)
    angles = steps_now.astype(f32)[:, None] * frequency[None, :]
    return jnp.concatenate([jnp.cos(angles), jnp.sin(angles)], axis=1)


def after(array, *others):
    return lax.optimization_barrier((array, *others))[0]


def per_device(
    state, noise_draws, class_vec, window_start, advance, step_dt, step_sigma, w_ada, w_up, w_down
):
    window = lax.axis_size("tm")
    core = lax.axis_index("batch") % CORES
    core_arg = core.astype(jnp.int32)[None]
    state, noise = state[0, 0], noise_draws[:, 0, 0]
    tokens, width = state.shape

    other = swap_cores(jnp.where(core == 0, w_down, w_up))
    rows = jnp.where(
        core == 0, jnp.concatenate([w_up, other]), jnp.concatenate([other, w_down])
    )
    third = rows.shape[0] // THIRDS
    parts = [rows[i * third : (i + 1) * third] for i in range(THIRDS)]
    orders = [(0, 1, 2), (1, 2, 0), (2, 0, 1)]
    for phase in range(2):
        parts = [grow(part, order[phase], core) for part, order in zip(parts, orders)]

    begin, ahead = window_start[0], advance[0]
    own_step = begin + lax.axis_index("tm")
    steps = begin + ahead + jnp.arange(window, dtype=jnp.int32)
    steps = jnp.concatenate([steps, jnp.full((8,), own_step, jnp.int32)])
    condition = jax.nn.silu(time_embed(steps, width // 2) + class_vec).astype(bf16)
    modulation = jnp.dot(condition, w_ada, preferred_element_type=f32)
    is_first = (lax.axis_index("tm") == 0).astype(f32)[None]

    last = [order[2] for order in orders]
    parts = [after(part, *parts) for part in parts]
    first = [send(part, axis, True) for part, axis in zip(parts, last)]
    ready = [after(part, near, modulation) for part, near in zip(parts, first)]
    second = [send(part, axis, False) for part, axis in zip(ready, last)]
    own_swapped = [swap_cores(after(part, modulation)) for part in parts]
    first_swapped = [swap_cores(after(part, *own_swapped)) for part in first]
    set_own = list(zip(parts, own_swapped))
    hidden, acc, *kept = own_piece(core_arg, state, modulation, [set_own])
    far = [send(after(near, other, acc), axis, False) for near, other, axis in zip(first, second, last)]
    second_swapped = [swap_cores(part) for part in second]
    set_low = list(zip(first, second_swapped))
    set_high = list(zip(second, first_swapped))
    acc, *more = next_piece(core_arg, hidden, acc, [set_low, set_high])
    kept += more

    far_swapped = [swap_cores(after(part, acc)) for part in far]
    set_far = list(zip(far, far_swapped))
    sent, *more = far_piece(
        core_arg, is_first, own_step[None], step_dt, step_sigma, hidden, acc, state, noise, modulation, [set_far], window
    )
    got = lax.all_to_all(sent, "tm", 0, 0, tiled=True)
    updated = second_sweep(
        window_start,
        advance,
        step_dt,
        step_sigma,
        got,
        modulation,
        kept + more,
    )
    final = lax.all_to_all(updated, "tm", 0, 0, tiled=True)
    return final.reshape(1, 1, tokens, width).astype(f32)


def solution(mesh):
    in_specs = (
        P("tm", "batch", None, None),
        P(None, "tm", "batch", None, None),
        P("batch", None),
        P("batch"),
        P("batch"),
        P(),
        P(),
        P(),
        P(("tm", "batch"), None),
        P(("tm", "batch"), None),
    )
    out_specs = P("tm", "batch", None, None)
    return jax.shard_map(
        per_device, mesh=mesh, in_specs=in_specs, out_specs=out_specs, check_vma=False
    )
```

time: 198 us -> 166 us (0.84)
  waiting for transfers between devices: 72.5 us -> 28.3 us
  blocking collectives: 17.1 us -> 40.1 us
  local copies, waits for them, and re-layouts: 23.9 us -> 6.98 us
  Pallas kernels: 32.5 us -> 40.7 us
    all_to_all x0 -> x1, blocking collectives: none -> 24.7 us  [per_device(): got = lax.all_to_all(sent, 'tm', 0, 0, tiled=True)]
    all_to_all x1 -> x0, waiting for transfers between devices: 23.9 us -> none  [per_device(): got = lax.all_to_all(sent, 'tm', 0, 0, tiled=True)]
    ppermute x21, waiting for transfers between devices: 47.2 us -> 24 us  [send(): return lax.ppermute(rows, ALL, neighbour(axis, first))]
    unnamed x67 -> x49, local copies, waits for them, and re-layouts: 15.6 us -> 5.44 us
    pallas_call x3, Pallas kernels: 17.3 us -> 26.7 us  [the longest x1 10.4 us: next_piece(): pl.pallas_call(functools.partial(next_kernel, len(weights)), out_shape=[j...]
    all_to_all x1 -> x0, starting transfers between devices: 4.55 us -> none  [per_device(): got = lax.all_to_all(sent, 'tm', 0, 0, tiled=True)]
    dynamic_slice x4 -> x0, local copies, waits for them, and re-layouts: 4.2 us -> none  [the longest x1 1.4 us: per_device(): lax.dynamic_index_in_dim(step_sigma, begin + position, 0, False)]
    ppermute x21, starting transfers between devices: 28.8 us -> 32.3 us  [send(): return lax.ppermute(rows, ALL, neighbour(axis, first))]
  transfers between devices with their start and end apart: 35 -> 34, of which waited for: 11 -> 13; matrix products, arithmetic and copies ran while one was open for 10% -> 7% of each run, Pallas kernels for 5% -> 11%
where the time goes in v2:
time: 166 us; the launch traced here: 165 us
  Pallas kernels  40.7 us (25%)
  blocking collectives  40.1 us (24%)
  starting transfers between devices  34.8 us (21%)
  waiting for transfers between devices  28.3 us (17%)
  other arithmetic  7.62 us (5%)
  local copies, waits for them, and re-layouts  6.98 us (4%)
  matrix products  5.2 us (3%)
    ppermute x21, starting transfers between devices, send(): return lax.ppermute(rows, ALL, neighbour(axis, first))  32.3 us
    all_to_all x1, blocking collectives, per_device(): got = lax.all_to_all(sent, 'tm', 0, 0, tiled=True)  24.7 us
    ppermute x21, waiting for transfers between devices, send(): return lax.ppermute(rows, ALL, neighbour(axis, first))  24 us
    all_to_all x1, blocking collectives, per_device(): final = lax.all_to_all(updated, 'tm', 0, 0, tiled=True)  15.4 us
    pallas_call x1, Pallas kernels, second_sweep(): pl.pallas_call(functools.partial(second_kernel, len(weights)), out_shape=...  14.1 us
    pallas_call x1, Pallas kernels, next_piece(): pl.pallas_call(functools.partial(next_kernel, len(weights)), out_shape=[j...  10.4 us
    pallas_call x1, Pallas kernels, own_piece(): pl.pallas_call(functools.partial(own_kernel, len(weights)), out_shape=[ja...  8.32 us
    pallas_call x1, Pallas kernels, far_piece(): pl.pallas_call(functools.partial(far_kernel, len(weights)), out_shape=[ja...  7.96 us
  transfers between devices with their start and end apart: 34, of which 13 were waited for; matrix products, arithmetic and copies ran while one was open for 7% of the time, Pallas kernels for 11%

profile of v2, /device:TPU:0, one launch (start us, length us, event | category | flops | bytes accessed | tf_op | source)
XLA Modules:
  0.0 165.3 jit_solution(3404773421538880569)
XLA Ops:
  0.0 0.9 broadcast_select_fusion
  2.3 1.0 maximum_select_fusion
  3.3 0.7 fusion.5
  4.0 1.6 collective-permute-start.1
  5.6 1.6 collective-permute-start.9
  7.2 1.9 %collective-permute-start.5 = (bf16[24,1152]{1,0:T(8,128)(2,1)S(1)}, bf16[24,1152]{1,0:T(8,128)(2,1)S(1)}, u32[]{:S(2)}, u32[]{:S(2)}) collective-permute-start(bf16[24,1152]{1,0:T(8,128)(2,1)S(1)} %get-tuple-element.84), channel_id=1, source_target_pairs={{0,8},{1,25},{2,10},{3,27},{4,12},{5,29},{6,14},{7,31},{8,0},{9,17... | collective-permute-start | bytes 165896 | tf_op jit(solution)/shard_map/ppermute | solution.py:45
  9.1 2.2 %collective-permute-start.2 = (bf16[48,1152]{1,0:T(8,128)(2,1)S(1)}, bf16[48,1152]{1,0:T(8,128)(2,1)S(1)}, u32[]{:S(2)}, u32[]{:S(2)}) collective-permute-start(bf16[48,1152]{1,0:T(8,128)(2,1)S(1)} %pad_maximum_fusion.3), channel_id=1, source_target_pairs={{0,96},{1,33},{2,98},{3,35},{4,100},{5,37},{6,102},{7,39},{8,104},... | collective-permute-start | bytes 331784 | tf_op jit(solution)/shard_map/ppermute | solution.py:45
  11.3 2.9 %collective-permute-start.10 = (bf16[48,1152]{1,0:T(8,128)(2,1)S(1)}, bf16[48,1152]{1,0:T(8,128)(2,1)S(1)}, u32[]{:S(2)}, u32[]{:S(2)}) collective-permute-start(bf16[48,1152]{1,0:T(8,128)(2,1)S(1)} %pad_maximum_fusion.5), channel_id=1, source_target_pairs={{0,6},{1,3},{2,4},{3,1},{4,2},{5,7},{6,0},{7,5},{8,14},{9,11},{10,... | collective-permute-start | bytes 331784 | tf_op jit(solution)/shard_map/ppermute | solution.py:45
  14.2 4.1 %collective-permute-start.6 = (bf16[48,1152]{1,0:T(8,128)(2,1)S(1)}, bf16[48,1152]{1,0:T(8,128)(2,1)S(1)}, u32[]{:S(2)}, u32[]{:S(2)}) collective-permute-start(bf16[48,1152]{1,0:T(8,128)(2,1)S(1)} %pad_maximum_fusion.4), channel_id=1, source_target_pairs={{0,24},{1,9},{2,26},{3,11},{4,28},{5,13},{6,30},{7,15},{8,16},{9,1... | collective-permute-start | bytes 331784 | tf_op jit(solution)/shard_map/ppermute | solution.py:45
  18.4 0.6 constant_dynamic-update-slice_fusion.3
  19.0 0.6 constant_dynamic-update-slice_fusion.2
  19.7 0.6 constant_dynamic-update-slice_fusion.1
  20.4 0.6 constant_dynamic-update-slice_fusion.21
  21.1 0.6 constant_dynamic-update-slice_fusion.20
  21.7 0.6 constant_dynamic-update-slice_fusion.19
  22.4 0.3 collective-permute-start.11
  22.8 0.2 collective-permute-start.7
  23.1 3.3 %collective-permute-done.3 = bf16[96,1152]{1,0:T(8,128)(2,1)S(1)} collective-permute-done((bf16[96,1152]{1,0:T(8,128)(2,1)S(1)}, bf16[96,1152]{1,0:T(8,128)(2,1)S(1)}, u32[]{:S(2)}, u32[]{:S(2)}) %collective-permute-start.3) | collective-permute-done | bytes 221216 | tf_op jit(solution)/shard_map/ppermute | solution.py:45
  26.4 0.1 collective-permute-start.4
  26.5 1.9 %collective-permute-done.11 = bf16[96,1152]{1,0:T(8,128)(2,1)S(1)} collective-permute-done((bf16[96,1152]{1,0:T(8,128)(2,1)S(1)}, bf16[96,1152]{1,0:T(8,128)(2,1)S(1)}, u32[]{:S(2)}, u32[]{:S(2)}) %collective-permute-start.11) | collective-permute-done | bytes 221216 | tf_op jit(solution)/shard_map/ppermute | solution.py:45
  28.4 0.7 constant_dynamic-update-slice_fusion.18
  29.1 0.8 collective-permute-start.12
  29.9 3.1 %collective-permute-start.8 = (bf16[192,1152]{1,0:T(8,128)(2,1)S(1)}, bf16[192,1152]{1,0:T(8,128)(2,1)S(1)}, u32[]{:S(2)}, u32[]{:S(2)}) collective-permute-start(bf16[192,1152]{1,0:T(8,128)(2,1)S(1)} %constant_dynamic-update-slice_fusion.9), channel_id=1, source_target_pairs={{0,6},{1,3},{2,4},{3,1},{4,2},{5,7},{6,0},{7,5},{8,14},{9,11},{10,... | collective-permute-start | bytes 1327112 | tf_op jit(solution)/shard_map/ppermute | solution.py:45
  33.0 2.9 %collective-permute-done.4 = bf16[192,1152]{1,0:T(8,128)(2,1)S(1)} collective-permute-done((bf16[192,1152]{1,0:T(8,128)(2,1)S(1)}, bf16[192,1152]{1,0:T(8,128)(2,1)S(1)}, u32[]{:S(2)}, u32[]{:S(2)}) %collective-permute-start.4) | collective-permute-done | bytes 442400 | tf_op jit(solution)/shard_map/ppermute | solution.py:45
  36.1 2.7 %collective-permute-done.12 = bf16[192,1152]{1,0:T(8,128)(2,1)S(1)} collective-permute-done((bf16[192,1152]{1,0:T(8,128)(2,1)}, bf16[192,1152]{1,0:T(8,128)(2,1)S(1)}, u32[]{:S(2)}, u32[]{:S(2)}) %collective-permute-start.12) | collective-permute-done | bytes 442400 | tf_op jit(solution)/shard_map/ppermute | solution.py:45
  38.8 0.7 collective-permute-done.8
  39.5 0.1 select_dynamic-update-slice_fusion.1
  39.9 0.4 collective-permute-start.16
  40.3 0.5 collective-permute-start.19
  40.8 2.0 %collective-permute-start.22 = (bf16[384,1152]{1,0:T(8,128)(2,1)S(1)}, bf16[384,1152]{1,0:T(8,128)(2,1)S(1)}, u32[]{:S(2)}, u32[]{:S(2)}) collective-permute-start(bf16[384,1152]{1,0:T(8,128)(2,1)S(1)} %slice_dynamic-update-slice_fusion.refs_4_), channel_id=1, source_target_pairs={{0,8},{1,25},{2,10},{3,27},{4,12},{5,29},{6,14},{7,31},{8,0},{9,17... | collective-permute-start | bytes 2654216 | tf_op jit(solution)/shard_map/ppermute | solution.py:45
  42.8 0.5 pad_convert_fusion
  43.4 1.0 multiply_cosine_fusion
  44.3 5.2 %fusion.mod_ref = f32[24,3456]{1,0:T(8,128)} fusion(bf16[1152,3456]{1,0:T(8,128)(2,1)} %param.17, f32[24,576]{1,0:T(8,128)S(1)} %get-tuple-element.96, f32[24,576]{1,0:T(8,128)S(1)} %get-tuple-element.95, f32[1152]{0:T(1024)S(1)} %reduce), kind=kOutput, calls=%fused_computation.48 | convolution fusion | flops 191296512 | bytes 8409600 | tf_op jit(solution)/shard_map/dot_general | solution.py:379
  49.5 0.5 collective-permute-start.14
  50.0 3.1 %collective-permute-done.16.refs_0_ = bf16[384,1152]{1,0:T(8,128)(2,1)} collective-permute-done((bf16[384,1152]{1,0:T(8,128)(2,1)S(1)}, bf16[384,1152]{1,0:T(8,128)(2,1)}, u32[]{:S(2)}, u32[]{:S(2)}) %collective-permute-start.16) | collective-permute-done | bytes 884768 | tf_op jit(solution)/shard_map/ppermute | solution.py:45
  53.1 0.4 collective-permute-done.19.refs_2_
  53.5 2.7 %collective-permute-start.17 = (bf16[384,1152]{1,0:T(8,128)(2,1)S(1)}, bf16[384,1152]{1,0:T(8,128)(2,1)S(1)}, u32[]{:S(2)}, u32[]{:S(2)}) collective-permute-start(bf16[384,1152]{1,0:T(8,128)(2,1)S(1)} %slice_dynamic-update-slice_fusion.2.refs_0_), channel_id=1, source_target_pairs={{0,6},{1,3},{2,4},{3,1},{4,2},{5,7},{6,0},{7,5},{8,14},{9,11},{10,... | collective-permute-start | bytes 2654216 | tf_op jit(solution)/shard_map/ppermute | solution.py:45
  56.2 0.8 collective-permute-start.20
  57.1 2.5 %collective-permute-start.23 = (bf16[384,1152]{1,0:T(8,128)(2,1)S(1)}, bf16[384,1152]{1,0:T(8,128)(2,1)S(1)}, u32[]{:S(2)}, u32[]{:S(2)}) collective-permute-start(bf16[384,1152]{1,0:T(8,128)(2,1)S(1)} %slice_dynamic-update-slice_fusion.refs_4_), channel_id=1, source_target_pairs={{0,24},{1,9},{2,26},{3,11},{4,28},{5,13},{6,30},{7,15},{8,16},{9,1... | collective-permute-start | bytes 2654216 | tf_op jit(solution)/shard_map/ppermute | solution.py:45
  59.6 0.9 copy-done.13
  60.5 0.9 copy-done.14
  61.4 0.5 collective-permute-start.26
  61.9 5.8 %collective-permute-done.17.refs_6_ = bf16[384,1152]{1,0:T(8,128)(2,1)S(1)} collective-permute-done((bf16[384,1152]{1,0:T(8,128)(2,1)S(1)}, bf16[384,1152]{1,0:T(8,128)(2,1)S(1)}, u32[]{:S(2)}, u32[]{:S(2)}) %collective-permute-start.17) | collective-permute-done | bytes 884768 | tf_op jit(solution)/shard_map/ppermute | solution.py:45
  67.8 2.8 %collective-permute-done.20.refs_8_ = bf16[384,1152]{1,0:T(8,128)(2,1)S(1)} collective-permute-done((bf16[384,1152]{1,0:T(8,128)(2,1)S(1)}, bf16[384,1152]{1,0:T(8,128)(2,1)S(1)}, u32[]{:S(2)}, u32[]{:S(2)}) %collective-permute-start.20) | collective-permute-done | bytes 884768 | tf_op jit(solution)/shard_map/ppermute | solution.py:45
  70.6 8.3 %own_piece.1 = (bf16[256,1152]{1,0:T(8,128)(2,1)}, f32[256,1152]{1,0:T(8,128)}, bf16[1152,1152]{1,0:T(8,128)(2,1)}, bf16[1152,1152]{1,0:T(8,128)(2,1)}) custom-call(s32[1]{0:T(128)} %bitcast.core_ref, f32[256,1152]{1,0:T(8,128)} %bitcast.13, f32[24,3456]{1,0:T(8,128)} %fusion.mod_ref, bf16[384,1152]{1,0:T(8,128)(2,1)} %copy-done.2, ...), custom_call_target="tpu_custom_call" | custom-call | tf_op jit(solution)/shard_map/own_piece/pallas_call | solution.py:187
  79.0 0.4 collective-permute-start.21
  79.4 0.3 collective-permute-start.24
  79.7 0.5 collective-permute-start.28
  80.2 2.2 %collective-permute-start.30 = (bf16[384,1152]{1,0:T(8,128)(2,1)}, bf16[384,1152]{1,0:T(8,128)(2,1)}, u32[]{:S(2)}, u32[]{:S(2)}) collective-permute-start(bf16[384,1152]{1,0:T(8,128)(2,1)} %collective-permute-done.19.refs_2_), channel_id=1, source_target_pairs={{0,96},{1,33},{2,98},{3,35},{4,100},{5,37},{6,102},{7,39},{8,104},... | collective-permute-start | bytes 2654216 | tf_op jit(solution)/shard_map/ppermute | solution.py:45
  82.4 1.8 %collective-permute-start.32 = (bf16[384,1152]{1,0:T(8,128)(2,1)S(1)}, bf16[384,1152]{1,0:T(8,128)(2,1)}, u32[]{:S(2)}, u32[]{:S(2)}) collective-permute-start(bf16[384,1152]{1,0:T(8,128)(2,1)S(1)} %collective-permute-done.22.refs_4_), channel_id=1, source_target_pairs={{0,24},{1,9},{2,26},{3,11},{4,28},{5,13},{6,30},{7,15},{8,16},{9,1... | collective-permute-start | bytes 2654216 | tf_op jit(solution)/shard_map/ppermute | solution.py:45
  84.3 0.9 copy-done.12
  85.2 0.3 copy-done.11
  85.5 10.4 %next_piece.1 = (f32[256,1152]{1,0:T(8,128)}, bf16[1152,1152]{1,0:T(8,128)(2,1)}, bf16[1152,1152]{1,0:T(8,128)(2,1)}, bf16[1152,1152]{1,0:T(8,128)(2,1)}, bf16[1152,1152]{1,0:T(8,128)(2,1)}) custom-call(s32[1]{0:T(128)} %bitcast.core_ref, bf16[256,1152]{1,0:T(8,128)(2,1)} %get-tuple-element.41.hidden_ref, f32[256,1152]{1,0:T(8,128)} %get-tuple-element.42.acc_in, ...), custom_call_target="tpu_custom_call" | custom-call | tf_op jit(solution)/shard_map/next_piece/pallas_call | solution.py:211
  96.0 0.5 collective-permute-start.31
  96.5 0.3 collective-permute-done.32.refs_4_
  96.9 1.8 %collective-permute-done.29.refs_1_ = bf16[384,1152]{1,0:T(8,128)(2,1)S(1)} collective-permute-done((bf16[384,1152]{1,0:T(8,128)(2,1)}, bf16[384,1152]{1,0:T(8,128)(2,1)S(1)}, u32[]{:S(2)}, u32[]{:S(2)}) %collective-permute-start.29) | collective-permute-done | bytes 884768 | tf_op jit(solution)/shard_map/ppermute | solution.py:49
  98.7 1.3 collective-permute-done.31.refs_3_
  99.9 1.3 collective-permute-done.33.refs_5_
  101.2 0.9 copy-done.17
  102.1 8.0 %far_piece.1 = (bf16[16,32,1152]{2,1,0:T(8,128)(2,1)}, bf16[1152,1152]{1,0:T(8,128)(2,1)}, bf16[1152,1152]{1,0:T(8,128)(2,1)}) custom-call(s32[1]{0:T(128)} %bitcast.core_ref, f32[1]{0:T(128)} %bitcast.1.first_ref, s32[1]{0:T(128)} %bitcast.3.begin_ref, f32[1000]{0:T(1024)} %dt_ref.3, f32[1000]{0:T(1024)} %sigma_ref.3, ...), custom_call_target="tpu_custom_call" | custom-call | tf_op jit(solution)/shard_map/far_piece/pallas_call | solution.py:257
  110.1 24.7 %all_to_all.10.got_ref = bf16[16,32,1152]{2,1,0:T(8,128)(2,1)} all-to-all(bf16[16,32,1152]{2,1,0:T(8,128)(2,1)} %get-tuple-element.56), channel_id=1, replica_groups=mesh['tm'=16,'batch'=8] {'tm'}, dimensions={0} | all-to-all | bytes 2359296 | tf_op jit(solution)/shard_map/all_to_all | solution.py:403
  134.8 14.1 %second_sweep.1 = bf16[16,16,1152]{2,1,0:T(8,128)(2,1)} custom-call(s32[1]{0:T(128)} %copy.41.begin_ref, s32[1]{0:T(128)} %copy.42.advance_ref, f32[1000]{0:T(1024)} %dt_ref.3, f32[1000]{0:T(1024)} %sigma_ref.3, bf16[16,32,1152]{2,1,0:T(8,128)(2,1)} %all_to_all.10.got_ref, f32[24,3456]{1,0:T(8,128)} %fusion.mod_ref, ...), custom_call_target="tpu_custom_call" | custom-call | tf_op jit(solution)/shard_map/second_sweep/pallas_call | solution.py:329
  148.9 15.4 %all_to_all.11 = bf16[16,16,1152]{2,1,0:T(8,128)(2,1)S(1)} all-to-all(bf16[16,16,1152]{2,1,0:T(8,128)(2,1)} %second_sweep.1), channel_id=1, replica_groups=mesh['tm'=16,'batch'=8] {'tm'}, dimensions={0} | all-to-all | bytes 1179648 | tf_op jit(solution)/shard_map/all_to_all | solution.py:413
  164.2 1.1 convert.2
  (92 shorter events, 1.1 us)
Async XLA Ops:
  0.9 1.4 collective-permute-start
  4.0 5.1 %collective-permute-start.1 = (bf16[24,1152]{1,0:T(8,128)(2,1)S(1)}, bf16[24,1152]{1,0:T(8,128)(2,1)S(1)}, u32[]{:S(2)}, u32[]{:S(2)}) collective-permute-start(bf16[24,1152]{1,0:T(8,128)(2,1)S(1)} %get-tuple-element.85), channel_id=1, source_target_pairs={{0,32},{1,97},{2,34},{3,99},{4,36},{5,101},{6,38},{7,103},{8,40},{... | collective-permute-start | bytes 165896 | tf_op jit(solution)/shard_map/ppermute | solution.py:45
  5.6 5.7 %collective-permute-start.9 = (bf16[24,1152]{1,0:T(8,128)(2,1)S(1)}, bf16[24,1152]{1,0:T(8,128)(2,1)S(1)}, u32[]{:S(2)}, u32[]{:S(2)}) collective-permute-start(bf16[24,1152]{1,0:T(8,128)(2,1)S(1)} %get-tuple-element.77), channel_id=1, source_target_pairs={{0,2},{1,7},{2,0},{3,5},{4,6},{5,3},{6,4},{7,1},{8,10},{9,15},{10,... | collective-permute-start | bytes 165896 | tf_op jit(solution)/shard_map/ppermute | solution.py:45
  7.2 7.0 %collective-permute-start.5 = (bf16[24,1152]{1,0:T(8,128)(2,1)S(1)}, bf16[24,1152]{1,0:T(8,128)(2,1)S(1)}, u32[]{:S(2)}, u32[]{:S(2)}) collective-permute-start(bf16[24,1152]{1,0:T(8,128)(2,1)S(1)} %get-tuple-element.84), channel_id=1, source_target_pairs={{0,8},{1,25},{2,10},{3,27},{4,12},{5,29},{6,14},{7,31},{8,0},{9,17... | collective-permute-start | bytes 165896 | tf_op jit(solution)/shard_map/ppermute | solution.py:45
  9.1 9.2 %collective-permute-start.2 = (bf16[48,1152]{1,0:T(8,128)(2,1)S(1)}, bf16[48,1152]{1,0:T(8,128)(2,1)S(1)}, u32[]{:S(2)}, u32[]{:S(2)}) collective-permute-start(bf16[48,1152]{1,0:T(8,128)(2,1)S(1)} %pad_maximum_fusion.3), channel_id=1, source_target_pairs={{0,96},{1,33},{2,98},{3,35},{4,100},{5,37},{6,102},{7,39},{8,104},... | collective-permute-start | bytes 331784 | tf_op jit(solution)/shard_map/ppermute | solution.py:45
  11.3 9.1 %collective-permute-start.10 = (bf16[48,1152]{1,0:T(8,128)(2,1)S(1)}, bf16[48,1152]{1,0:T(8,128)(2,1)S(1)}, u32[]{:S(2)}, u32[]{:S(2)}) collective-permute-start(bf16[48,1152]{1,0:T(8,128)(2,1)S(1)} %pad_maximum_fusion.5), channel_id=1, source_target_pairs={{0,6},{1,3},{2,4},{3,1},{4,2},{5,7},{6,0},{7,5},{8,14},{9,11},{10,... | collective-permute-start | bytes 331784 | tf_op jit(solution)/shard_map/ppermute | solution.py:45
  14.2 8.5 %collective-permute-start.6 = (bf16[48,1152]{1,0:T(8,128)(2,1)S(1)}, bf16[48,1152]{1,0:T(8,128)(2,1)S(1)}, u32[]{:S(2)}, u32[]{:S(2)}) collective-permute-start(bf16[48,1152]{1,0:T(8,128)(2,1)S(1)} %pad_maximum_fusion.4), channel_id=1, source_target_pairs={{0,24},{1,9},{2,26},{3,11},{4,28},{5,13},{6,30},{7,15},{8,16},{9,1... | collective-permute-start | bytes 331784 | tf_op jit(solution)/shard_map/ppermute | solution.py:45
  20.3 6.0 %copy-start.18 = (bf16[192,1152]{1,0:T(8,128)(2,1)S(1)}, bf16[192,1152]{1,0:T(8,128)(2,1)}, u32[]{:S(2)}) copy-start(bf16[192,1152]{1,0:T(8,128)(2,1)} %get-tuple-element.92) | copy-start | bytes 1327108
  20.3 6.0 %collective-permute-start.3 = (bf16[96,1152]{1,0:T(8,128)(2,1)S(1)}, bf16[96,1152]{1,0:T(8,128)(2,1)S(1)}, u32[]{:S(2)}, u32[]{:S(2)}) collective-permute-start(bf16[96,1152]{1,0:T(8,128)(2,1)S(1)} %pad_maximum_fusion), channel_id=1, source_target_pairs={{0,8},{1,25},{2,10},{3,27},{4,12},{5,29},{6,14},{7,31},{8,0},{9,17... | collective-permute-start | bytes 663560 | tf_op jit(solution)/shard_map/ppermute | solution.py:45
  22.4 6.0 %collective-permute-start.11 = (bf16[96,1152]{1,0:T(8,128)(2,1)S(1)}, bf16[96,1152]{1,0:T(8,128)(2,1)S(1)}, u32[]{:S(2)}, u32[]{:S(2)}) collective-permute-start(bf16[96,1152]{1,0:T(8,128)(2,1)S(1)} %pad_maximum_fusion.2), channel_id=1, source_target_pairs={{0,32},{1,97},{2,34},{3,99},{4,36},{5,101},{6,38},{7,103},{8,40},{... | collective-permute-start | bytes 663560 | tf_op jit(solution)/shard_map/ppermute | solution.py:45
  22.8 7.1 %collective-permute-start.7 = (bf16[96,1152]{1,0:T(8,128)(2,1)S(1)}, bf16[96,1152]{1,0:T(8,128)(2,1)S(1)}, u32[]{:S(2)}, u32[]{:S(2)}) collective-permute-start(bf16[96,1152]{1,0:T(8,128)(2,1)S(1)} %pad_maximum_fusion.1), channel_id=1, source_target_pairs={{0,2},{1,7},{2,0},{3,5},{4,6},{5,3},{6,4},{7,1},{8,10},{9,15},{10,... | collective-permute-start | bytes 663560 | tf_op jit(solution)/shard_map/ppermute | solution.py:45
  26.4 9.6 %collective-permute-start.4 = (bf16[192,1152]{1,0:T(8,128)(2,1)S(1)}, bf16[192,1152]{1,0:T(8,128)(2,1)S(1)}, u32[]{:S(2)}, u32[]{:S(2)}) collective-permute-start(bf16[192,1152]{1,0:T(8,128)(2,1)S(1)} %constant_dynamic-update-slice_fusion), channel_id=1, source_target_pairs={{0,24},{1,9},{2,26},{3,11},{4,28},{5,13},{6,30},{7,15},{8,16},{9,1... | collective-permute-start | bytes 1327112 | tf_op jit(solution)/shard_map/ppermute | solution.py:45
  29.1 9.7 %collective-permute-start.12 = (bf16[192,1152]{1,0:T(8,128)(2,1)}, bf16[192,1152]{1,0:T(8,128)(2,1)S(1)}, u32[]{:S(2)}, u32[]{:S(2)}) collective-permute-start(bf16[192,1152]{1,0:T(8,128)(2,1)} %constant_dynamic-update-slice_fusion.18), channel_id=1, source_target_pairs={{0,96},{1,33},{2,98},{3,35},{4,100},{5,37},{6,102},{7,39},{8,104},... | collective-permute-start | bytes 1327112 | tf_op jit(solution)/shard_map/ppermute | solution.py:45
  29.9 9.6 %collective-permute-start.8 = (bf16[192,1152]{1,0:T(8,128)(2,1)S(1)}, bf16[192,1152]{1,0:T(8,128)(2,1)S(1)}, u32[]{:S(2)}, u32[]{:S(2)}) collective-permute-start(bf16[192,1152]{1,0:T(8,128)(2,1)S(1)} %constant_dynamic-update-slice_fusion.9), channel_id=1, source_target_pairs={{0,6},{1,3},{2,4},{3,1},{4,2},{5,7},{6,0},{7,5},{8,14},{9,11},{10,... | collective-permute-start | bytes 1327112 | tf_op jit(solution)/shard_map/ppermute | solution.py:45
  36.0 7.4 %copy-start.19 = (f32[1,1152]{1,0:T(1,128)S(1)}, f32[1,1152]{1,0:T(1,128)}, u32[]{:S(2)}) copy-start(f32[1,1152]{1,0:T(1,128)} %param.12) | copy-start | bytes 13828
  36.1 17.4 %copy-start.2 = (bf16[384,1152]{1,0:T(8,128)(2,1)}, bf16[384,1152]{1,0:T(8,128)(2,1)S(1)}, u32[]{:S(2)}) copy-start(bf16[384,1152]{1,0:T(8,128)(2,1)S(1)} %slice_dynamic-update-slice_fusion.2.refs_0_) | copy-start | bytes 2654212
  39.8 16.5 %copy-start = (bf16[384,1152]{1,0:T(8,128)(2,1)}, bf16[384,1152]{1,0:T(8,128)(2,1)S(1)}, u32[]{:S(2)}) copy-start(bf16[384,1152]{1,0:T(8,128)(2,1)S(1)} %slice_dynamic-update-slice_fusion.1.refs_2_) | copy-start | bytes 2654212
  39.9 17.2 %copy-start.1 = (bf16[384,1152]{1,0:T(8,128)(2,1)}, bf16[384,1152]{1,0:T(8,128)(2,1)S(1)}, u32[]{:S(2)}) copy-start(bf16[384,1152]{1,0:T(8,128)(2,1)S(1)} %slice_dynamic-update-slice_fusion.refs_4_) | copy-start | bytes 2654212
  39.9 13.2 %collective-permute-start.16 = (bf16[384,1152]{1,0:T(8,128)(2,1)S(1)}, bf16[384,1152]{1,0:T(8,128)(2,1)}, u32[]{:S(2)}, u32[]{:S(2)}) collective-permute-start(bf16[384,1152]{1,0:T(8,128)(2,1)S(1)} %slice_dynamic-update-slice_fusion.2.refs_0_), channel_id=1, source_target_pairs={{0,2},{1,7},{2,0},{3,5},{4,6},{5,3},{6,4},{7,1},{8,10},{9,15},{10,... | collective-permute-start | bytes 2654216 | tf_op jit(solution)/shard_map/ppermute | solution.py:45
  40.3 13.1 %collective-permute-start.19 = (bf16[384,1152]{1,0:T(8,128)(2,1)S(1)}, bf16[384,1152]{1,0:T(8,128)(2,1)}, u32[]{:S(2)}, u32[]{:S(2)}) collective-permute-start(bf16[384,1152]{1,0:T(8,128)(2,1)S(1)} %slice_dynamic-update-slice_fusion.1.refs_2_), channel_id=1, source_target_pairs={{0,32},{1,97},{2,34},{3,99},{4,36},{5,101},{6,38},{7,103},{8,40},{... | collective-permute-start | bytes 2654216 | tf_op jit(solution)/shard_map/ppermute | solution.py:45
  40.8 15.4 %collective-permute-start.22 = (bf16[384,1152]{1,0:T(8,128)(2,1)S(1)}, bf16[384,1152]{1,0:T(8,128)(2,1)S(1)}, u32[]{:S(2)}, u32[]{:S(2)}) collective-permute-start(bf16[384,1152]{1,0:T(8,128)(2,1)S(1)} %slice_dynamic-update-slice_fusion.refs_4_), channel_id=1, source_target_pairs={{0,8},{1,25},{2,10},{3,27},{4,12},{5,29},{6,14},{7,31},{8,0},{9,17... | collective-permute-start | bytes 2654216 | tf_op jit(solution)/shard_map/ppermute | solution.py:45
  49.5 7.6 %collective-permute-start.13 = (bf16[384,1152]{1,0:T(8,128)(2,1)S(1)}, bf16[384,1152]{1,0:T(8,128)(2,1)}, u32[]{:S(2)}, u32[]{:S(2)}) collective-permute-start(bf16[384,1152]{1,0:T(8,128)(2,1)S(1)} %slice_dynamic-update-slice_fusion.2.refs_0_), channel_id=1, source_target_pairs={{0,1},{1,0},{2,3},{3,2},{4,5},{5,4},{6,7},{7,6},{8,9},{9,8},{10,11... | collective-permute-start | bytes 2654216 | tf_op jit(solution)/shard_map/ppermute | solution.py:49
  49.5 10.0 %collective-permute-start.14 = (bf16[384,1152]{1,0:T(8,128)(2,1)S(1)}, bf16[384,1152]{1,0:T(8,128)(2,1)S(1)}, u32[]{:S(2)}, u32[]{:S(2)}) collective-permute-start(bf16[384,1152]{1,0:T(8,128)(2,1)S(1)} %slice_dynamic-update-slice_fusion.1.refs_2_), channel_id=1, source_target_pairs={{0,1},{1,0},{2,3},{3,2},{4,5},{5,4},{6,7},{7,6},{8,9},{9,8},{10,11... | collective-permute-start | bytes 2654216 | tf_op jit(solution)/shard_map/ppermute | solution.py:49
  53.1 7.4 %collective-permute-start.15 = (bf16[384,1152]{1,0:T(8,128)(2,1)S(1)}, bf16[384,1152]{1,0:T(8,128)(2,1)S(1)}, u32[]{:S(2)}, u32[]{:S(2)}) collective-permute-start(bf16[384,1152]{1,0:T(8,128)(2,1)S(1)} %slice_dynamic-update-slice_fusion.refs_4_), channel_id=1, source_target_pairs={{0,1},{1,0},{2,3},{3,2},{4,5},{5,4},{6,7},{7,6},{8,9},{9,8},{10,11... | collective-permute-start | bytes 2654216 | tf_op jit(solution)/shard_map/ppermute | solution.py:49
  53.5 14.3 %collective-permute-start.17 = (bf16[384,1152]{1,0:T(8,128)(2,1)S(1)}, bf16[384,1152]{1,0:T(8,128)(2,1)S(1)}, u32[]{:S(2)}, u32[]{:S(2)}) collective-permute-start(bf16[384,1152]{1,0:T(8,128)(2,1)S(1)} %slice_dynamic-update-slice_fusion.2.refs_0_), channel_id=1, source_target_pairs={{0,6},{1,3},{2,4},{3,1},{4,2},{5,7},{6,0},{7,5},{8,14},{9,11},{10,... | collective-permute-start | bytes 2654216 | tf_op jit(solution)/shard_map/ppermute | solution.py:45
  56.2 26.2 %copy-start.3 = (bf16[384,1152]{1,0:T(8,128)(2,1)}, bf16[384,1152]{1,0:T(8,128)(2,1)S(1)}, u32[]{:S(2)}) copy-start(bf16[384,1152]{1,0:T(8,128)(2,1)S(1)} %collective-permute-done.22.refs_4_) | copy-start | bytes 2654212
  56.2 14.3 %collective-permute-start.20 = (bf16[384,1152]{1,0:T(8,128)(2,1)S(1)}, bf16[384,1152]{1,0:T(8,128)(2,1)S(1)}, u32[]{:S(2)}, u32[]{:S(2)}) collective-permute-start(bf16[384,1152]{1,0:T(8,128)(2,1)S(1)} %slice_dynamic-update-slice_fusion.1.refs_2_), channel_id=1, source_target_pairs={{0,96},{1,33},{2,98},{3,35},{4,100},{5,37},{6,102},{7,39},{8,104},... | collective-permute-start | bytes 2654216 | tf_op jit(solution)/shard_map/ppermute | solution.py:45
  57.1 21.8 %collective-permute-start.23 = (bf16[384,1152]{1,0:T(8,128)(2,1)S(1)}, bf16[384,1152]{1,0:T(8,128)(2,1)S(1)}, u32[]{:S(2)}, u32[]{:S(2)}) collective-permute-start(bf16[384,1152]{1,0:T(8,128)(2,1)S(1)} %slice_dynamic-update-slice_fusion.refs_4_), channel_id=1, source_target_pairs={{0,24},{1,9},{2,26},{3,11},{4,28},{5,13},{6,30},{7,15},{8,16},{9,1... | collective-permute-start | bytes 2654216 | tf_op jit(solution)/shard_map/ppermute | solution.py:45
  59.5 0.9 copy-start.13
  60.5 0.9 copy-start.14
  61.4 18.0 %collective-permute-start.25 = (bf16[384,1152]{1,0:T(8,128)(2,1)}, bf16[384,1152]{1,0:T(8,128)(2,1)S(1)}, u32[]{:S(2)}, u32[]{:S(2)}) collective-permute-start(bf16[384,1152]{1,0:T(8,128)(2,1)} %collective-permute-done.16.refs_0_), channel_id=1, source_target_pairs={{0,1},{1,0},{2,3},{3,2},{4,5},{5,4},{6,7},{7,6},{8,9},{9,8},{10,11... | collective-permute-start | bytes 2654216 | tf_op jit(solution)/shard_map/ppermute | solution.py:49
  61.4 18.3 %collective-permute-start.26 = (bf16[384,1152]{1,0:T(8,128)(2,1)}, bf16[384,1152]{1,0:T(8,128)(2,1)S(1)}, u32[]{:S(2)}, u32[]{:S(2)}) collective-permute-start(bf16[384,1152]{1,0:T(8,128)(2,1)} %collective-permute-done.19.refs_2_), channel_id=1, source_target_pairs={{0,1},{1,0},{2,3},{3,2},{4,5},{5,4},{6,7},{7,6},{8,9},{9,8},{10,11... | collective-permute-start | bytes 2654216 | tf_op jit(solution)/shard_map/ppermute | solution.py:49
  67.8 11.2 %copy-start.4 = (bf16[384,1152]{1,0:T(8,128)(2,1)}, bf16[384,1152]{1,0:T(8,128)(2,1)S(1)}, u32[]{:S(2)}) copy-start(bf16[384,1152]{1,0:T(8,128)(2,1)S(1)} %collective-permute-done.17.refs_6_) | copy-start | bytes 2654212
  67.8 12.5 %collective-permute-start.27 = (bf16[384,1152]{1,0:T(8,128)(2,1)S(1)}, bf16[384,1152]{1,0:T(8,128)(2,1)S(1)}, u32[]{:S(2)}, u32[]{:S(2)}) collective-permute-start(bf16[384,1152]{1,0:T(8,128)(2,1)S(1)} %collective-permute-done.22.refs_4_), channel_id=1, source_target_pairs={{0,1},{1,0},{2,3},{3,2},{4,5},{5,4},{6,7},{7,6},{8,9},{9,8},{10,11... | collective-permute-start | bytes 2654216 | tf_op jit(solution)/shard_map/ppermute | solution.py:49
  70.6 8.4 %copy-start.5 = (bf16[384,1152]{1,0:T(8,128)(2,1)}, bf16[384,1152]{1,0:T(8,128)(2,1)S(1)}, u32[]{:S(2)}) copy-start(bf16[384,1152]{1,0:T(8,128)(2,1)S(1)} %collective-permute-done.20.refs_8_) | copy-start | bytes 2654212
  70.6 11.8 %collective-permute-start.18 = (bf16[384,1152]{1,0:T(8,128)(2,1)S(1)}, bf16[384,1152]{1,0:T(8,128)(2,1)S(1)}, u32[]{:S(2)}, u32[]{:S(2)}) collective-permute-start(bf16[384,1152]{1,0:T(8,128)(2,1)S(1)} %collective-permute-done.17.refs_6_), channel_id=1, source_target_pairs={{0,1},{1,0},{2,3},{3,2},{4,5},{5,4},{6,7},{7,6},{8,9},{9,8},{10,11... | collective-permute-start | bytes 2654216 | tf_op jit(solution)/shard_map/ppermute | solution.py:49
  78.9 6.3 %copy-start.6 = (bf16[384,1152]{1,0:T(8,128)(2,1)}, bf16[384,1152]{1,0:T(8,128)(2,1)S(1)}, u32[]{:S(2)}) copy-start(bf16[384,1152]{1,0:T(8,128)(2,1)S(1)} %collective-permute-done.23.refs_10_) | copy-start | bytes 2654212
  79.0 5.3 %collective-permute-start.21 = (bf16[384,1152]{1,0:T(8,128)(2,1)S(1)}, bf16[384,1152]{1,0:T(8,128)(2,1)S(1)}, u32[]{:S(2)}, u32[]{:S(2)}) collective-permute-start(bf16[384,1152]{1,0:T(8,128)(2,1)S(1)} %collective-permute-done.20.refs_8_), channel_id=1, source_target_pairs={{0,1},{1,0},{2,3},{3,2},{4,5},{5,4},{6,7},{7,6},{8,9},{9,8},{10,11... | collective-permute-start | bytes 2654216 | tf_op jit(solution)/shard_map/ppermute | solution.py:49
  79.4 5.8 %copy-start.7 = (bf16[384,1152]{1,0:T(8,128)(2,1)}, bf16[384,1152]{1,0:T(8,128)(2,1)S(1)}, u32[]{:S(2)}) copy-start(bf16[384,1152]{1,0:T(8,128)(2,1)S(1)} %collective-permute-done.25.refs_7_) | copy-start | bytes 2654212
  79.4 4.9 %collective-permute-start.24 = (bf16[384,1152]{1,0:T(8,128)(2,1)S(1)}, bf16[384,1152]{1,0:T(8,128)(2,1)S(1)}, u32[]{:S(2)}, u32[]{:S(2)}) collective-permute-start(bf16[384,1152]{1,0:T(8,128)(2,1)S(1)} %collective-permute-done.23.refs_10_), channel_id=1, source_target_pairs={{0,1},{1,0},{2,3},{3,2},{4,5},{5,4},{6,7},{7,6},{8,9},{9,8},{10,11... | collective-permute-start | bytes 2654216 | tf_op jit(solution)/shard_map/ppermute | solution.py:49
  79.7 5.5 %copy-start.8 = (bf16[384,1152]{1,0:T(8,128)(2,1)}, bf16[384,1152]{1,0:T(8,128)(2,1)S(1)}, u32[]{:S(2)}) copy-start(bf16[384,1152]{1,0:T(8,128)(2,1)S(1)} %collective-permute-done.26.refs_9_) | copy-start | bytes 2654212
  79.7 16.2 %collective-permute-start.28 = (bf16[384,1152]{1,0:T(8,128)(2,1)}, bf16[384,1152]{1,0:T(8,128)(2,1)}, u32[]{:S(2)}, u32[]{:S(2)}) collective-permute-start(bf16[384,1152]{1,0:T(8,128)(2,1)} %collective-permute-done.16.refs_0_), channel_id=1, source_target_pairs={{0,6},{1,3},{2,4},{3,1},{4,2},{5,7},{6,0},{7,5},{8,14},{9,11},{10,... | collective-permute-start | bytes 2654216 | tf_op jit(solution)/shard_map/ppermute | solution.py:45
  80.2 5.0 %copy-start.9 = (bf16[384,1152]{1,0:T(8,128)(2,1)}, bf16[384,1152]{1,0:T(8,128)(2,1)S(1)}, u32[]{:S(2)}) copy-start(bf16[384,1152]{1,0:T(8,128)(2,1)S(1)} %collective-permute-done.27.refs_11_) | copy-start | bytes 2654212
  80.2 15.8 %collective-permute-start.30 = (bf16[384,1152]{1,0:T(8,128)(2,1)}, bf16[384,1152]{1,0:T(8,128)(2,1)}, u32[]{:S(2)}, u32[]{:S(2)}) collective-permute-start(bf16[384,1152]{1,0:T(8,128)(2,1)} %collective-permute-done.19.refs_2_), channel_id=1, source_target_pairs={{0,96},{1,33},{2,98},{3,35},{4,100},{5,37},{6,102},{7,39},{8,104},... | collective-permute-start | bytes 2654216 | tf_op jit(solution)/shard_map/ppermute | solution.py:45
  82.4 2.8 %copy-start.10 = (bf16[384,1152]{1,0:T(8,128)(2,1)}, bf16[384,1152]{1,0:T(8,128)(2,1)S(1)}, u32[]{:S(2)}) copy-start(bf16[384,1152]{1,0:T(8,128)(2,1)S(1)} %collective-permute-done.18.refs_1_) | copy-start | bytes 2654212
  82.4 14.4 %collective-permute-start.32 = (bf16[384,1152]{1,0:T(8,128)(2,1)S(1)}, bf16[384,1152]{1,0:T(8,128)(2,1)}, u32[]{:S(2)}, u32[]{:S(2)}) collective-permute-start(bf16[384,1152]{1,0:T(8,128)(2,1)S(1)} %collective-permute-done.22.refs_4_), channel_id=1, source_target_pairs={{0,24},{1,9},{2,26},{3,11},{4,28},{5,13},{6,30},{7,15},{8,16},{9,1... | collective-permute-start | bytes 2654216 | tf_op jit(solution)/shard_map/ppermute | solution.py:45
  84.3 1.3 copy-start.11
  84.3 0.9 copy-start.12
  95.9 2.7 %collective-permute-start.29 = (bf16[384,1152]{1,0:T(8,128)(2,1)}, bf16[384,1152]{1,0:T(8,128)(2,1)S(1)}, u32[]{:S(2)}, u32[]{:S(2)}) collective-permute-start(bf16[384,1152]{1,0:T(8,128)(2,1)} %collective-permute-done.28.refs_0_), channel_id=1, source_target_pairs={{0,1},{1,0},{2,3},{3,2},{4,5},{5,4},{6,7},{7,6},{8,9},{9,8},{10,11... | collective-permute-start | bytes 2654216 | tf_op jit(solution)/shard_map/ppermute | solution.py:49
  96.0 3.9 %collective-permute-start.31 = (bf16[384,1152]{1,0:T(8,128)(2,1)}, bf16[384,1152]{1,0:T(8,128)(2,1)S(1)}, u32[]{:S(2)}, u32[]{:S(2)}) collective-permute-start(bf16[384,1152]{1,0:T(8,128)(2,1)} %collective-permute-done.30.refs_2_), channel_id=1, source_target_pairs={{0,1},{1,0},{2,3},{3,2},{4,5},{5,4},{6,7},{7,6},{8,9},{9,8},{10,11... | collective-permute-start | bytes 2654216 | tf_op jit(solution)/shard_map/ppermute | solution.py:49
  96.8 4.3 %collective-permute-start.33 = (bf16[384,1152]{1,0:T(8,128)(2,1)}, bf16[384,1152]{1,0:T(8,128)(2,1)S(1)}, u32[]{:S(2)}, u32[]{:S(2)}) collective-permute-start(bf16[384,1152]{1,0:T(8,128)(2,1)} %collective-permute-done.32.refs_4_), channel_id=1, source_target_pairs={{0,1},{1,0},{2,3},{3,2},{4,5},{5,4},{6,7},{7,6},{8,9},{9,8},{10,11... | collective-permute-start | bytes 2654216 | tf_op jit(solution)/shard_map/ppermute | solution.py:49
  98.7 2.5 %copy-start.15 = (bf16[384,1152]{1,0:T(8,128)(2,1)}, bf16[384,1152]{1,0:T(8,128)(2,1)S(1)}, u32[]{:S(2)}) copy-start(bf16[384,1152]{1,0:T(8,128)(2,1)S(1)} %collective-permute-done.29.refs_1_) | copy-start | bytes 2654212
  99.9 1.3 copy-start.16
  101.2 0.9 copy-start.17

commit v3 on v2

--- a/solution.py
+++ b/solution.py
@@ -196,12 +196,21 @@
     )(core, state, mod, *weights)
 
 
-def next_kernel(count, core_ref, hidden_ref, acc_in, *refs):
+def fetch(pairs, sems):
+    copies = [pltpu.make_async_copy(array, buf, sems.at[index]) for index, (array, buf) in enumerate(pairs)]
+    for copy in copies:
+        copy.start()
+    return copies
+
+
+def next_kernel(count, core_ref, hidden_in, acc_in, *refs):
     sets = as_sets(refs[:count])
     acc_ref, *weights = refs[count:]
-    kept, weights = weights[:4], weights[4:]
+    kept, (hidden_ref, given_ref, own_sems), weights = weights[:4], weights[4:7], weights[7:]
     start_set(core_ref, sets[0], *weights[:3], 0)
-    mlp_sets(core_ref, sets, kept, hidden_ref, acc_ref, acc_in, *weights)
+    for copy in fetch([(hidden_in, hidden_ref), (acc_in, given_ref)], own_sems):
+        copy.wait()
+    mlp_sets(core_ref, sets, kept, hidden_ref, acc_ref, given_ref, *weights)
 
 
 def next_piece(core, hidden, acc, sets):
@@ -211,28 +220,32 @@
     return pl.pallas_call(
         functools.partial(next_kernel, len(weights)),
         out_shape=[jax.ShapeDtypeStruct((tokens, width), f32)] + kept_shapes(units, width, 2),
-        in_specs=[SMEM, VMEM, VMEM] + [ANY] * len(weights),
+        in_specs=[SMEM, ANY, ANY] + [ANY] * len(weights),
         out_specs=[VMEM] + [HBM] * 4,
-        scratch_shapes=weight_scratch(units, width, 2),
+        scratch_shapes=[
+            pltpu.VMEM((tokens, width), bf16),
+            pltpu.VMEM((tokens, width), f32),
+            pltpu.SemaphoreType.DMA((2,)),
+        ]
+        + weight_scratch(units, width, 2),
         compiler_params=room(56),
         name="next_piece",
     )(core, hidden, acc, *weights)
 
 
 def far_kernel(
-    count, core_ref, first_ref, begin_ref, dt_ref, sigma_ref, hidden_ref, acc_in, state_ref, noise_ref, mod_ref, *refs
+    count, core_ref, first_ref, begin_ref, dt_ref, sigma_ref, hidden_in, acc_in, state_ref, noise_ref, mod_ref, *refs
 ):
     sets = as_sets(refs[:count])
-    out_ref, up_kept, down_kept, acc_ref, state_buf, noise_buf, own_sems, *weights = refs[count:]
+    out_ref, up_kept, down_kept, hidden_ref, given_ref, acc_ref, state_buf, noise_buf, own_sems, *weights = refs[count:]
     start_set(core_ref, sets[0], *weights[:3], 0)
-    own = [
-        pltpu.make_async_copy(state_ref, state_buf, own_sems.at[0]),
-        pltpu.make_async_copy(noise_ref, noise_buf, own_sems.at[1]),
-    ]
-    for copy in own:
-        copy.start()
-    mlp_sets(core_ref, sets, [up_kept, down_kept], hidden_ref, acc_ref, acc_in, *weights)
-    for copy in own:
+    own = fetch(
+        [(hidden_in, hidden_ref), (acc_in, given_ref), (state_ref, state_buf), (noise_ref, noise_buf)], own_sems
+    )
+    for copy in own[:2]:
+        copy.wait()
+    mlp_sets(core_ref, sets, [up_kept, down_kept], hidden_ref, acc_ref, given_ref, *weights)
+    for copy in own[2:]:
         copy.wait()
     peers, rows, width = out_ref.shape
     rows = rows // 2
@@ -258,13 +271,15 @@
         functools.partial(far_kernel, len(weights)),
         out_shape=[jax.ShapeDtypeStruct((peers, 2 * (tokens // peers), width), bf16)]
         + kept_shapes(units, width, 1),
-        in_specs=[SMEM] * 5 + [VMEM] * 2 + [ANY] * 2 + [VMEM] + [ANY] * len(weights),
+        in_specs=[SMEM] * 5 + [ANY] * 4 + [VMEM] + [ANY] * len(weights),
         out_specs=[VMEM, HBM, HBM],
         scratch_shapes=[
+            pltpu.VMEM((tokens, width), bf16),
+            pltpu.VMEM((tokens, width), f32),
             pltpu.VMEM((tokens, width), f32),
             pltpu.VMEM(state.shape, f32),
             pltpu.VMEM(noise.shape, bf16),
-            pltpu.SemaphoreType.DMA((2,)),
+            pltpu.SemaphoreType.DMA((4,)),
         ]
         + weight_scratch(units, width, 1),
         compiler_params=room(56),
@@ -385,9 +400,9 @@
     ready = [after(part, near, modulation) for part, near in zip(parts, first)]
     second = [send(part, axis, False) for part, axis in zip(ready, last)]
     own_swapped = [swap_cores(after(part, modulation)) for part in parts]
-    first_swapped = [swap_cores(after(part, *own_swapped)) for part in first]
     set_own = list(zip(parts, own_swapped))
     hidden, acc, *kept = own_piece(core_arg, state, modulation, [set_own])
+    first_swapped = [swap_cores(after(part, acc)) for part in first]
     far = [send(after(near, other, acc), axis, False) for near, other, axis in zip(first, second, last)]
     second_swapped = [swap_cores(part) for part in second]
     set_low = list(zip(first, second_swapped))

time: 166 us -> 160 us (0.964)
  waiting for transfers between devices: 28.3 us -> 23.8 us
    ppermute x21, waiting for transfers between devices: 24 us -> 18.1 us  [send(): return lax.ppermute(rows, ALL, neighbour(axis, first))]
    unnamed x49 -> x51, local copies, waits for them, and re-layouts: 5.44 us -> 4.74 us
  transfers between devices with their start and end apart: 34 -> 34, of which waited for: 13 -> 15; matrix products, arithmetic and copies ran while one was open for 7% -> 7% of each run, Pallas kernels for 11% -> 12%
where the time goes in v3:
time: 160 us
  Pallas kernels  41 us (26%)
  blocking collectives  39.9 us (25%)
  starting transfers between devices  34.2 us (21%)
  waiting for transfers between devices  23.8 us (15%)
  other arithmetic  7.63 us (5%)
  local copies, waits for them, and re-layouts  6.28 us (4%)
  matrix products  5.2 us (3%)
    ppermute x21, starting transfers between devices, send(): return lax.ppermute(rows, ALL, neighbour(axis, first))  32 us
    all_to_all x1, blocking collectives, per_device(): got = lax.all_to_all(sent, 'tm', 0, 0, tiled=True)  24.6 us
    ppermute x21, waiting for transfers between devices, send(): return lax.ppermute(rows, ALL, neighbour(axis, first))  18.1 us
    all_to_all x1, blocking collectives, per_device(): final = lax.all_to_all(updated, 'tm', 0, 0, tiled=True)  15.3 us
    pallas_call x1, Pallas kernels, second_sweep(): pl.pallas_call(functools.partial(second_kernel, len(weights)), out_shape=...  14 us
    pallas_call x1, Pallas kernels, next_piece(): pl.pallas_call(functools.partial(next_kernel, len(weights)), out_shape=[j...  11 us
    pallas_call x1, Pallas kernels, own_piece(): pl.pallas_call(functools.partial(own_kernel, len(weights)), out_shape=[ja...  8 us
    pallas_call x1, Pallas kernels, far_piece(): pl.pallas_call(functools.partial(far_kernel, len(weights)), out_shape=[ja...  7.99 us
  transfers between devices with their start and end apart: 34, of which 15 were waited for; matrix products, arithmetic and copies ran while one was open for 7% of the time, Pallas kernels for 12%

profile of v3, /device:TPU:0, one launch (start us, length us, event | category | flops | bytes accessed | tf_op | source)
XLA Modules:
  0.0 159.7 jit_solution(12584317967722121595)
XLA Ops:
  0.0 0.9 broadcast_select_fusion
  2.3 1.0 maximum_select_fusion
  3.3 0.7 fusion.5
  4.0 1.6 collective-permute-start.1
  5.6 1.6 collective-permute-start.9
  7.2 1.9 %collective-permute-start.5 = (bf16[24,1152]{1,0:T(8,128)(2,1)S(1)}, bf16[24,1152]{1,0:T(8,128)(2,1)S(1)}, u32[]{:S(2)}, u32[]{:S(2)}) collective-permute-start(bf16[24,1152]{1,0:T(8,128)(2,1)S(1)} %get-tuple-element.84), channel_id=1, source_target_pairs={{0,8},{1,25},{2,10},{3,27},{4,12},{5,29},{6,14},{7,31},{8,0},{9,17... | collective-permute-start | bytes 165896 | tf_op jit(solution)/shard_map/ppermute | solution.py:45
  9.1 2.2 %collective-permute-start.2 = (bf16[48,1152]{1,0:T(8,128)(2,1)S(1)}, bf16[48,1152]{1,0:T(8,128)(2,1)S(1)}, u32[]{:S(2)}, u32[]{:S(2)}) collective-permute-start(bf16[48,1152]{1,0:T(8,128)(2,1)S(1)} %pad_maximum_fusion.3), channel_id=1, source_target_pairs={{0,96},{1,33},{2,98},{3,35},{4,100},{5,37},{6,102},{7,39},{8,104},... | collective-permute-start | bytes 331784 | tf_op jit(solution)/shard_map/ppermute | solution.py:45
  11.3 2.9 %collective-permute-start.10 = (bf16[48,1152]{1,0:T(8,128)(2,1)S(1)}, bf16[48,1152]{1,0:T(8,128)(2,1)S(1)}, u32[]{:S(2)}, u32[]{:S(2)}) collective-permute-start(bf16[48,1152]{1,0:T(8,128)(2,1)S(1)} %pad_maximum_fusion.5), channel_id=1, source_target_pairs={{0,6},{1,3},{2,4},{3,1},{4,2},{5,7},{6,0},{7,5},{8,14},{9,11},{10,... | collective-permute-start | bytes 331784 | tf_op jit(solution)/shard_map/ppermute | solution.py:45
  14.2 4.1 %collective-permute-start.6 = (bf16[48,1152]{1,0:T(8,128)(2,1)S(1)}, bf16[48,1152]{1,0:T(8,128)(2,1)S(1)}, u32[]{:S(2)}, u32[]{:S(2)}) collective-permute-start(bf16[48,1152]{1,0:T(8,128)(2,1)S(1)} %pad_maximum_fusion.4), channel_id=1, source_target_pairs={{0,24},{1,9},{2,26},{3,11},{4,28},{5,13},{6,30},{7,15},{8,16},{9,1... | collective-permute-start | bytes 331784 | tf_op jit(solution)/shard_map/ppermute | solution.py:45
  18.4 0.6 constant_dynamic-update-slice_fusion.3
  19.0 0.6 constant_dynamic-update-slice_fusion.2
  19.7 0.6 constant_dynamic-update-slice_fusion.1
  20.4 0.6 constant_dynamic-update-slice_fusion.21
  21.1 0.6 constant_dynamic-update-slice_fusion.20
  21.7 0.6 constant_dynamic-update-slice_fusion.19
  22.4 0.3 collective-permute-start.11
  22.8 0.2 collective-permute-start.7
  23.1 3.3 %collective-permute-done.3 = bf16[96,1152]{1,0:T(8,128)(2,1)S(1)} collective-permute-done((bf16[96,1152]{1,0:T(8,128)(2,1)S(1)}, bf16[96,1152]{1,0:T(8,128)(2,1)S(1)}, u32[]{:S(2)}, u32[]{:S(2)}) %collective-permute-start.3) | collective-permute-done | bytes 221216 | tf_op jit(solution)/shard_map/ppermute | solution.py:45
  26.5 1.9 %collective-permute-done.11 = bf16[96,1152]{1,0:T(8,128)(2,1)S(1)} collective-permute-done((bf16[96,1152]{1,0:T(8,128)(2,1)S(1)}, bf16[96,1152]{1,0:T(8,128)(2,1)S(1)}, u32[]{:S(2)}, u32[]{:S(2)}) %collective-permute-start.11) | collective-permute-done | bytes 221216 | tf_op jit(solution)/shard_map/ppermute | solution.py:45
  28.4 0.7 constant_dynamic-update-slice_fusion.18
  29.1 0.8 collective-permute-start.12
  29.9 3.1 %collective-permute-start.8 = (bf16[192,1152]{1,0:T(8,128)(2,1)S(1)}, bf16[192,1152]{1,0:T(8,128)(2,1)S(1)}, u32[]{:S(2)}, u32[]{:S(2)}) collective-permute-start(bf16[192,1152]{1,0:T(8,128)(2,1)S(1)} %constant_dynamic-update-slice_fusion.9), channel_id=1, source_target_pairs={{0,6},{1,3},{2,4},{3,1},{4,2},{5,7},{6,0},{7,5},{8,14},{9,11},{10,... | collective-permute-start | bytes 1327112 | tf_op jit(solution)/shard_map/ppermute | solution.py:45
  33.0 2.9 %collective-permute-done.4 = bf16[192,1152]{1,0:T(8,128)(2,1)S(1)} collective-permute-done((bf16[192,1152]{1,0:T(8,128)(2,1)S(1)}, bf16[192,1152]{1,0:T(8,128)(2,1)S(1)}, u32[]{:S(2)}, u32[]{:S(2)}) %collective-permute-start.4) | collective-permute-done | bytes 442400 | tf_op jit(solution)/shard_map/ppermute | solution.py:45
  36.1 2.7 %collective-permute-done.12 = bf16[192,1152]{1,0:T(8,128)(2,1)S(1)} collective-permute-done((bf16[192,1152]{1,0:T(8,128)(2,1)}, bf16[192,1152]{1,0:T(8,128)(2,1)S(1)}, u32[]{:S(2)}, u32[]{:S(2)}) %collective-permute-start.12) | collective-permute-done | bytes 442400 | tf_op jit(solution)/shard_map/ppermute | solution.py:45
  38.9 0.7 collective-permute-done.8
  39.5 0.1 select_dynamic-update-slice_fusion.1
  39.9 0.4 collective-permute-start.16
  40.3 0.5 collective-permute-start.19
  40.8 2.0 %collective-permute-start.22 = (bf16[384,1152]{1,0:T(8,128)(2,1)S(1)}, bf16[384,1152]{1,0:T(8,128)(2,1)S(1)}, u32[]{:S(2)}, u32[]{:S(2)}) collective-permute-start(bf16[384,1152]{1,0:T(8,128)(2,1)S(1)} %slice_dynamic-update-slice_fusion.refs_4_), channel_id=1, source_target_pairs={{0,8},{1,25},{2,10},{3,27},{4,12},{5,29},{6,14},{7,31},{8,0},{9,17... | collective-permute-start | bytes 2654216 | tf_op jit(solution)/shard_map/ppermute | solution.py:45
  42.8 0.5 pad_convert_fusion
  43.4 1.0 multiply_cosine_fusion
  44.3 5.2 %fusion.mod_ref = f32[24,3456]{1,0:T(8,128)} fusion(bf16[1152,3456]{1,0:T(8,128)(2,1)} %param.17, f32[24,576]{1,0:T(8,128)S(1)} %get-tuple-element.96, f32[24,576]{1,0:T(8,128)S(1)} %get-tuple-element.95, f32[1152]{0:T(1024)S(1)} %reduce), kind=kOutput, calls=%fused_computation.48 | convolution fusion | flops 191296512 | bytes 8409600 | tf_op jit(solution)/shard_map/dot_general | solution.py:394
  49.5 0.5 collective-permute-start.14
  50.0 3.1 %collective-permute-done.16.refs_0_ = bf16[384,1152]{1,0:T(8,128)(2,1)} collective-permute-done((bf16[384,1152]{1,0:T(8,128)(2,1)S(1)}, bf16[384,1152]{1,0:T(8,128)(2,1)}, u32[]{:S(2)}, u32[]{:S(2)}) %collective-permute-start.16) | collective-permute-done | bytes 884768 | tf_op jit(solution)/shard_map/ppermute | solution.py:45
  53.1 0.4 collective-permute-done.19.refs_2_
  53.5 2.7 %collective-permute-start.17 = (bf16[384,1152]{1,0:T(8,128)(2,1)S(1)}, bf16[384,1152]{1,0:T(8,128)(2,1)S(1)}, u32[]{:S(2)}, u32[]{:S(2)}) collective-permute-start(bf16[384,1152]{1,0:T(8,128)(2,1)S(1)} %slice_dynamic-update-slice_fusion.2.refs_0_), channel_id=1, source_target_pairs={{0,6},{1,3},{2,4},{3,1},{4,2},{5,7},{6,0},{7,5},{8,14},{9,11},{10,... | collective-permute-start | bytes 2654216 | tf_op jit(solution)/shard_map/ppermute | solution.py:45
  56.2 0.8 collective-permute-start.20
  57.1 2.5 %collective-permute-start.23 = (bf16[384,1152]{1,0:T(8,128)(2,1)S(1)}, bf16[384,1152]{1,0:T(8,128)(2,1)S(1)}, u32[]{:S(2)}, u32[]{:S(2)}) collective-permute-start(bf16[384,1152]{1,0:T(8,128)(2,1)S(1)} %slice_dynamic-update-slice_fusion.refs_4_), channel_id=1, source_target_pairs={{0,24},{1,9},{2,26},{3,11},{4,28},{5,13},{6,30},{7,15},{8,16},{9,1... | collective-permute-start | bytes 2654216 | tf_op jit(solution)/shard_map/ppermute | solution.py:45
  59.7 0.9 copy-done.15
  60.6 0.3 copy-done.14
  60.9 8.0 %own_piece.1 = (bf16[256,1152]{1,0:T(8,128)(2,1)}, f32[256,1152]{1,0:T(8,128)}, bf16[1152,1152]{1,0:T(8,128)(2,1)}, bf16[1152,1152]{1,0:T(8,128)(2,1)}) custom-call(s32[1]{0:T(128)} %bitcast.core_ref, f32[256,1152]{1,0:T(8,128)} %bitcast.13, f32[24,3456]{1,0:T(8,128)} %fusion.mod_ref, bf16[384,1152]{1,0:T(8,128)(2,1)} %copy-done.2, ...), custom_call_target="tpu_custom_call" | custom-call | tf_op jit(solution)/shard_map/own_piece/pallas_call | solution.py:187
  69.0 0.5 collective-permute-start.26
  69.5 1.0 collective-permute-done.20.refs_8_
  70.6 0.8 collective-permute-done.23.refs_10_
  71.4 0.2 collective-permute-done.25.refs_7_
  71.6 0.4 collective-permute-start.24
  71.9 2.2 %collective-permute-done.26.refs_9_ = bf16[384,1152]{1,0:T(8,128)(2,1)S(1)} collective-permute-done((bf16[384,1152]{1,0:T(8,128)(2,1)}, bf16[384,1152]{1,0:T(8,128)(2,1)S(1)}, u32[]{:S(2)}, u32[]{:S(2)}) %collective-permute-start.26) | collective-permute-done | bytes 884768 | tf_op jit(solution)/shard_map/ppermute | solution.py:49
  74.1 1.2 collective-permute-start.28
  75.3 2.5 %collective-permute-start.30 = (bf16[384,1152]{1,0:T(8,128)(2,1)}, bf16[384,1152]{1,0:T(8,128)(2,1)}, u32[]{:S(2)}, u32[]{:S(2)}) collective-permute-start(bf16[384,1152]{1,0:T(8,128)(2,1)} %collective-permute-done.19.refs_2_), channel_id=1, source_target_pairs={{0,96},{1,33},{2,98},{3,35},{4,100},{5,37},{6,102},{7,39},{8,104},... | collective-permute-start | bytes 2654216 | tf_op jit(solution)/shard_map/ppermute | solution.py:45
  77.9 0.4 collective-permute-start.32
  78.3 0.9 copy-done.12
  79.2 0.3 copy-done.11
  79.5 11.0 %next_piece.1 = (f32[256,1152]{1,0:T(8,128)}, bf16[1152,1152]{1,0:T(8,128)(2,1)}, bf16[1152,1152]{1,0:T(8,128)(2,1)}, bf16[1152,1152]{1,0:T(8,128)(2,1)}, bf16[1152,1152]{1,0:T(8,128)(2,1)}) custom-call(s32[1]{0:T(128)} %bitcast.core_ref, bf16[256,1152]{1,0:T(8,128)(2,1)} %get-tuple-element.41.hidden_in, f32[256,1152]{1,0:T(8,128)} %get-tuple-element.42.acc_in, ...), custom_call_target="tpu_custom_call" | custom-call | tf_op jit(solution)/shard_map/next_piece/pallas_call | solution.py:220
  90.6 0.5 collective-permute-start.31
  91.1 1.2 collective-permute-done.32.refs_4_
  92.3 0.9 collective-permute-done.29.refs_1_
  93.2 1.3 collective-permute-done.31.refs_3_
  94.5 1.3 collective-permute-done.33.refs_5_
  95.8 0.9 copy-done.18
  96.7 8.0 %far_piece.1 = (bf16[16,32,1152]{2,1,0:T(8,128)(2,1)}, bf16[1152,1152]{1,0:T(8,128)(2,1)}, bf16[1152,1152]{1,0:T(8,128)(2,1)}) custom-call(s32[1]{0:T(128)} %bitcast.core_ref, f32[1]{0:T(128)} %bitcast.1.first_ref, s32[1]{0:T(128)} %bitcast.3.begin_ref, f32[1000]{0:T(1024)} %dt_ref.3, f32[1000]{0:T(1024)} %sigma_ref.3, ...), custom_call_target="tpu_custom_call" | custom-call | tf_op jit(solution)/shard_map/far_piece/pallas_call | solution.py:270
  104.7 24.6 %all_to_all.10.got_ref = bf16[16,32,1152]{2,1,0:T(8,128)(2,1)} all-to-all(bf16[16,32,1152]{2,1,0:T(8,128)(2,1)} %get-tuple-element.56), channel_id=1, replica_groups=mesh['tm'=16,'batch'=8] {'tm'}, dimensions={0} | all-to-all | bytes 2359296 | tf_op jit(solution)/shard_map/all_to_all | solution.py:418
  129.2 14.0 %second_sweep.1 = bf16[16,16,1152]{2,1,0:T(8,128)(2,1)} custom-call(s32[1]{0:T(128)} %copy.41.begin_ref, s32[1]{0:T(128)} %copy.42.advance_ref, f32[1000]{0:T(1024)} %dt_ref.3, f32[1000]{0:T(1024)} %sigma_ref.3, bf16[16,32,1152]{2,1,0:T(8,128)(2,1)} %all_to_all.10.got_ref, f32[24,3456]{1,0:T(8,128)} %fusion.mod_ref, ...), custom_call_target="tpu_custom_call" | custom-call | tf_op jit(solution)/shard_map/second_sweep/pallas_call | solution.py:344
  143.3 15.3 %all_to_all.11 = bf16[16,16,1152]{2,1,0:T(8,128)(2,1)S(1)} all-to-all(bf16[16,16,1152]{2,1,0:T(8,128)(2,1)} %second_sweep.1), channel_id=1, replica_groups=mesh['tm'=16,'batch'=8] {'tm'}, dimensions={0} | all-to-all | bytes 1179648 | tf_op jit(solution)/shard_map/all_to_all | solution.py:428
  158.6 1.1 convert.2
  (94 shorter events, 1.3 us)
Async XLA Ops:
  0.9 1.4 collective-permute-start
  4.0 5.1 %collective-permute-start.1 = (bf16[24,1152]{1,0:T(8,128)(2,1)S(1)}, bf16[24,1152]{1,0:T(8,128)(2,1)S(1)}, u32[]{:S(2)}, u32[]{:S(2)}) collective-permute-start(bf16[24,1152]{1,0:T(8,128)(2,1)S(1)} %get-tuple-element.85), channel_id=1, source_target_pairs={{0,32},{1,97},{2,34},{3,99},{4,36},{5,101},{6,38},{7,103},{8,40},{... | collective-permute-start | bytes 165896 | tf_op jit(solution)/shard_map/ppermute | solution.py:45
  5.6 5.7 %collective-permute-start.9 = (bf16[24,1152]{1,0:T(8,128)(2,1)S(1)}, bf16[24,1152]{1,0:T(8,128)(2,1)S(1)}, u32[]{:S(2)}, u32[]{:S(2)}) collective-permute-start(bf16[24,1152]{1,0:T(8,128)(2,1)S(1)} %get-tuple-element.77), channel_id=1, source_target_pairs={{0,2},{1,7},{2,0},{3,5},{4,6},{5,3},{6,4},{7,1},{8,10},{9,15},{10,... | collective-permute-start | bytes 165896 | tf_op jit(solution)/shard_map/ppermute | solution.py:45
  7.2 7.0 %collective-permute-start.5 = (bf16[24,1152]{1,0:T(8,128)(2,1)S(1)}, bf16[24,1152]{1,0:T(8,128)(2,1)S(1)}, u32[]{:S(2)}, u32[]{:S(2)}) collective-permute-start(bf16[24,1152]{1,0:T(8,128)(2,1)S(1)} %get-tuple-element.84), channel_id=1, source_target_pairs={{0,8},{1,25},{2,10},{3,27},{4,12},{5,29},{6,14},{7,31},{8,0},{9,17... | collective-permute-start | bytes 165896 | tf_op jit(solution)/shard_map/ppermute | solution.py:45
  9.1 9.2 %collective-permute-start.2 = (bf16[48,1152]{1,0:T(8,128)(2,1)S(1)}, bf16[48,1152]{1,0:T(8,128)(2,1)S(1)}, u32[]{:S(2)}, u32[]{:S(2)}) collective-permute-start(bf16[48,1152]{1,0:T(8,128)(2,1)S(1)} %pad_maximum_fusion.3), channel_id=1, source_target_pairs={{0,96},{1,33},{2,98},{3,35},{4,100},{5,37},{6,102},{7,39},{8,104},... | collective-permute-start | bytes 331784 | tf_op jit(solution)/shard_map/ppermute | solution.py:45
  11.3 9.1 %collective-permute-start.10 = (bf16[48,1152]{1,0:T(8,128)(2,1)S(1)}, bf16[48,1152]{1,0:T(8,128)(2,1)S(1)}, u32[]{:S(2)}, u32[]{:S(2)}) collective-permute-start(bf16[48,1152]{1,0:T(8,128)(2,1)S(1)} %pad_maximum_fusion.5), channel_id=1, source_target_pairs={{0,6},{1,3},{2,4},{3,1},{4,2},{5,7},{6,0},{7,5},{8,14},{9,11},{10,... | collective-permute-start | bytes 331784 | tf_op jit(solution)/shard_map/ppermute | solution.py:45
  14.2 8.5 %collective-permute-start.6 = (bf16[48,1152]{1,0:T(8,128)(2,1)S(1)}, bf16[48,1152]{1,0:T(8,128)(2,1)S(1)}, u32[]{:S(2)}, u32[]{:S(2)}) collective-permute-start(bf16[48,1152]{1,0:T(8,128)(2,1)S(1)} %pad_maximum_fusion.4), channel_id=1, source_target_pairs={{0,24},{1,9},{2,26},{3,11},{4,28},{5,13},{6,30},{7,15},{8,16},{9,1... | collective-permute-start | bytes 331784 | tf_op jit(solution)/shard_map/ppermute | solution.py:45
  20.3 6.0 %copy-start.19 = (bf16[192,1152]{1,0:T(8,128)(2,1)S(1)}, bf16[192,1152]{1,0:T(8,128)(2,1)}, u32[]{:S(2)}) copy-start(bf16[192,1152]{1,0:T(8,128)(2,1)} %get-tuple-element.92) | copy-start | bytes 1327108
  20.3 6.0 %collective-permute-start.3 = (bf16[96,1152]{1,0:T(8,128)(2,1)S(1)}, bf16[96,1152]{1,0:T(8,128)(2,1)S(1)}, u32[]{:S(2)}, u32[]{:S(2)}) collective-permute-start(bf16[96,1152]{1,0:T(8,128)(2,1)S(1)} %pad_maximum_fusion), channel_id=1, source_target_pairs={{0,8},{1,25},{2,10},{3,27},{4,12},{5,29},{6,14},{7,31},{8,0},{9,17... | collective-permute-start | bytes 663560 | tf_op jit(solution)/shard_map/ppermute | solution.py:45
  22.4 6.0 %collective-permute-start.11 = (bf16[96,1152]{1,0:T(8,128)(2,1)S(1)}, bf16[96,1152]{1,0:T(8,128)(2,1)S(1)}, u32[]{:S(2)}, u32[]{:S(2)}) collective-permute-start(bf16[96,1152]{1,0:T(8,128)(2,1)S(1)} %pad_maximum_fusion.2), channel_id=1, source_target_pairs={{0,32},{1,97},{2,34},{3,99},{4,36},{5,101},{6,38},{7,103},{8,40},{... | collective-permute-start | bytes 663560 | tf_op jit(solution)/shard_map/ppermute | solution.py:45
  22.8 7.1 %collective-permute-start.7 = (bf16[96,1152]{1,0:T(8,128)(2,1)S(1)}, bf16[96,1152]{1,0:T(8,128)(2,1)S(1)}, u32[]{:S(2)}, u32[]{:S(2)}) collective-permute-start(bf16[96,1152]{1,0:T(8,128)(2,1)S(1)} %pad_maximum_fusion.1), channel_id=1, source_target_pairs={{0,2},{1,7},{2,0},{3,5},{4,6},{5,3},{6,4},{7,1},{8,10},{9,15},{10,... | collective-permute-start | bytes 663560 | tf_op jit(solution)/shard_map/ppermute | solution.py:45
  26.4 9.6 %collective-permute-start.4 = (bf16[192,1152]{1,0:T(8,128)(2,1)S(1)}, bf16[192,1152]{1,0:T(8,128)(2,1)S(1)}, u32[]{:S(2)}, u32[]{:S(2)}) collective-permute-start(bf16[192,1152]{1,0:T(8,128)(2,1)S(1)} %constant_dynamic-update-slice_fusion), channel_id=1, source_target_pairs={{0,24},{1,9},{2,26},{3,11},{4,28},{5,13},{6,30},{7,15},{8,16},{9,1... | collective-permute-start | bytes 1327112 | tf_op jit(solution)/shard_map/ppermute | solution.py:45
  29.1 9.7 %collective-permute-start.12 = (bf16[192,1152]{1,0:T(8,128)(2,1)}, bf16[192,1152]{1,0:T(8,128)(2,1)S(1)}, u32[]{:S(2)}, u32[]{:S(2)}) collective-permute-start(bf16[192,1152]{1,0:T(8,128)(2,1)} %constant_dynamic-update-slice_fusion.18), channel_id=1, source_target_pairs={{0,96},{1,33},{2,98},{3,35},{4,100},{5,37},{6,102},{7,39},{8,104},... | collective-permute-start | bytes 1327112 | tf_op jit(solution)/shard_map/ppermute | solution.py:45
  29.9 9.6 %collective-permute-start.8 = (bf16[192,1152]{1,0:T(8,128)(2,1)S(1)}, bf16[192,1152]{1,0:T(8,128)(2,1)S(1)}, u32[]{:S(2)}, u32[]{:S(2)}) collective-permute-start(bf16[192,1152]{1,0:T(8,128)(2,1)S(1)} %constant_dynamic-update-slice_fusion.9), channel_id=1, source_target_pairs={{0,6},{1,3},{2,4},{3,1},{4,2},{5,7},{6,0},{7,5},{8,14},{9,11},{10,... | collective-permute-start | bytes 1327112 | tf_op jit(solution)/shard_map/ppermute | solution.py:45
  36.0 7.4 %copy-start.20 = (f32[1,1152]{1,0:T(1,128)S(1)}, f32[1,1152]{1,0:T(1,128)}, u32[]{:S(2)}) copy-start(f32[1,1152]{1,0:T(1,128)} %param.12) | copy-start | bytes 13828
  36.1 17.4 %copy-start.2 = (bf16[384,1152]{1,0:T(8,128)(2,1)}, bf16[384,1152]{1,0:T(8,128)(2,1)S(1)}, u32[]{:S(2)}) copy-start(bf16[384,1152]{1,0:T(8,128)(2,1)S(1)} %slice_dynamic-update-slice_fusion.2.refs_0_) | copy-start | bytes 2654212
  39.8 16.5 %copy-start = (bf16[384,1152]{1,0:T(8,128)(2,1)}, bf16[384,1152]{1,0:T(8,128)(2,1)S(1)}, u32[]{:S(2)}) copy-start(bf16[384,1152]{1,0:T(8,128)(2,1)S(1)} %slice_dynamic-update-slice_fusion.1.refs_2_) | copy-start | bytes 2654212
  39.9 17.2 %copy-start.1 = (bf16[384,1152]{1,0:T(8,128)(2,1)}, bf16[384,1152]{1,0:T(8,128)(2,1)S(1)}, u32[]{:S(2)}) copy-start(bf16[384,1152]{1,0:T(8,128)(2,1)S(1)} %slice_dynamic-update-slice_fusion.refs_4_) | copy-start | bytes 2654212
  39.9 13.2 %collective-permute-start.16 = (bf16[384,1152]{1,0:T(8,128)(2,1)S(1)}, bf16[384,1152]{1,0:T(8,128)(2,1)}, u32[]{:S(2)}, u32[]{:S(2)}) collective-permute-start(bf16[384,1152]{1,0:T(8,128)(2,1)S(1)} %slice_dynamic-update-slice_fusion.2.refs_0_), channel_id=1, source_target_pairs={{0,2},{1,7},{2,0},{3,5},{4,6},{5,3},{6,4},{7,1},{8,10},{9,15},{10,... | collective-permute-start | bytes 2654216 | tf_op jit(solution)/shard_map/ppermute | solution.py:45
  40.3 13.1 %collective-permute-start.19 = (bf16[384,1152]{1,0:T(8,128)(2,1)S(1)}, bf16[384,1152]{1,0:T(8,128)(2,1)}, u32[]{:S(2)}, u32[]{:S(2)}) collective-permute-start(bf16[384,1152]{1,0:T(8,128)(2,1)S(1)} %slice_dynamic-update-slice_fusion.1.refs_2_), channel_id=1, source_target_pairs={{0,32},{1,97},{2,34},{3,99},{4,36},{5,101},{6,38},{7,103},{8,40},{... | collective-permute-start | bytes 2654216 | tf_op jit(solution)/shard_map/ppermute | solution.py:45
  40.8 15.4 %collective-permute-start.22 = (bf16[384,1152]{1,0:T(8,128)(2,1)S(1)}, bf16[384,1152]{1,0:T(8,128)(2,1)S(1)}, u32[]{:S(2)}, u32[]{:S(2)}) collective-permute-start(bf16[384,1152]{1,0:T(8,128)(2,1)S(1)} %slice_dynamic-update-slice_fusion.refs_4_), channel_id=1, source_target_pairs={{0,8},{1,25},{2,10},{3,27},{4,12},{5,29},{6,14},{7,31},{8,0},{9,17... | collective-permute-start | bytes 2654216 | tf_op jit(solution)/shard_map/ppermute | solution.py:45
  49.5 7.6 %collective-permute-start.13 = (bf16[384,1152]{1,0:T(8,128)(2,1)S(1)}, bf16[384,1152]{1,0:T(8,128)(2,1)S(1)}, u32[]{:S(2)}, u32[]{:S(2)}) collective-permute-start(bf16[384,1152]{1,0:T(8,128)(2,1)S(1)} %slice_dynamic-update-slice_fusion.2.refs_0_), channel_id=1, source_target_pairs={{0,1},{1,0},{2,3},{3,2},{4,5},{5,4},{6,7},{7,6},{8,9},{9,8},{10,11... | collective-permute-start | bytes 2654216 | tf_op jit(solution)/shard_map/ppermute | solution.py:49
  49.5 10.1 %collective-permute-start.14 = (bf16[384,1152]{1,0:T(8,128)(2,1)S(1)}, bf16[384,1152]{1,0:T(8,128)(2,1)S(1)}, u32[]{:S(2)}, u32[]{:S(2)}) collective-permute-start(bf16[384,1152]{1,0:T(8,128)(2,1)S(1)} %slice_dynamic-update-slice_fusion.1.refs_2_), channel_id=1, source_target_pairs={{0,1},{1,0},{2,3},{3,2},{4,5},{5,4},{6,7},{7,6},{8,9},{9,8},{10,11... | collective-permute-start | bytes 2654216 | tf_op jit(solution)/shard_map/ppermute | solution.py:49
  53.1 6.5 %collective-permute-start.15 = (bf16[384,1152]{1,0:T(8,128)(2,1)S(1)}, bf16[384,1152]{1,0:T(8,128)(2,1)S(1)}, u32[]{:S(2)}, u32[]{:S(2)}) collective-permute-start(bf16[384,1152]{1,0:T(8,128)(2,1)S(1)} %slice_dynamic-update-slice_fusion.refs_4_), channel_id=1, source_target_pairs={{0,1},{1,0},{2,3},{3,2},{4,5},{5,4},{6,7},{7,6},{8,9},{9,8},{10,11... | collective-permute-start | bytes 2654216 | tf_op jit(solution)/shard_map/ppermute | solution.py:49
  53.5 16.0 %collective-permute-start.17 = (bf16[384,1152]{1,0:T(8,128)(2,1)S(1)}, bf16[384,1152]{1,0:T(8,128)(2,1)S(1)}, u32[]{:S(2)}, u32[]{:S(2)}) collective-permute-start(bf16[384,1152]{1,0:T(8,128)(2,1)S(1)} %slice_dynamic-update-slice_fusion.2.refs_0_), channel_id=1, source_target_pairs={{0,6},{1,3},{2,4},{3,1},{4,2},{5,7},{6,0},{7,5},{8,14},{9,11},{10,... | collective-permute-start | bytes 2654216 | tf_op jit(solution)/shard_map/ppermute | solution.py:45
  56.2 21.6 %copy-start.3 = (bf16[384,1152]{1,0:T(8,128)(2,1)}, bf16[384,1152]{1,0:T(8,128)(2,1)S(1)}, u32[]{:S(2)}) copy-start(bf16[384,1152]{1,0:T(8,128)(2,1)S(1)} %collective-permute-done.22.refs_4_) | copy-start | bytes 2654212
  56.2 14.3 %collective-permute-start.20 = (bf16[384,1152]{1,0:T(8,128)(2,1)S(1)}, bf16[384,1152]{1,0:T(8,128)(2,1)S(1)}, u32[]{:S(2)}, u32[]{:S(2)}) collective-permute-start(bf16[384,1152]{1,0:T(8,128)(2,1)S(1)} %slice_dynamic-update-slice_fusion.1.refs_2_), channel_id=1, source_target_pairs={{0,96},{1,33},{2,98},{3,35},{4,100},{5,37},{6,102},{7,39},{8,104},... | collective-permute-start | bytes 2654216 | tf_op jit(solution)/shard_map/ppermute | solution.py:45
  57.1 3.5 %copy-start.13 = (bf16[384,1152]{1,0:T(8,128)(2,1)}, bf16[384,1152]{1,0:T(8,128)(2,1)S(1)}, u32[]{:S(2)}) copy-start(bf16[384,1152]{1,0:T(8,128)(2,1)S(1)} %collective-permute-done.13.refs_1_) | copy-start | bytes 2654212
  57.1 14.3 %collective-permute-start.23 = (bf16[384,1152]{1,0:T(8,128)(2,1)S(1)}, bf16[384,1152]{1,0:T(8,128)(2,1)S(1)}, u32[]{:S(2)}, u32[]{:S(2)}) collective-permute-start(bf16[384,1152]{1,0:T(8,128)(2,1)S(1)} %slice_dynamic-update-slice_fusion.refs_4_), channel_id=1, source_target_pairs={{0,24},{1,9},{2,26},{3,11},{4,28},{5,13},{6,30},{7,15},{8,16},{9,1... | collective-permute-start | bytes 2654216 | tf_op jit(solution)/shard_map/ppermute | solution.py:45
  59.6 1.2 copy-start.14
  59.6 0.9 copy-start.15
  68.9 2.7 %collective-permute-start.25 = (bf16[384,1152]{1,0:T(8,128)(2,1)}, bf16[384,1152]{1,0:T(8,128)(2,1)S(1)}, u32[]{:S(2)}, u32[]{:S(2)}) collective-permute-start(bf16[384,1152]{1,0:T(8,128)(2,1)} %collective-permute-done.16.refs_0_), channel_id=1, source_target_pairs={{0,1},{1,0},{2,3},{3,2},{4,5},{5,4},{6,7},{7,6},{8,9},{9,8},{10,11... | collective-permute-start | bytes 2654216 | tf_op jit(solution)/shard_map/ppermute | solution.py:49
  69.0 5.2 %collective-permute-start.26 = (bf16[384,1152]{1,0:T(8,128)(2,1)}, bf16[384,1152]{1,0:T(8,128)(2,1)S(1)}, u32[]{:S(2)}, u32[]{:S(2)}) collective-permute-start(bf16[384,1152]{1,0:T(8,128)(2,1)} %collective-permute-done.19.refs_2_), channel_id=1, source_target_pairs={{0,1},{1,0},{2,3},{3,2},{4,5},{5,4},{6,7},{7,6},{8,9},{9,8},{10,11... | collective-permute-start | bytes 2654216 | tf_op jit(solution)/shard_map/ppermute | solution.py:49
  69.5 9.7 %copy-start.4 = (bf16[384,1152]{1,0:T(8,128)(2,1)}, bf16[384,1152]{1,0:T(8,128)(2,1)S(1)}, u32[]{:S(2)}) copy-start(bf16[384,1152]{1,0:T(8,128)(2,1)S(1)} %collective-permute-done.17.refs_6_) | copy-start | bytes 2654212
  69.5 5.8 %collective-permute-start.27 = (bf16[384,1152]{1,0:T(8,128)(2,1)S(1)}, bf16[384,1152]{1,0:T(8,128)(2,1)S(1)}, u32[]{:S(2)}, u32[]{:S(2)}) collective-permute-start(bf16[384,1152]{1,0:T(8,128)(2,1)S(1)} %collective-permute-done.22.refs_4_), channel_id=1, source_target_pairs={{0,1},{1,0},{2,3},{3,2},{4,5},{5,4},{6,7},{7,6},{8,9},{9,8},{10,11... | collective-permute-start | bytes 2654216 | tf_op jit(solution)/shard_map/ppermute | solution.py:49
  70.6 8.6 %copy-start.5 = (bf16[384,1152]{1,0:T(8,128)(2,1)}, bf16[384,1152]{1,0:T(8,128)(2,1)S(1)}, u32[]{:S(2)}) copy-start(bf16[384,1152]{1,0:T(8,128)(2,1)S(1)} %collective-permute-done.20.refs_8_) | copy-start | bytes 2654212
  70.6 7.3 %collective-permute-start.18 = (bf16[384,1152]{1,0:T(8,128)(2,1)S(1)}, bf16[384,1152]{1,0:T(8,128)(2,1)S(1)}, u32[]{:S(2)}, u32[]{:S(2)}) collective-permute-start(bf16[384,1152]{1,0:T(8,128)(2,1)S(1)} %collective-permute-done.17.refs_6_), channel_id=1, source_target_pairs={{0,1},{1,0},{2,3},{3,2},{4,5},{5,4},{6,7},{7,6},{8,9},{9,8},{10,11... | collective-permute-start | bytes 2654216 | tf_op jit(solution)/shard_map/ppermute | solution.py:49
  71.4 7.8 %copy-start.6 = (bf16[384,1152]{1,0:T(8,128)(2,1)}, bf16[384,1152]{1,0:T(8,128)(2,1)S(1)}, u32[]{:S(2)}) copy-start(bf16[384,1152]{1,0:T(8,128)(2,1)S(1)} %collective-permute-done.23.refs_10_) | copy-start | bytes 2654212
  71.4 6.8 %collective-permute-start.21 = (bf16[384,1152]{1,0:T(8,128)(2,1)S(1)}, bf16[384,1152]{1,0:T(8,128)(2,1)S(1)}, u32[]{:S(2)}, u32[]{:S(2)}) collective-permute-start(bf16[384,1152]{1,0:T(8,128)(2,1)S(1)} %collective-permute-done.20.refs_8_), channel_id=1, source_target_pairs={{0,1},{1,0},{2,3},{3,2},{4,5},{5,4},{6,7},{7,6},{8,9},{9,8},{10,11... | collective-permute-start | bytes 2654216 | tf_op jit(solution)/shard_map/ppermute | solution.py:49
  71.6 7.6 %copy-start.7 = (bf16[384,1152]{1,0:T(8,128)(2,1)}, bf16[384,1152]{1,0:T(8,128)(2,1)S(1)}, u32[]{:S(2)}) copy-start(bf16[384,1152]{1,0:T(8,128)(2,1)S(1)} %collective-permute-done.25.refs_7_) | copy-start | bytes 2654212
  71.6 6.7 %collective-permute-start.24 = (bf16[384,1152]{1,0:T(8,128)(2,1)S(1)}, bf16[384,1152]{1,0:T(8,128)(2,1)S(1)}, u32[]{:S(2)}, u32[]{:S(2)}) collective-permute-start(bf16[384,1152]{1,0:T(8,128)(2,1)S(1)} %collective-permute-done.23.refs_10_), channel_id=1, source_target_pairs={{0,1},{1,0},{2,3},{3,2},{4,5},{5,4},{6,7},{7,6},{8,9},{9,8},{10,11... | collective-permute-start | bytes 2654216 | tf_op jit(solution)/shard_map/ppermute | solution.py:49
  74.1 5.1 %copy-start.8 = (bf16[384,1152]{1,0:T(8,128)(2,1)}, bf16[384,1152]{1,0:T(8,128)(2,1)S(1)}, u32[]{:S(2)}) copy-start(bf16[384,1152]{1,0:T(8,128)(2,1)S(1)} %collective-permute-done.26.refs_9_) | copy-start | bytes 2654212
  74.1 16.4 %collective-permute-start.28 = (bf16[384,1152]{1,0:T(8,128)(2,1)}, bf16[384,1152]{1,0:T(8,128)(2,1)}, u32[]{:S(2)}, u32[]{:S(2)}) collective-permute-start(bf16[384,1152]{1,0:T(8,128)(2,1)} %collective-permute-done.16.refs_0_), channel_id=1, source_target_pairs={{0,6},{1,3},{2,4},{3,1},{4,2},{5,7},{6,0},{7,5},{8,14},{9,11},{10,... | collective-permute-start | bytes 2654216 | tf_op jit(solution)/shard_map/ppermute | solution.py:45
  75.3 3.9 %copy-start.9 = (bf16[384,1152]{1,0:T(8,128)(2,1)}, bf16[384,1152]{1,0:T(8,128)(2,1)S(1)}, u32[]{:S(2)}) copy-start(bf16[384,1152]{1,0:T(8,128)(2,1)S(1)} %collective-permute-done.27.refs_11_) | copy-start | bytes 2654212
  75.3 15.3 %collective-permute-start.30 = (bf16[384,1152]{1,0:T(8,128)(2,1)}, bf16[384,1152]{1,0:T(8,128)(2,1)}, u32[]{:S(2)}, u32[]{:S(2)}) collective-permute-start(bf16[384,1152]{1,0:T(8,128)(2,1)} %collective-permute-done.19.refs_2_), channel_id=1, source_target_pairs={{0,96},{1,33},{2,98},{3,35},{4,100},{5,37},{6,102},{7,39},{8,104},... | collective-permute-start | bytes 2654216 | tf_op jit(solution)/shard_map/ppermute | solution.py:45
  77.9 1.4 copy-start.10
  77.9 14.4 %collective-permute-start.32 = (bf16[384,1152]{1,0:T(8,128)(2,1)S(1)}, bf16[384,1152]{1,0:T(8,128)(2,1)}, u32[]{:S(2)}, u32[]{:S(2)}) collective-permute-start(bf16[384,1152]{1,0:T(8,128)(2,1)S(1)} %collective-permute-done.22.refs_4_), channel_id=1, source_target_pairs={{0,24},{1,9},{2,26},{3,11},{4,28},{5,13},{6,30},{7,15},{8,16},{9,1... | collective-permute-start | bytes 2654216 | tf_op jit(solution)/shard_map/ppermute | solution.py:45
  78.2 1.3 copy-start.11
  78.2 0.9 copy-start.12
  90.5 2.7 %collective-permute-start.29 = (bf16[384,1152]{1,0:T(8,128)(2,1)}, bf16[384,1152]{1,0:T(8,128)(2,1)S(1)}, u32[]{:S(2)}, u32[]{:S(2)}) collective-permute-start(bf16[384,1152]{1,0:T(8,128)(2,1)} %collective-permute-done.28.refs_0_), channel_id=1, source_target_pairs={{0,1},{1,0},{2,3},{3,2},{4,5},{5,4},{6,7},{7,6},{8,9},{9,8},{10,11... | collective-permute-start | bytes 2654216 | tf_op jit(solution)/shard_map/ppermute | solution.py:49
  90.6 3.9 %collective-permute-start.31 = (bf16[384,1152]{1,0:T(8,128)(2,1)}, bf16[384,1152]{1,0:T(8,128)(2,1)S(1)}, u32[]{:S(2)}, u32[]{:S(2)}) collective-permute-start(bf16[384,1152]{1,0:T(8,128)(2,1)} %collective-permute-done.30.refs_2_), channel_id=1, source_target_pairs={{0,1},{1,0},{2,3},{3,2},{4,5},{5,4},{6,7},{7,6},{8,9},{9,8},{10,11... | collective-permute-start | bytes 2654216 | tf_op jit(solution)/shard_map/ppermute | solution.py:49
  92.3 3.5 %collective-permute-start.33 = (bf16[384,1152]{1,0:T(8,128)(2,1)}, bf16[384,1152]{1,0:T(8,128)(2,1)S(1)}, u32[]{:S(2)}, u32[]{:S(2)}) collective-permute-start(bf16[384,1152]{1,0:T(8,128)(2,1)} %collective-permute-done.32.refs_4_), channel_id=1, source_target_pairs={{0,1},{1,0},{2,3},{3,2},{4,5},{5,4},{6,7},{7,6},{8,9},{9,8},{10,11... | collective-permute-start | bytes 2654216 | tf_op jit(solution)/shard_map/ppermute | solution.py:49
  93.2 2.5 %copy-start.16 = (bf16[384,1152]{1,0:T(8,128)(2,1)}, bf16[384,1152]{1,0:T(8,128)(2,1)S(1)}, u32[]{:S(2)}) copy-start(bf16[384,1152]{1,0:T(8,128)(2,1)S(1)} %collective-permute-done.29.refs_1_) | copy-start | bytes 2654212
  94.5 1.3 copy-start.17
  95.8 0.9 copy-start.18

commit v4 on v3

--- a/solution.py
+++ b/solution.py
@@ -97,15 +97,21 @@
 
 def mlp_sets(core_ref, sets, kept_refs, hidden_ref, acc_ref, given, up_buf, down_buf, sems, kept_sems):
     kept = []
+
+    def keep(index):
+        for kind, buf in enumerate((up_buf, down_buf)):
+            place = 2 * index + kind
+            kept.append(pltpu.make_async_copy(buf.at[index % 2], kept_refs[place], kept_sems.at[place]))
+            kept[-1].start()
+
     for index, pairs in enumerate(sets):
         slot = index % 2
         if index + 1 < len(sets):
             start_set(core_ref, sets[index + 1], up_buf, down_buf, sems, 1 - slot)
         wait_set(pairs, up_buf, down_buf, sems, slot)
-        for kind, buf in enumerate((up_buf, down_buf)):
-            place = 2 * index + kind
-            kept.append(pltpu.make_async_copy(buf.at[slot], kept_refs[place], kept_sems.at[place]))
-            kept[-1].start()
+        if index + 1 == len(sets):
+            for done in range(len(sets)):
+                keep(done)
         part = mlp_part(hidden_ref[...], up_buf[slot], down_buf[slot])
         if index > 0:
             acc_ref[...] += part
@@ -317,7 +323,7 @@
         )
         return carry
 
-    lax.fori_loop(0, window, modulate, 0)
+    lax.fori_loop(0, window - 1, modulate, 0)
     for index in range(len(sets)):
         if index + 1 < len(sets):
             for copy in copies(index + 1):
@@ -334,7 +340,7 @@
         noise = got_ref[place, rows : 2 * rows, :].astype(f32)
         return updated + (dt_ref[begin + place] * drift + sigma_ref[begin + place] * noise)
 
-    lax.fori_loop(0, window, update, prefix_ref[advance])
+    out_ref[window - 1] = lax.fori_loop(0, window - 1, update, prefix_ref[advance]).astype(bf16)
 
 
 def second_sweep(begin, advance, dt, sigma, got, mod, weights):
@@ -348,8 +354,8 @@
         out_specs=VMEM,
         scratch_shapes=[
             pltpu.VMEM((window + SLIDE, rows, width), f32),
-            pltpu.VMEM((window * rows, width), bf16),
-            pltpu.VMEM((window * rows, width), f32),
+            pltpu.VMEM(((window - 1) * rows, width), bf16),
+            pltpu.VMEM(((window - 1) * rows, width), f32),
         ]
         + weight_scratch(units, width, 2)[:3],
         compiler_params=room(56),

time: 160 us -> 160 us (level)
  no operation moved by 1% of the time
where the time goes in v4:
time: 160 us; the launch traced here: 159 us
  Pallas kernels  40.7 us (25%)
  blocking collectives  39.9 us (25%)
  starting transfers between devices  34.2 us (21%)
  waiting for transfers between devices  23.8 us (15%)
  other arithmetic  7.63 us (5%)
  local copies, waits for them, and re-layouts  6.28 us (4%)
  matrix products  5.2 us (3%)
    ppermute x21, starting transfers between devices, send(): return lax.ppermute(rows, ALL, neighbour(axis, first))  32 us
    all_to_all x1, blocking collectives, per_device(): got = lax.all_to_all(sent, 'tm', 0, 0, tiled=True)  24.6 us
    ppermute x21, waiting for transfers between devices, send(): return lax.ppermute(rows, ALL, neighbour(axis, first))  18.4 us
    all_to_all x1, blocking collectives, per_device(): final = lax.all_to_all(updated, 'tm', 0, 0, tiled=True)  15.3 us
    pallas_call x1, Pallas kernels, second_sweep(): pl.pallas_call(functools.partial(second_kernel, len(weights)), out_shape=...  14 us
    pallas_call x1, Pallas kernels, next_piece(): pl.pallas_call(functools.partial(next_kernel, len(weights)), out_shape=[j...  10.6 us
    pallas_call x1, Pallas kernels, own_piece(): pl.pallas_call(functools.partial(own_kernel, len(weights)), out_shape=[ja...  8 us
    pallas_call x1, Pallas kernels, far_piece(): pl.pallas_call(functools.partial(far_kernel, len(weights)), out_shape=[ja...  7.99 us
  transfers between devices with their start and end apart: 34, of which 15 were waited for; matrix products, arithmetic and copies ran while one was open for 7% of the time, Pallas kernels for 12%

profile of v4, /device:TPU:0, one launch (start us, length us, event | category | flops | bytes accessed | tf_op | source)
XLA Modules:
  0.0 159.4 jit_solution(14249108127418510748)
XLA Ops:
  0.0 0.9 broadcast_select_fusion
  2.3 1.0 maximum_select_fusion
  3.3 0.7 fusion.5
  4.0 1.6 collective-permute-start.1
  5.6 1.6 collective-permute-start.9
  7.2 1.9 %collective-permute-start.5 = (bf16[24,1152]{1,0:T(8,128)(2,1)S(1)}, bf16[24,1152]{1,0:T(8,128)(2,1)S(1)}, u32[]{:S(2)}, u32[]{:S(2)}) collective-permute-start(bf16[24,1152]{1,0:T(8,128)(2,1)S(1)} %get-tuple-element.84), channel_id=1, source_target_pairs={{0,8},{1,25},{2,10},{3,27},{4,12},{5,29},{6,14},{7,31},{8,0},{9,17... | collective-permute-start | bytes 165896 | tf_op jit(solution)/shard_map/ppermute | solution.py:45
  9.1 2.2 %collective-permute-start.2 = (bf16[48,1152]{1,0:T(8,128)(2,1)S(1)}, bf16[48,1152]{1,0:T(8,128)(2,1)S(1)}, u32[]{:S(2)}, u32[]{:S(2)}) collective-permute-start(bf16[48,1152]{1,0:T(8,128)(2,1)S(1)} %pad_maximum_fusion.3), channel_id=1, source_target_pairs={{0,96},{1,33},{2,98},{3,35},{4,100},{5,37},{6,102},{7,39},{8,104},... | collective-permute-start | bytes 331784 | tf_op jit(solution)/shard_map/ppermute | solution.py:45
  11.3 2.9 %collective-permute-start.10 = (bf16[48,1152]{1,0:T(8,128)(2,1)S(1)}, bf16[48,1152]{1,0:T(8,128)(2,1)S(1)}, u32[]{:S(2)}, u32[]{:S(2)}) collective-permute-start(bf16[48,1152]{1,0:T(8,128)(2,1)S(1)} %pad_maximum_fusion.5), channel_id=1, source_target_pairs={{0,6},{1,3},{2,4},{3,1},{4,2},{5,7},{6,0},{7,5},{8,14},{9,11},{10,... | collective-permute-start | bytes 331784 | tf_op jit(solution)/shard_map/ppermute | solution.py:45
  14.2 4.1 %collective-permute-start.6 = (bf16[48,1152]{1,0:T(8,128)(2,1)S(1)}, bf16[48,1152]{1,0:T(8,128)(2,1)S(1)}, u32[]{:S(2)}, u32[]{:S(2)}) collective-permute-start(bf16[48,1152]{1,0:T(8,128)(2,1)S(1)} %pad_maximum_fusion.4), channel_id=1, source_target_pairs={{0,24},{1,9},{2,26},{3,11},{4,28},{5,13},{6,30},{7,15},{8,16},{9,1... | collective-permute-start | bytes 331784 | tf_op jit(solution)/shard_map/ppermute | solution.py:45
  18.4 0.6 constant_dynamic-update-slice_fusion.3
  19.0 0.6 constant_dynamic-update-slice_fusion.2
  19.7 0.6 constant_dynamic-update-slice_fusion.1
  20.4 0.6 constant_dynamic-update-slice_fusion.21
  21.1 0.6 constant_dynamic-update-slice_fusion.20
  21.7 0.6 constant_dynamic-update-slice_fusion.19
  22.4 0.3 collective-permute-start.11
  22.8 0.2 collective-permute-start.7
  23.1 3.3 %collective-permute-done.3 = bf16[96,1152]{1,0:T(8,128)(2,1)S(1)} collective-permute-done((bf16[96,1152]{1,0:T(8,128)(2,1)S(1)}, bf16[96,1152]{1,0:T(8,128)(2,1)S(1)}, u32[]{:S(2)}, u32[]{:S(2)}) %collective-permute-start.3) | collective-permute-done | bytes 221216 | tf_op jit(solution)/shard_map/ppermute | solution.py:45
  26.5 1.9 %collective-permute-done.11 = bf16[96,1152]{1,0:T(8,128)(2,1)S(1)} collective-permute-done((bf16[96,1152]{1,0:T(8,128)(2,1)S(1)}, bf16[96,1152]{1,0:T(8,128)(2,1)S(1)}, u32[]{:S(2)}, u32[]{:S(2)}) %collective-permute-start.11) | collective-permute-done | bytes 221216 | tf_op jit(solution)/shard_map/ppermute | solution.py:45
  28.4 0.7 constant_dynamic-update-slice_fusion.18
  29.1 0.8 collective-permute-start.12
  29.9 3.1 %collective-permute-start.8 = (bf16[192,1152]{1,0:T(8,128)(2,1)S(1)}, bf16[192,1152]{1,0:T(8,128)(2,1)S(1)}, u32[]{:S(2)}, u32[]{:S(2)}) collective-permute-start(bf16[192,1152]{1,0:T(8,128)(2,1)S(1)} %constant_dynamic-update-slice_fusion.9), channel_id=1, source_target_pairs={{0,6},{1,3},{2,4},{3,1},{4,2},{5,7},{6,0},{7,5},{8,14},{9,11},{10,... | collective-permute-start | bytes 1327112 | tf_op jit(solution)/shard_map/ppermute | solution.py:45
  33.0 2.9 %collective-permute-done.4 = bf16[192,1152]{1,0:T(8,128)(2,1)S(1)} collective-permute-done((bf16[192,1152]{1,0:T(8,128)(2,1)S(1)}, bf16[192,1152]{1,0:T(8,128)(2,1)S(1)}, u32[]{:S(2)}, u32[]{:S(2)}) %collective-permute-start.4) | collective-permute-done | bytes 442400 | tf_op jit(solution)/shard_map/ppermute | solution.py:45
  36.1 2.7 %collective-permute-done.12 = bf16[192,1152]{1,0:T(8,128)(2,1)S(1)} collective-permute-done((bf16[192,1152]{1,0:T(8,128)(2,1)}, bf16[192,1152]{1,0:T(8,128)(2,1)S(1)}, u32[]{:S(2)}, u32[]{:S(2)}) %collective-permute-start.12) | collective-permute-done | bytes 442400 | tf_op jit(solution)/shard_map/ppermute | solution.py:45
  38.9 0.7 collective-permute-done.8
  39.5 0.1 select_dynamic-update-slice_fusion.1
  39.9 0.4 collective-permute-start.16
  40.3 0.5 collective-permute-start.19
  40.8 2.0 %collective-permute-start.22 = (bf16[384,1152]{1,0:T(8,128)(2,1)S(1)}, bf16[384,1152]{1,0:T(8,128)(2,1)S(1)}, u32[]{:S(2)}, u32[]{:S(2)}) collective-permute-start(bf16[384,1152]{1,0:T(8,128)(2,1)S(1)} %slice_dynamic-update-slice_fusion.refs_4_), channel_id=1, source_target_pairs={{0,8},{1,25},{2,10},{3,27},{4,12},{5,29},{6,14},{7,31},{8,0},{9,17... | collective-permute-start | bytes 2654216 | tf_op jit(solution)/shard_map/ppermute | solution.py:45
  42.8 0.5 pad_convert_fusion
  43.4 1.0 multiply_cosine_fusion
  44.3 5.2 %fusion.mod_ref = f32[24,3456]{1,0:T(8,128)} fusion(bf16[1152,3456]{1,0:T(8,128)(2,1)} %param.17, f32[24,576]{1,0:T(8,128)S(1)} %get-tuple-element.96, f32[24,576]{1,0:T(8,128)S(1)} %get-tuple-element.95, f32[1152]{0:T(1024)S(1)} %reduce), kind=kOutput, calls=%fused_computation.48 | convolution fusion | flops 191296512 | bytes 8409600 | tf_op jit(solution)/shard_map/dot_general | solution.py:400
  49.5 0.5 collective-permute-start.14
  50.0 3.1 %collective-permute-done.16.refs_0_ = bf16[384,1152]{1,0:T(8,128)(2,1)} collective-permute-done((bf16[384,1152]{1,0:T(8,128)(2,1)S(1)}, bf16[384,1152]{1,0:T(8,128)(2,1)}, u32[]{:S(2)}, u32[]{:S(2)}) %collective-permute-start.16) | collective-permute-done | bytes 884768 | tf_op jit(solution)/shard_map/ppermute | solution.py:45
  53.1 0.4 collective-permute-done.19.refs_2_
  53.5 2.7 %collective-permute-start.17 = (bf16[384,1152]{1,0:T(8,128)(2,1)S(1)}, bf16[384,1152]{1,0:T(8,128)(2,1)S(1)}, u32[]{:S(2)}, u32[]{:S(2)}) collective-permute-start(bf16[384,1152]{1,0:T(8,128)(2,1)S(1)} %slice_dynamic-update-slice_fusion.2.refs_0_), channel_id=1, source_target_pairs={{0,6},{1,3},{2,4},{3,1},{4,2},{5,7},{6,0},{7,5},{8,14},{9,11},{10,... | collective-permute-start | bytes 2654216 | tf_op jit(solution)/shard_map/ppermute | solution.py:45
  56.2 0.8 collective-permute-start.20
  57.1 2.5 %collective-permute-start.23 = (bf16[384,1152]{1,0:T(8,128)(2,1)S(1)}, bf16[384,1152]{1,0:T(8,128)(2,1)S(1)}, u32[]{:S(2)}, u32[]{:S(2)}) collective-permute-start(bf16[384,1152]{1,0:T(8,128)(2,1)S(1)} %slice_dynamic-update-slice_fusion.refs_4_), channel_id=1, source_target_pairs={{0,24},{1,9},{2,26},{3,11},{4,28},{5,13},{6,30},{7,15},{8,16},{9,1... | collective-permute-start | bytes 2654216 | tf_op jit(solution)/shard_map/ppermute | solution.py:45
  59.7 0.9 copy-done.15
  60.6 0.3 copy-done.14
  60.9 8.0 %own_piece.1 = (bf16[256,1152]{1,0:T(8,128)(2,1)}, f32[256,1152]{1,0:T(8,128)}, bf16[1152,1152]{1,0:T(8,128)(2,1)}, bf16[1152,1152]{1,0:T(8,128)(2,1)}) custom-call(s32[1]{0:T(128)} %bitcast.core_ref, f32[256,1152]{1,0:T(8,128)} %bitcast.13, f32[24,3456]{1,0:T(8,128)} %fusion.mod_ref, bf16[384,1152]{1,0:T(8,128)(2,1)} %copy-done.2, ...), custom_call_target="tpu_custom_call" | custom-call | tf_op jit(solution)/shard_map/own_piece/pallas_call | solution.py:193
  69.0 0.5 collective-permute-start.26
  69.5 1.0 collective-permute-done.20.refs_8_
  70.6 0.8 collective-permute-done.23.refs_10_
  71.4 0.2 collective-permute-done.25.refs_7_
  71.6 0.4 collective-permute-start.24
  71.9 2.2 %collective-permute-done.26.refs_9_ = bf16[384,1152]{1,0:T(8,128)(2,1)S(1)} collective-permute-done((bf16[384,1152]{1,0:T(8,128)(2,1)}, bf16[384,1152]{1,0:T(8,128)(2,1)S(1)}, u32[]{:S(2)}, u32[]{:S(2)}) %collective-permute-start.26) | collective-permute-done | bytes 884768 | tf_op jit(solution)/shard_map/ppermute | solution.py:49
  74.1 1.2 collective-permute-start.28
  75.3 2.5 %collective-permute-start.30 = (bf16[384,1152]{1,0:T(8,128)(2,1)}, bf16[384,1152]{1,0:T(8,128)(2,1)}, u32[]{:S(2)}, u32[]{:S(2)}) collective-permute-start(bf16[384,1152]{1,0:T(8,128)(2,1)} %collective-permute-done.19.refs_2_), channel_id=1, source_target_pairs={{0,96},{1,33},{2,98},{3,35},{4,100},{5,37},{6,102},{7,39},{8,104},... | collective-permute-start | bytes 2654216 | tf_op jit(solution)/shard_map/ppermute | solution.py:45
  77.9 0.4 collective-permute-start.32
  78.3 0.9 copy-done.12
  79.2 0.3 copy-done.11
  79.5 10.6 %next_piece.1 = (f32[256,1152]{1,0:T(8,128)}, bf16[1152,1152]{1,0:T(8,128)(2,1)}, bf16[1152,1152]{1,0:T(8,128)(2,1)}, bf16[1152,1152]{1,0:T(8,128)(2,1)}, bf16[1152,1152]{1,0:T(8,128)(2,1)}) custom-call(s32[1]{0:T(128)} %bitcast.core_ref, bf16[256,1152]{1,0:T(8,128)(2,1)} %get-tuple-element.41.hidden_in, f32[256,1152]{1,0:T(8,128)} %get-tuple-element.42.acc_in, ...), custom_call_target="tpu_custom_call" | custom-call | tf_op jit(solution)/shard_map/next_piece/pallas_call | solution.py:226
  90.3 0.5 collective-permute-start.31
  90.8 1.5 collective-permute-done.32.refs_4_
  92.3 0.6 collective-permute-done.29.refs_1_
  92.9 1.3 collective-permute-done.31.refs_3_
  94.2 1.3 collective-permute-done.33.refs_5_
  95.4 0.9 copy-done.18
  96.3 8.0 %far_piece.1 = (bf16[16,32,1152]{2,1,0:T(8,128)(2,1)}, bf16[1152,1152]{1,0:T(8,128)(2,1)}, bf16[1152,1152]{1,0:T(8,128)(2,1)}) custom-call(s32[1]{0:T(128)} %bitcast.core_ref, f32[1]{0:T(128)} %bitcast.1.first_ref, s32[1]{0:T(128)} %bitcast.3.begin_ref, f32[1000]{0:T(1024)} %dt_ref.3, f32[1000]{0:T(1024)} %sigma_ref.3, ...), custom_call_target="tpu_custom_call" | custom-call | tf_op jit(solution)/shard_map/far_piece/pallas_call | solution.py:276
  104.3 24.6 %all_to_all.10.got_ref = bf16[16,32,1152]{2,1,0:T(8,128)(2,1)} all-to-all(bf16[16,32,1152]{2,1,0:T(8,128)(2,1)} %get-tuple-element.56), channel_id=1, replica_groups=mesh['tm'=16,'batch'=8] {'tm'}, dimensions={0} | all-to-all | bytes 2359296 | tf_op jit(solution)/shard_map/all_to_all | solution.py:424
  128.9 14.0 %second_sweep.1 = bf16[16,16,1152]{2,1,0:T(8,128)(2,1)} custom-call(s32[1]{0:T(128)} %copy.41.begin_ref, s32[1]{0:T(128)} %copy.42.advance_ref, f32[1000]{0:T(1024)} %dt_ref.3, f32[1000]{0:T(1024)} %sigma_ref.3, bf16[16,32,1152]{2,1,0:T(8,128)(2,1)} %all_to_all.10.got_ref, f32[24,3456]{1,0:T(8,128)} %fusion.mod_ref, ...), custom_call_target="tpu_custom_call" | custom-call | tf_op jit(solution)/shard_map/second_sweep/pallas_call | solution.py:350
  143.0 15.3 %all_to_all.11 = bf16[16,16,1152]{2,1,0:T(8,128)(2,1)S(1)} all-to-all(bf16[16,16,1152]{2,1,0:T(8,128)(2,1)} %second_sweep.1), channel_id=1, replica_groups=mesh['tm'=16,'batch'=8] {'tm'}, dimensions={0} | all-to-all | bytes 1179648 | tf_op jit(solution)/shard_map/all_to_all | solution.py:434
  158.3 1.1 convert.2
  (94 shorter events, 1.3 us)
Async XLA Ops:
  0.9 1.4 collective-permute-start
  4.0 5.1 %collective-permute-start.1 = (bf16[24,1152]{1,0:T(8,128)(2,1)S(1)}, bf16[24,1152]{1,0:T(8,128)(2,1)S(1)}, u32[]{:S(2)}, u32[]{:S(2)}) collective-permute-start(bf16[24,1152]{1,0:T(8,128)(2,1)S(1)} %get-tuple-element.85), channel_id=1, source_target_pairs={{0,32},{1,97},{2,34},{3,99},{4,36},{5,101},{6,38},{7,103},{8,40},{... | collective-permute-start | bytes 165896 | tf_op jit(solution)/shard_map/ppermute | solution.py:45
  5.6 5.7 %collective-permute-start.9 = (bf16[24,1152]{1,0:T(8,128)(2,1)S(1)}, bf16[24,1152]{1,0:T(8,128)(2,1)S(1)}, u32[]{:S(2)}, u32[]{:S(2)}) collective-permute-start(bf16[24,1152]{1,0:T(8,128)(2,1)S(1)} %get-tuple-element.77), channel_id=1, source_target_pairs={{0,2},{1,7},{2,0},{3,5},{4,6},{5,3},{6,4},{7,1},{8,10},{9,15},{10,... | collective-permute-start | bytes 165896 | tf_op jit(solution)/shard_map/ppermute | solution.py:45
  7.2 7.0 %collective-permute-start.5 = (bf16[24,1152]{1,0:T(8,128)(2,1)S(1)}, bf16[24,1152]{1,0:T(8,128)(2,1)S(1)}, u32[]{:S(2)}, u32[]{:S(2)}) collective-permute-start(bf16[24,1152]{1,0:T(8,128)(2,1)S(1)} %get-tuple-element.84), channel_id=1, source_target_pairs={{0,8},{1,25},{2,10},{3,27},{4,12},{5,29},{6,14},{7,31},{8,0},{9,17... | collective-permute-start | bytes 165896 | tf_op jit(solution)/shard_map/ppermute | solution.py:45
  9.1 9.2 %collective-permute-start.2 = (bf16[48,1152]{1,0:T(8,128)(2,1)S(1)}, bf16[48,1152]{1,0:T(8,128)(2,1)S(1)}, u32[]{:S(2)}, u32[]{:S(2)}) collective-permute-start(bf16[48,1152]{1,0:T(8,128)(2,1)S(1)} %pad_maximum_fusion.3), channel_id=1, source_target_pairs={{0,96},{1,33},{2,98},{3,35},{4,100},{5,37},{6,102},{7,39},{8,104},... | collective-permute-start | bytes 331784 | tf_op jit(solution)/shard_map/ppermute | solution.py:45
  11.3 9.1 %collective-permute-start.10 = (bf16[48,1152]{1,0:T(8,128)(2,1)S(1)}, bf16[48,1152]{1,0:T(8,128)(2,1)S(1)}, u32[]{:S(2)}, u32[]{:S(2)}) collective-permute-start(bf16[48,1152]{1,0:T(8,128)(2,1)S(1)} %pad_maximum_fusion.5), channel_id=1, source_target_pairs={{0,6},{1,3},{2,4},{3,1},{4,2},{5,7},{6,0},{7,5},{8,14},{9,11},{10,... | collective-permute-start | bytes 331784 | tf_op jit(solution)/shard_map/ppermute | solution.py:45
  14.2 8.5 %collective-permute-start.6 = (bf16[48,1152]{1,0:T(8,128)(2,1)S(1)}, bf16[48,1152]{1,0:T(8,128)(2,1)S(1)}, u32[]{:S(2)}, u32[]{:S(2)}) collective-permute-start(bf16[48,1152]{1,0:T(8,128)(2,1)S(1)} %pad_maximum_fusion.4), channel_id=1, source_target_pairs={{0,24},{1,9},{2,26},{3,11},{4,28},{5,13},{6,30},{7,15},{8,16},{9,1... | collective-permute-start | bytes 331784 | tf_op jit(solution)/shard_map/ppermute | solution.py:45
  20.3 6.0 %copy-start.19 = (bf16[192,1152]{1,0:T(8,128)(2,1)S(1)}, bf16[192,1152]{1,0:T(8,128)(2,1)}, u32[]{:S(2)}) copy-start(bf16[192,1152]{1,0:T(8,128)(2,1)} %get-tuple-element.92) | copy-start | bytes 1327108
  20.3 6.0 %collective-permute-start.3 = (bf16[96,1152]{1,0:T(8,128)(2,1)S(1)}, bf16[96,1152]{1,0:T(8,128)(2,1)S(1)}, u32[]{:S(2)}, u32[]{:S(2)}) collective-permute-start(bf16[96,1152]{1,0:T(8,128)(2,1)S(1)} %pad_maximum_fusion), channel_id=1, source_target_pairs={{0,8},{1,25},{2,10},{3,27},{4,12},{5,29},{6,14},{7,31},{8,0},{9,17... | collective-permute-start | bytes 663560 | tf_op jit(solution)/shard_map/ppermute | solution.py:45
  22.4 6.0 %collective-permute-start.11 = (bf16[96,1152]{1,0:T(8,128)(2,1)S(1)}, bf16[96,1152]{1,0:T(8,128)(2,1)S(1)}, u32[]{:S(2)}, u32[]{:S(2)}) collective-permute-start(bf16[96,1152]{1,0:T(8,128)(2,1)S(1)} %pad_maximum_fusion.2), channel_id=1, source_target_pairs={{0,32},{1,97},{2,34},{3,99},{4,36},{5,101},{6,38},{7,103},{8,40},{... | collective-permute-start | bytes 663560 | tf_op jit(solution)/shard_map/ppermute | solution.py:45
  22.8 7.1 %collective-permute-start.7 = (bf16[96,1152]{1,0:T(8,128)(2,1)S(1)}, bf16[96,1152]{1,0:T(8,128)(2,1)S(1)}, u32[]{:S(2)}, u32[]{:S(2)}) collective-permute-start(bf16[96,1152]{1,0:T(8,128)(2,1)S(1)} %pad_maximum_fusion.1), channel_id=1, source_target_pairs={{0,2},{1,7},{2,0},{3,5},{4,6},{5,3},{6,4},{7,1},{8,10},{9,15},{10,... | collective-permute-start | bytes 663560 | tf_op jit(solution)/shard_map/ppermute | solution.py:45
  26.4 9.6 %collective-permute-start.4 = (bf16[192,1152]{1,0:T(8,128)(2,1)S(1)}, bf16[192,1152]{1,0:T(8,128)(2,1)S(1)}, u32[]{:S(2)}, u32[]{:S(2)}) collective-permute-start(bf16[192,1152]{1,0:T(8,128)(2,1)S(1)} %constant_dynamic-update-slice_fusion), channel_id=1, source_target_pairs={{0,24},{1,9},{2,26},{3,11},{4,28},{5,13},{6,30},{7,15},{8,16},{9,1... | collective-permute-start | bytes 1327112 | tf_op jit(solution)/shard_map/ppermute | solution.py:45
  29.1 9.7 %collective-permute-start.12 = (bf16[192,1152]{1,0:T(8,128)(2,1)}, bf16[192,1152]{1,0:T(8,128)(2,1)S(1)}, u32[]{:S(2)}, u32[]{:S(2)}) collective-permute-start(bf16[192,1152]{1,0:T(8,128)(2,1)} %constant_dynamic-update-slice_fusion.18), channel_id=1, source_target_pairs={{0,96},{1,33},{2,98},{3,35},{4,100},{5,37},{6,102},{7,39},{8,104},... | collective-permute-start | bytes 1327112 | tf_op jit(solution)/shard_map/ppermute | solution.py:45
  29.9 9.6 %collective-permute-start.8 = (bf16[192,1152]{1,0:T(8,128)(2,1)S(1)}, bf16[192,1152]{1,0:T(8,128)(2,1)S(1)}, u32[]{:S(2)}, u32[]{:S(2)}) collective-permute-start(bf16[192,1152]{1,0:T(8,128)(2,1)S(1)} %constant_dynamic-update-slice_fusion.9), channel_id=1, source_target_pairs={{0,6},{1,3},{2,4},{3,1},{4,2},{5,7},{6,0},{7,5},{8,14},{9,11},{10,... | collective-permute-start | bytes 1327112 | tf_op jit(solution)/shard_map/ppermute | solution.py:45
  36.0 7.4 %copy-start.20 = (f32[1,1152]{1,0:T(1,128)S(1)}, f32[1,1152]{1,0:T(1,128)}, u32[]{:S(2)}) copy-start(f32[1,1152]{1,0:T(1,128)} %param.12) | copy-start | bytes 13828
  36.1 17.4 %copy-start.2 = (bf16[384,1152]{1,0:T(8,128)(2,1)}, bf16[384,1152]{1,0:T(8,128)(2,1)S(1)}, u32[]{:S(2)}) copy-start(bf16[384,1152]{1,0:T(8,128)(2,1)S(1)} %slice_dynamic-update-slice_fusion.2.refs_0_) | copy-start | bytes 2654212
  39.8 16.5 %copy-start = (bf16[384,1152]{1,0:T(8,128)(2,1)}, bf16[384,1152]{1,0:T(8,128)(2,1)S(1)}, u32[]{:S(2)}) copy-start(bf16[384,1152]{1,0:T(8,128)(2,1)S(1)} %slice_dynamic-update-slice_fusion.1.refs_2_) | copy-start | bytes 2654212
  39.9 17.2 %copy-start.1 = (bf16[384,1152]{1,0:T(8,128)(2,1)}, bf16[384,1152]{1,0:T(8,128)(2,1)S(1)}, u32[]{:S(2)}) copy-start(bf16[384,1152]{1,0:T(8,128)(2,1)S(1)} %slice_dynamic-update-slice_fusion.refs_4_) | copy-start | bytes 2654212
  39.9 13.2 %collective-permute-start.16 = (bf16[384,1152]{1,0:T(8,128)(2,1)S(1)}, bf16[384,1152]{1,0:T(8,128)(2,1)}, u32[]{:S(2)}, u32[]{:S(2)}) collective-permute-start(bf16[384,1152]{1,0:T(8,128)(2,1)S(1)} %slice_dynamic-update-slice_fusion.2.refs_0_), channel_id=1, source_target_pairs={{0,2},{1,7},{2,0},{3,5},{4,6},{5,3},{6,4},{7,1},{8,10},{9,15},{10,... | collective-permute-start | bytes 2654216 | tf_op jit(solution)/shard_map/ppermute | solution.py:45
  40.3 13.1 %collective-permute-start.19 = (bf16[384,1152]{1,0:T(8,128)(2,1)S(1)}, bf16[384,1152]{1,0:T(8,128)(2,1)}, u32[]{:S(2)}, u32[]{:S(2)}) collective-permute-start(bf16[384,1152]{1,0:T(8,128)(2,1)S(1)} %slice_dynamic-update-slice_fusion.1.refs_2_), channel_id=1, source_target_pairs={{0,32},{1,97},{2,34},{3,99},{4,36},{5,101},{6,38},{7,103},{8,40},{... | collective-permute-start | bytes 2654216 | tf_op jit(solution)/shard_map/ppermute | solution.py:45
  40.8 15.4 %collective-permute-start.22 = (bf16[384,1152]{1,0:T(8,128)(2,1)S(1)}, bf16[384,1152]{1,0:T(8,128)(2,1)S(1)}, u32[]{:S(2)}, u32[]{:S(2)}) collective-permute-start(bf16[384,1152]{1,0:T(8,128)(2,1)S(1)} %slice_dynamic-update-slice_fusion.refs_4_), channel_id=1, source_target_pairs={{0,8},{1,25},{2,10},{3,27},{4,12},{5,29},{6,14},{7,31},{8,0},{9,17... | collective-permute-start | bytes 2654216 | tf_op jit(solution)/shard_map/ppermute | solution.py:45
  49.5 7.6 %collective-permute-start.13 = (bf16[384,1152]{1,0:T(8,128)(2,1)S(1)}, bf16[384,1152]{1,0:T(8,128)(2,1)S(1)}, u32[]{:S(2)}, u32[]{:S(2)}) collective-permute-start(bf16[384,1152]{1,0:T(8,128)(2,1)S(1)} %slice_dynamic-update-slice_fusion.2.refs_0_), channel_id=1, source_target_pairs={{0,1},{1,0},{2,3},{3,2},{4,5},{5,4},{6,7},{7,6},{8,9},{9,8},{10,11... | collective-permute-start | bytes 2654216 | tf_op jit(solution)/shard_map/ppermute | solution.py:49
  49.5 10.1 %collective-permute-start.14 = (bf16[384,1152]{1,0:T(8,128)(2,1)S(1)}, bf16[384,1152]{1,0:T(8,128)(2,1)S(1)}, u32[]{:S(2)}, u32[]{:S(2)}) collective-permute-start(bf16[384,1152]{1,0:T(8,128)(2,1)S(1)} %slice_dynamic-update-slice_fusion.1.refs_2_), channel_id=1, source_target_pairs={{0,1},{1,0},{2,3},{3,2},{4,5},{5,4},{6,7},{7,6},{8,9},{9,8},{10,11... | collective-permute-start | bytes 2654216 | tf_op jit(solution)/shard_map/ppermute | solution.py:49
  53.1 6.5 %collective-permute-start.15 = (bf16[384,1152]{1,0:T(8,128)(2,1)S(1)}, bf16[384,1152]{1,0:T(8,128)(2,1)S(1)}, u32[]{:S(2)}, u32[]{:S(2)}) collective-permute-start(bf16[384,1152]{1,0:T(8,128)(2,1)S(1)} %slice_dynamic-update-slice_fusion.refs_4_), channel_id=1, source_target_pairs={{0,1},{1,0},{2,3},{3,2},{4,5},{5,4},{6,7},{7,6},{8,9},{9,8},{10,11... | collective-permute-start | bytes 2654216 | tf_op jit(solution)/shard_map/ppermute | solution.py:49
  53.5 16.0 %collective-permute-start.17 = (bf16[384,1152]{1,0:T(8,128)(2,1)S(1)}, bf16[384,1152]{1,0:T(8,128)(2,1)S(1)}, u32[]{:S(2)}, u32[]{:S(2)}) collective-permute-start(bf16[384,1152]{1,0:T(8,128)(2,1)S(1)} %slice_dynamic-update-slice_fusion.2.refs_0_), channel_id=1, source_target_pairs={{0,6},{1,3},{2,4},{3,1},{4,2},{5,7},{6,0},{7,5},{8,14},{9,11},{10,... | collective-permute-start | bytes 2654216 | tf_op jit(solution)/shard_map/ppermute | solution.py:45
  56.2 21.6 %copy-start.3 = (bf16[384,1152]{1,0:T(8,128)(2,1)}, bf16[384,1152]{1,0:T(8,128)(2,1)S(1)}, u32[]{:S(2)}) copy-start(bf16[384,1152]{1,0:T(8,128)(2,1)S(1)} %collective-permute-done.22.refs_4_) | copy-start | bytes 2654212
  56.2 14.3 %collective-permute-start.20 = (bf16[384,1152]{1,0:T(8,128)(2,1)S(1)}, bf16[384,1152]{1,0:T(8,128)(2,1)S(1)}, u32[]{:S(2)}, u32[]{:S(2)}) collective-permute-start(bf16[384,1152]{1,0:T(8,128)(2,1)S(1)} %slice_dynamic-update-slice_fusion.1.refs_2_), channel_id=1, source_target_pairs={{0,96},{1,33},{2,98},{3,35},{4,100},{5,37},{6,102},{7,39},{8,104},... | collective-permute-start | bytes 2654216 | tf_op jit(solution)/shard_map/ppermute | solution.py:45
  57.1 3.5 %copy-start.13 = (bf16[384,1152]{1,0:T(8,128)(2,1)}, bf16[384,1152]{1,0:T(8,128)(2,1)S(1)}, u32[]{:S(2)}) copy-start(bf16[384,1152]{1,0:T(8,128)(2,1)S(1)} %collective-permute-done.13.refs_1_) | copy-start | bytes 2654212
  57.1 14.3 %collective-permute-start.23 = (bf16[384,1152]{1,0:T(8,128)(2,1)S(1)}, bf16[384,1152]{1,0:T(8,128)(2,1)S(1)}, u32[]{:S(2)}, u32[]{:S(2)}) collective-permute-start(bf16[384,1152]{1,0:T(8,128)(2,1)S(1)} %slice_dynamic-update-slice_fusion.refs_4_), channel_id=1, source_target_pairs={{0,24},{1,9},{2,26},{3,11},{4,28},{5,13},{6,30},{7,15},{8,16},{9,1... | collective-permute-start | bytes 2654216 | tf_op jit(solution)/shard_map/ppermute | solution.py:45
  59.6 1.2 copy-start.14
  59.6 0.9 copy-start.15
  68.9 2.7 %collective-permute-start.25 = (bf16[384,1152]{1,0:T(8,128)(2,1)}, bf16[384,1152]{1,0:T(8,128)(2,1)S(1)}, u32[]{:S(2)}, u32[]{:S(2)}) collective-permute-start(bf16[384,1152]{1,0:T(8,128)(2,1)} %collective-permute-done.16.refs_0_), channel_id=1, source_target_pairs={{0,1},{1,0},{2,3},{3,2},{4,5},{5,4},{6,7},{7,6},{8,9},{9,8},{10,11... | collective-permute-start | bytes 2654216 | tf_op jit(solution)/shard_map/ppermute | solution.py:49
  69.0 5.2 %collective-permute-start.26 = (bf16[384,1152]{1,0:T(8,128)(2,1)}, bf16[384,1152]{1,0:T(8,128)(2,1)S(1)}, u32[]{:S(2)}, u32[]{:S(2)}) collective-permute-start(bf16[384,1152]{1,0:T(8,128)(2,1)} %collective-permute-done.19.refs_2_), channel_id=1, source_target_pairs={{0,1},{1,0},{2,3},{3,2},{4,5},{5,4},{6,7},{7,6},{8,9},{9,8},{10,11... | collective-permute-start | bytes 2654216 | tf_op jit(solution)/shard_map/ppermute | solution.py:49
  69.5 9.7 %copy-start.4 = (bf16[384,1152]{1,0:T(8,128)(2,1)}, bf16[384,1152]{1,0:T(8,128)(2,1)S(1)}, u32[]{:S(2)}) copy-start(bf16[384,1152]{1,0:T(8,128)(2,1)S(1)} %collective-permute-done.17.refs_6_) | copy-start | bytes 2654212
  69.5 5.8 %collective-permute-start.27 = (bf16[384,1152]{1,0:T(8,128)(2,1)S(1)}, bf16[384,1152]{1,0:T(8,128)(2,1)S(1)}, u32[]{:S(2)}, u32[]{:S(2)}) collective-permute-start(bf16[384,1152]{1,0:T(8,128)(2,1)S(1)} %collective-permute-done.22.refs_4_), channel_id=1, source_target_pairs={{0,1},{1,0},{2,3},{3,2},{4,5},{5,4},{6,7},{7,6},{8,9},{9,8},{10,11... | collective-permute-start | bytes 2654216 | tf_op jit(solution)/shard_map/ppermute | solution.py:49
  70.6 8.6 %copy-start.5 = (bf16[384,1152]{1,0:T(8,128)(2,1)}, bf16[384,1152]{1,0:T(8,128)(2,1)S(1)}, u32[]{:S(2)}) copy-start(bf16[384,1152]{1,0:T(8,128)(2,1)S(1)} %collective-permute-done.20.refs_8_) | copy-start | bytes 2654212
  70.6 7.3 %collective-permute-start.18 = (bf16[384,1152]{1,0:T(8,128)(2,1)S(1)}, bf16[384,1152]{1,0:T(8,128)(2,1)S(1)}, u32[]{:S(2)}, u32[]{:S(2)}) collective-permute-start(bf16[384,1152]{1,0:T(8,128)(2,1)S(1)} %collective-permute-done.17.refs_6_), channel_id=1, source_target_pairs={{0,1},{1,0},{2,3},{3,2},{4,5},{5,4},{6,7},{7,6},{8,9},{9,8},{10,11... | collective-permute-start | bytes 2654216 | tf_op jit(solution)/shard_map/ppermute | solution.py:49
  71.4 7.8 %copy-start.6 = (bf16[384,1152]{1,0:T(8,128)(2,1)}, bf16[384,1152]{1,0:T(8,128)(2,1)S(1)}, u32[]{:S(2)}) copy-start(bf16[384,1152]{1,0:T(8,128)(2,1)S(1)} %collective-permute-done.23.refs_10_) | copy-start | bytes 2654212
  71.4 6.8 %collective-permute-start.21 = (bf16[384,1152]{1,0:T(8,128)(2,1)S(1)}, bf16[384,1152]{1,0:T(8,128)(2,1)S(1)}, u32[]{:S(2)}, u32[]{:S(2)}) collective-permute-start(bf16[384,1152]{1,0:T(8,128)(2,1)S(1)} %collective-permute-done.20.refs_8_), channel_id=1, source_target_pairs={{0,1},{1,0},{2,3},{3,2},{4,5},{5,4},{6,7},{7,6},{8,9},{9,8},{10,11... | collective-permute-start | bytes 2654216 | tf_op jit(solution)/shard_map/ppermute | solution.py:49
  71.6 7.6 %copy-start.7 = (bf16[384,1152]{1,0:T(8,128)(2,1)}, bf16[384,1152]{1,0:T(8,128)(2,1)S(1)}, u32[]{:S(2)}) copy-start(bf16[384,1152]{1,0:T(8,128)(2,1)S(1)} %collective-permute-done.25.refs_7_) | copy-start | bytes 2654212
  71.6 6.7 %collective-permute-start.24 = (bf16[384,1152]{1,0:T(8,128)(2,1)S(1)}, bf16[384,1152]{1,0:T(8,128)(2,1)S(1)}, u32[]{:S(2)}, u32[]{:S(2)}) collective-permute-start(bf16[384,1152]{1,0:T(8,128)(2,1)S(1)} %collective-permute-done.23.refs_10_), channel_id=1, source_target_pairs={{0,1},{1,0},{2,3},{3,2},{4,5},{5,4},{6,7},{7,6},{8,9},{9,8},{10,11... | collective-permute-start | bytes 2654216 | tf_op jit(solution)/shard_map/ppermute | solution.py:49
  74.1 5.1 %copy-start.8 = (bf16[384,1152]{1,0:T(8,128)(2,1)}, bf16[384,1152]{1,0:T(8,128)(2,1)S(1)}, u32[]{:S(2)}) copy-start(bf16[384,1152]{1,0:T(8,128)(2,1)S(1)} %collective-permute-done.26.refs_9_) | copy-start | bytes 2654212
  74.1 16.1 %collective-permute-start.28 = (bf16[384,1152]{1,0:T(8,128)(2,1)}, bf16[384,1152]{1,0:T(8,128)(2,1)}, u32[]{:S(2)}, u32[]{:S(2)}) collective-permute-start(bf16[384,1152]{1,0:T(8,128)(2,1)} %collective-permute-done.16.refs_0_), channel_id=1, source_target_pairs={{0,6},{1,3},{2,4},{3,1},{4,2},{5,7},{6,0},{7,5},{8,14},{9,11},{10,... | collective-permute-start | bytes 2654216 | tf_op jit(solution)/shard_map/ppermute | solution.py:45
  75.3 3.9 %copy-start.9 = (bf16[384,1152]{1,0:T(8,128)(2,1)}, bf16[384,1152]{1,0:T(8,128)(2,1)S(1)}, u32[]{:S(2)}) copy-start(bf16[384,1152]{1,0:T(8,128)(2,1)S(1)} %collective-permute-done.27.refs_11_) | copy-start | bytes 2654212
  75.3 15.0 %collective-permute-start.30 = (bf16[384,1152]{1,0:T(8,128)(2,1)}, bf16[384,1152]{1,0:T(8,128)(2,1)}, u32[]{:S(2)}, u32[]{:S(2)}) collective-permute-start(bf16[384,1152]{1,0:T(8,128)(2,1)} %collective-permute-done.19.refs_2_), channel_id=1, source_target_pairs={{0,96},{1,33},{2,98},{3,35},{4,100},{5,37},{6,102},{7,39},{8,104},... | collective-permute-start | bytes 2654216 | tf_op jit(solution)/shard_map/ppermute | solution.py:45
  77.9 1.4 copy-start.10
  77.9 14.4 %collective-permute-start.32 = (bf16[384,1152]{1,0:T(8,128)(2,1)S(1)}, bf16[384,1152]{1,0:T(8,128)(2,1)}, u32[]{:S(2)}, u32[]{:S(2)}) collective-permute-start(bf16[384,1152]{1,0:T(8,128)(2,1)S(1)} %collective-permute-done.22.refs_4_), channel_id=1, source_target_pairs={{0,24},{1,9},{2,26},{3,11},{4,28},{5,13},{6,30},{7,15},{8,16},{9,1... | collective-permute-start | bytes 2654216 | tf_op jit(solution)/shard_map/ppermute | solution.py:45
  78.2 1.3 copy-start.11
  78.2 0.9 copy-start.12
  90.2 2.7 %collective-permute-start.29 = (bf16[384,1152]{1,0:T(8,128)(2,1)}, bf16[384,1152]{1,0:T(8,128)(2,1)S(1)}, u32[]{:S(2)}, u32[]{:S(2)}) collective-permute-start(bf16[384,1152]{1,0:T(8,128)(2,1)} %collective-permute-done.28.refs_0_), channel_id=1, source_target_pairs={{0,1},{1,0},{2,3},{3,2},{4,5},{5,4},{6,7},{7,6},{8,9},{9,8},{10,11... | collective-permute-start | bytes 2654216 | tf_op jit(solution)/shard_map/ppermute | solution.py:49
  90.3 3.9 %collective-permute-start.31 = (bf16[384,1152]{1,0:T(8,128)(2,1)}, bf16[384,1152]{1,0:T(8,128)(2,1)S(1)}, u32[]{:S(2)}, u32[]{:S(2)}) collective-permute-start(bf16[384,1152]{1,0:T(8,128)(2,1)} %collective-permute-done.30.refs_2_), channel_id=1, source_target_pairs={{0,1},{1,0},{2,3},{3,2},{4,5},{5,4},{6,7},{7,6},{8,9},{9,8},{10,11... | collective-permute-start | bytes 2654216 | tf_op jit(solution)/shard_map/ppermute | solution.py:49
  92.3 3.1 %collective-permute-start.33 = (bf16[384,1152]{1,0:T(8,128)(2,1)}, bf16[384,1152]{1,0:T(8,128)(2,1)S(1)}, u32[]{:S(2)}, u32[]{:S(2)}) collective-permute-start(bf16[384,1152]{1,0:T(8,128)(2,1)} %collective-permute-done.32.refs_4_), channel_id=1, source_target_pairs={{0,1},{1,0},{2,3},{3,2},{4,5},{5,4},{6,7},{7,6},{8,9},{9,8},{10,11... | collective-permute-start | bytes 2654216 | tf_op jit(solution)/shard_map/ppermute | solution.py:49
  92.9 2.5 %copy-start.16 = (bf16[384,1152]{1,0:T(8,128)(2,1)}, bf16[384,1152]{1,0:T(8,128)(2,1)S(1)}, u32[]{:S(2)}) copy-start(bf16[384,1152]{1,0:T(8,128)(2,1)S(1)} %collective-permute-done.29.refs_1_) | copy-start | bytes 2654212
  94.2 1.3 copy-start.17
  95.4 0.9 copy-start.18

commit v5 on v4

--- a/solution.py
+++ b/solution.py
@@ -168,11 +168,14 @@
     return pl.ds(pl.multiple_of(place * rows, rows), rows)
 
 
-def own_kernel(count, core_ref, state_ref, mod_ref, *refs):
+def own_kernel(count, core_ref, state_in, mod_in, *refs):
     sets = as_sets(refs[:count])
     hidden_ref, acc_ref, *weights = refs[count:]
-    kept, weights = weights[:2], weights[2:]
+    kept, (state_ref, mod_ref, own_sems), weights = weights[:2], weights[2:5], weights[5:]
+    own = fetch([(state_in, state_ref), (mod_in, mod_ref)], own_sems)
     start_set(core_ref, sets[0], *weights[:3], 0)
+    for copy in own:
+        copy.wait()
     tokens, width = state_ref.shape
 
     def one(place, carry):
@@ -194,9 +197,14 @@
         functools.partial(own_kernel, len(weights)),
         out_shape=[jax.ShapeDtypeStruct((tokens, width), bf16), jax.ShapeDtypeStruct((tokens, width), f32)]
         + kept_shapes(units, width, 1),
-        in_specs=[SMEM, VMEM, VMEM] + [ANY] * len(weights),
+        in_specs=[SMEM, ANY, ANY] + [ANY] * len(weights),
         out_specs=[VMEM, VMEM, HBM, HBM],
-        scratch_shapes=weight_scratch(units, width, 1),
+        scratch_shapes=[
+            pltpu.VMEM(state.shape, f32),
+            pltpu.VMEM(mod.shape, f32),
+            pltpu.SemaphoreType.DMA((2,)),
+        ]
+        + weight_scratch(units, width, 1),
         compiler_params=room(56),
         name="own_piece",
     )(core, state, mod, *weights)

time: 160 us -> 161 us (level)
    ppermute x21, waiting for transfers between devices: 18.4 us -> 16.6 us  [send(): return lax.ppermute(rows, ALL, neighbour(axis, first))]
  transfers between devices with their start and end apart: 34 -> 34, of which waited for: 15 -> 13; matrix products, arithmetic and copies ran while one was open for 7% -> 7% of each run, Pallas kernels for 12% -> 13%
where the time goes in v5:
time: 161 us
  Pallas kernels  42.3 us (26%)
  blocking collectives  40 us (25%)
  starting transfers between devices  34.6 us (21%)
  waiting for transfers between devices  23.4 us (15%)
  other arithmetic  7.63 us (5%)
  local copies, waits for them, and re-layouts  6.28 us (4%)
  matrix products  5.2 us (3%)
    ppermute x21, starting transfers between devices, send(): return lax.ppermute(rows, ALL, neighbour(axis, first))  31.9 us
    all_to_all x1, blocking collectives, per_device(): got = lax.all_to_all(sent, 'tm', 0, 0, tiled=True)  24.7 us
    ppermute x21, waiting for transfers between devices, send(): return lax.ppermute(rows, ALL, neighbour(axis, first))  16.6 us
    all_to_all x1, blocking collectives, per_device(): final = lax.all_to_all(updated, 'tm', 0, 0, tiled=True)  15.3 us
    pallas_call x1, Pallas kernels, second_sweep(): pl.pallas_call(functools.partial(second_kernel, len(weights)), out_shape=...  14 us
    pallas_call x1, Pallas kernels, next_piece(): pl.pallas_call(functools.partial(next_kernel, len(weights)), out_shape=[j...  10.6 us
    pallas_call x1, Pallas kernels, own_piece(): pl.pallas_call(functools.partial(own_kernel, len(weights)), out_shape=[ja...  9.58 us
    pallas_call x1, Pallas kernels, far_piece(): pl.pallas_call(functools.partial(far_kernel, len(weights)), out_shape=[ja...  7.99 us
  transfers between devices with their start and end apart: 34, of which 13 were waited for; matrix products, arithmetic and copies ran while one was open for 7% of the time, Pallas kernels for 13%

profile of v5, /device:TPU:0, one launch (start us, length us, event | category | flops | bytes accessed | tf_op | source)
XLA Modules:
  0.0 161.0 jit_solution(3879844963892516740)
XLA Ops:
  0.0 0.9 broadcast_select_fusion
  2.3 1.0 maximum_select_fusion
  3.3 0.7 fusion.5
  4.0 1.6 collective-permute-start.1
  5.6 1.6 collective-permute-start.9
  7.2 1.9 %collective-permute-start.5 = (bf16[24,1152]{1,0:T(8,128)(2,1)S(1)}, bf16[24,1152]{1,0:T(8,128)(2,1)S(1)}, u32[]{:S(2)}, u32[]{:S(2)}) collective-permute-start(bf16[24,1152]{1,0:T(8,128)(2,1)S(1)} %get-tuple-element.84), channel_id=1, source_target_pairs={{0,8},{1,25},{2,10},{3,27},{4,12},{5,29},{6,14},{7,31},{8,0},{9,17... | collective-permute-start | bytes 165896 | tf_op jit(solution)/shard_map/ppermute | solution.py:45
  9.1 2.2 %collective-permute-start.2 = (bf16[48,1152]{1,0:T(8,128)(2,1)S(1)}, bf16[48,1152]{1,0:T(8,128)(2,1)S(1)}, u32[]{:S(2)}, u32[]{:S(2)}) collective-permute-start(bf16[48,1152]{1,0:T(8,128)(2,1)S(1)} %pad_maximum_fusion.3), channel_id=1, source_target_pairs={{0,96},{1,33},{2,98},{3,35},{4,100},{5,37},{6,102},{7,39},{8,104},... | collective-permute-start | bytes 331784 | tf_op jit(solution)/shard_map/ppermute | solution.py:45
  11.3 2.9 %collective-permute-start.10 = (bf16[48,1152]{1,0:T(8,128)(2,1)S(1)}, bf16[48,1152]{1,0:T(8,128)(2,1)S(1)}, u32[]{:S(2)}, u32[]{:S(2)}) collective-permute-start(bf16[48,1152]{1,0:T(8,128)(2,1)S(1)} %pad_maximum_fusion.5), channel_id=1, source_target_pairs={{0,6},{1,3},{2,4},{3,1},{4,2},{5,7},{6,0},{7,5},{8,14},{9,11},{10,... | collective-permute-start | bytes 331784 | tf_op jit(solution)/shard_map/ppermute | solution.py:45
  14.2 4.1 %collective-permute-start.6 = (bf16[48,1152]{1,0:T(8,128)(2,1)S(1)}, bf16[48,1152]{1,0:T(8,128)(2,1)S(1)}, u32[]{:S(2)}, u32[]{:S(2)}) collective-permute-start(bf16[48,1152]{1,0:T(8,128)(2,1)S(1)} %pad_maximum_fusion.4), channel_id=1, source_target_pairs={{0,24},{1,9},{2,26},{3,11},{4,28},{5,13},{6,30},{7,15},{8,16},{9,1... | collective-permute-start | bytes 331784 | tf_op jit(solution)/shard_map/ppermute | solution.py:45
  18.4 0.6 constant_dynamic-update-slice_fusion.3
  19.0 0.6 constant_dynamic-update-slice_fusion.2
  19.7 0.6 constant_dynamic-update-slice_fusion.1
  20.4 0.6 constant_dynamic-update-slice_fusion.21
  21.1 0.6 constant_dynamic-update-slice_fusion.20
  21.7 0.6 constant_dynamic-update-slice_fusion.19
  22.4 0.3 collective-permute-start.11
  22.8 0.2 collective-permute-start.7
  23.1 3.3 %collective-permute-done.3 = bf16[96,1152]{1,0:T(8,128)(2,1)S(1)} collective-permute-done((bf16[96,1152]{1,0:T(8,128)(2,1)S(1)}, bf16[96,1152]{1,0:T(8,128)(2,1)S(1)}, u32[]{:S(2)}, u32[]{:S(2)}) %collective-permute-start.3) | collective-permute-done | bytes 221216 | tf_op jit(solution)/shard_map/ppermute | solution.py:45
  26.5 1.9 %collective-permute-done.11 = bf16[96,1152]{1,0:T(8,128)(2,1)S(1)} collective-permute-done((bf16[96,1152]{1,0:T(8,128)(2,1)S(1)}, bf16[96,1152]{1,0:T(8,128)(2,1)S(1)}, u32[]{:S(2)}, u32[]{:S(2)}) %collective-permute-start.11) | collective-permute-done | bytes 221216 | tf_op jit(solution)/shard_map/ppermute | solution.py:45
  28.4 0.7 constant_dynamic-update-slice_fusion.18
  29.1 0.8 collective-permute-start.12
  29.9 3.1 %collective-permute-start.8 = (bf16[192,1152]{1,0:T(8,128)(2,1)S(1)}, bf16[192,1152]{1,0:T(8,128)(2,1)S(1)}, u32[]{:S(2)}, u32[]{:S(2)}) collective-permute-start(bf16[192,1152]{1,0:T(8,128)(2,1)S(1)} %constant_dynamic-update-slice_fusion.9), channel_id=1, source_target_pairs={{0,6},{1,3},{2,4},{3,1},{4,2},{5,7},{6,0},{7,5},{8,14},{9,11},{10,... | collective-permute-start | bytes 1327112 | tf_op jit(solution)/shard_map/ppermute | solution.py:45
  33.0 2.9 %collective-permute-done.4 = bf16[192,1152]{1,0:T(8,128)(2,1)S(1)} collective-permute-done((bf16[192,1152]{1,0:T(8,128)(2,1)S(1)}, bf16[192,1152]{1,0:T(8,128)(2,1)S(1)}, u32[]{:S(2)}, u32[]{:S(2)}) %collective-permute-start.4) | collective-permute-done | bytes 442400 | tf_op jit(solution)/shard_map/ppermute | solution.py:45
  36.1 2.7 %collective-permute-done.12 = bf16[192,1152]{1,0:T(8,128)(2,1)S(1)} collective-permute-done((bf16[192,1152]{1,0:T(8,128)(2,1)}, bf16[192,1152]{1,0:T(8,128)(2,1)S(1)}, u32[]{:S(2)}, u32[]{:S(2)}) %collective-permute-start.12) | collective-permute-done | bytes 442400 | tf_op jit(solution)/shard_map/ppermute | solution.py:45
  38.9 0.7 collective-permute-done.8
  39.5 0.1 select_dynamic-update-slice_fusion.1
  39.9 0.4 collective-permute-start.16
  40.3 0.5 collective-permute-start.19
  40.8 2.0 %collective-permute-start.22 = (bf16[384,1152]{1,0:T(8,128)(2,1)S(1)}, bf16[384,1152]{1,0:T(8,128)(2,1)S(1)}, u32[]{:S(2)}, u32[]{:S(2)}) collective-permute-start(bf16[384,1152]{1,0:T(8,128)(2,1)S(1)} %slice_dynamic-update-slice_fusion.refs_4_), channel_id=1, source_target_pairs={{0,8},{1,25},{2,10},{3,27},{4,12},{5,29},{6,14},{7,31},{8,0},{9,17... | collective-permute-start | bytes 2654216 | tf_op jit(solution)/shard_map/ppermute | solution.py:45
  42.8 0.5 pad_convert_fusion
  43.4 1.0 multiply_cosine_fusion
  44.3 5.2 %fusion.mod_in.mod_ref = f32[24,3456]{1,0:T(8,128)} fusion(bf16[1152,3456]{1,0:T(8,128)(2,1)} %param.17, f32[24,576]{1,0:T(8,128)S(1)} %get-tuple-element.96, f32[24,576]{1,0:T(8,128)S(1)} %get-tuple-element.95, f32[1152]{0:T(1024)S(1)} %reduce), kind=kOutput, calls=%fused_computation.48 | convolution fusion | flops 191296512 | bytes 8409600 | tf_op jit(solution)/shard_map/dot_general | solution.py:408
  49.5 0.5 collective-permute-start.14
  50.0 3.1 %collective-permute-done.16.refs_0_ = bf16[384,1152]{1,0:T(8,128)(2,1)} collective-permute-done((bf16[384,1152]{1,0:T(8,128)(2,1)S(1)}, bf16[384,1152]{1,0:T(8,128)(2,1)}, u32[]{:S(2)}, u32[]{:S(2)}) %collective-permute-start.16) | collective-permute-done | bytes 884768 | tf_op jit(solution)/shard_map/ppermute | solution.py:45
  53.1 0.4 collective-permute-done.19.refs_2_
  53.5 2.7 %collective-permute-start.17 = (bf16[384,1152]{1,0:T(8,128)(2,1)S(1)}, bf16[384,1152]{1,0:T(8,128)(2,1)S(1)}, u32[]{:S(2)}, u32[]{:S(2)}) collective-permute-start(bf16[384,1152]{1,0:T(8,128)(2,1)S(1)} %slice_dynamic-update-slice_fusion.2.refs_0_), channel_id=1, source_target_pairs={{0,6},{1,3},{2,4},{3,1},{4,2},{5,7},{6,0},{7,5},{8,14},{9,11},{10,... | collective-permute-start | bytes 2654216 | tf_op jit(solution)/shard_map/ppermute | solution.py:45
  56.2 0.8 collective-permute-start.20
  57.1 2.5 %collective-permute-start.23 = (bf16[384,1152]{1,0:T(8,128)(2,1)S(1)}, bf16[384,1152]{1,0:T(8,128)(2,1)S(1)}, u32[]{:S(2)}, u32[]{:S(2)}) collective-permute-start(bf16[384,1152]{1,0:T(8,128)(2,1)S(1)} %slice_dynamic-update-slice_fusion.refs_4_), channel_id=1, source_target_pairs={{0,24},{1,9},{2,26},{3,11},{4,28},{5,13},{6,30},{7,15},{8,16},{9,1... | collective-permute-start | bytes 2654216 | tf_op jit(solution)/shard_map/ppermute | solution.py:45
  59.7 0.9 copy-done.15
  60.6 0.3 copy-done.14
  60.9 9.6 %own_piece.1 = (bf16[256,1152]{1,0:T(8,128)(2,1)}, f32[256,1152]{1,0:T(8,128)}, bf16[1152,1152]{1,0:T(8,128)(2,1)}, bf16[1152,1152]{1,0:T(8,128)(2,1)}) custom-call(s32[1]{0:T(128)} %bitcast.core_ref, f32[256,1152]{1,0:T(8,128)} %bitcast.13, f32[24,3456]{1,0:T(8,128)} %fusion.mod_in.mod_ref, bf16[384,1152]{1,0:T(8,128)(2,1)} %copy-done.2, ...), custom_call_target="tpu_custom_call" | custom-call | tf_op jit(solution)/shard_map/own_piece/pallas_call | solution.py:196
  70.5 0.5 collective-permute-start.26
  71.1 0.4 collective-permute-start.18
  71.6 0.3 collective-permute-start.21
  71.8 1.3 collective-permute-done.25.refs_7_
  73.2 0.1 collective-permute-start.24
  73.3 2.4 %collective-permute-done.26.refs_9_ = bf16[384,1152]{1,0:T(8,128)(2,1)S(1)} collective-permute-done((bf16[384,1152]{1,0:T(8,128)(2,1)}, bf16[384,1152]{1,0:T(8,128)(2,1)S(1)}, u32[]{:S(2)}, u32[]{:S(2)}) %collective-permute-start.26) | collective-permute-done | bytes 884768 | tf_op jit(solution)/shard_map/ppermute | solution.py:49
  75.7 1.2 collective-permute-start.28
  76.9 2.5 %collective-permute-start.30 = (bf16[384,1152]{1,0:T(8,128)(2,1)}, bf16[384,1152]{1,0:T(8,128)(2,1)}, u32[]{:S(2)}, u32[]{:S(2)}) collective-permute-start(bf16[384,1152]{1,0:T(8,128)(2,1)} %collective-permute-done.19.refs_2_), channel_id=1, source_target_pairs={{0,96},{1,33},{2,98},{3,35},{4,100},{5,37},{6,102},{7,39},{8,104},... | collective-permute-start | bytes 2654216 | tf_op jit(solution)/shard_map/ppermute | solution.py:45
  79.4 0.3 collective-permute-start.32
  79.8 0.9 copy-done.12
  80.7 0.3 copy-done.11
  81.0 10.6 %next_piece.1 = (f32[256,1152]{1,0:T(8,128)}, bf16[1152,1152]{1,0:T(8,128)(2,1)}, bf16[1152,1152]{1,0:T(8,128)(2,1)}, bf16[1152,1152]{1,0:T(8,128)(2,1)}, bf16[1152,1152]{1,0:T(8,128)(2,1)}) custom-call(s32[1]{0:T(128)} %bitcast.core_ref, bf16[256,1152]{1,0:T(8,128)(2,1)} %get-tuple-element.41.hidden_in, f32[256,1152]{1,0:T(8,128)} %get-tuple-element.42.acc_in, ...), custom_call_target="tpu_custom_call" | custom-call | tf_op jit(solution)/shard_map/next_piece/pallas_call | solution.py:234
  91.8 0.5 collective-permute-start.31
  92.3 1.6 collective-permute-done.32.refs_4_
  93.9 0.5 collective-permute-done.29.refs_1_
  94.4 1.3 collective-permute-done.31.refs_3_
  95.7 1.3 collective-permute-done.33.refs_5_
  96.9 0.9 copy-done.18
  97.8 8.0 %far_piece.1 = (bf16[16,32,1152]{2,1,0:T(8,128)(2,1)}, bf16[1152,1152]{1,0:T(8,128)(2,1)}, bf16[1152,1152]{1,0:T(8,128)(2,1)}) custom-call(s32[1]{0:T(128)} %bitcast.core_ref, f32[1]{0:T(128)} %bitcast.1.first_ref, s32[1]{0:T(128)} %bitcast.3.begin_ref, f32[1000]{0:T(1024)} %dt_ref.3, f32[1000]{0:T(1024)} %sigma_ref.3, ...), custom_call_target="tpu_custom_call" | custom-call | tf_op jit(solution)/shard_map/far_piece/pallas_call | solution.py:284
  105.8 24.7 %all_to_all.10.got_ref = bf16[16,32,1152]{2,1,0:T(8,128)(2,1)} all-to-all(bf16[16,32,1152]{2,1,0:T(8,128)(2,1)} %get-tuple-element.56), channel_id=1, replica_groups=mesh['tm'=16,'batch'=8] {'tm'}, dimensions={0} | all-to-all | bytes 2359296 | tf_op jit(solution)/shard_map/all_to_all | solution.py:432
  130.5 14.0 %second_sweep.1 = bf16[16,16,1152]{2,1,0:T(8,128)(2,1)} custom-call(s32[1]{0:T(128)} %copy.41.begin_ref, s32[1]{0:T(128)} %copy.42.advance_ref, f32[1000]{0:T(1024)} %dt_ref.3, f32[1000]{0:T(1024)} %sigma_ref.3, bf16[16,32,1152]{2,1,0:T(8,128)(2,1)} %all_to_all.10.got_ref, f32[24,3456]{1,0:T(8,128)} %fusion.mod_in.mod_ref, ...), custom_call_target="tpu_custom_call" | custom-call | tf_op jit(solution)/shard_map/second_sweep/pallas_call | solution.py:358
  144.5 15.3 %all_to_all.11 = bf16[16,16,1152]{2,1,0:T(8,128)(2,1)S(1)} all-to-all(bf16[16,16,1152]{2,1,0:T(8,128)(2,1)} %second_sweep.1), channel_id=1, replica_groups=mesh['tm'=16,'batch'=8] {'tm'}, dimensions={0} | all-to-all | bytes 1179648 | tf_op jit(solution)/shard_map/all_to_all | solution.py:442
  159.9 1.1 convert.2
  (94 shorter events, 1.3 us)
Async XLA Ops:
  0.9 1.4 collective-permute-start
  4.0 5.1 %collective-permute-start.1 = (bf16[24,1152]{1,0:T(8,128)(2,1)S(1)}, bf16[24,1152]{1,0:T(8,128)(2,1)S(1)}, u32[]{:S(2)}, u32[]{:S(2)}) collective-permute-start(bf16[24,1152]{1,0:T(8,128)(2,1)S(1)} %get-tuple-element.85), channel_id=1, source_target_pairs={{0,32},{1,97},{2,34},{3,99},{4,36},{5,101},{6,38},{7,103},{8,40},{... | collective-permute-start | bytes 165896 | tf_op jit(solution)/shard_map/ppermute | solution.py:45
  5.6 5.7 %collective-permute-start.9 = (bf16[24,1152]{1,0:T(8,128)(2,1)S(1)}, bf16[24,1152]{1,0:T(8,128)(2,1)S(1)}, u32[]{:S(2)}, u32[]{:S(2)}) collective-permute-start(bf16[24,1152]{1,0:T(8,128)(2,1)S(1)} %get-tuple-element.77), channel_id=1, source_target_pairs={{0,2},{1,7},{2,0},{3,5},{4,6},{5,3},{6,4},{7,1},{8,10},{9,15},{10,... | collective-permute-start | bytes 165896 | tf_op jit(solution)/shard_map/ppermute | solution.py:45
  7.2 7.0 %collective-permute-start.5 = (bf16[24,1152]{1,0:T(8,128)(2,1)S(1)}, bf16[24,1152]{1,0:T(8,128)(2,1)S(1)}, u32[]{:S(2)}, u32[]{:S(2)}) collective-permute-start(bf16[24,1152]{1,0:T(8,128)(2,1)S(1)} %get-tuple-element.84), channel_id=1, source_target_pairs={{0,8},{1,25},{2,10},{3,27},{4,12},{5,29},{6,14},{7,31},{8,0},{9,17... | collective-permute-start | bytes 165896 | tf_op jit(solution)/shard_map/ppermute | solution.py:45
  9.1 9.2 %collective-permute-start.2 = (bf16[48,1152]{1,0:T(8,128)(2,1)S(1)}, bf16[48,1152]{1,0:T(8,128)(2,1)S(1)}, u32[]{:S(2)}, u32[]{:S(2)}) collective-permute-start(bf16[48,1152]{1,0:T(8,128)(2,1)S(1)} %pad_maximum_fusion.3), channel_id=1, source_target_pairs={{0,96},{1,33},{2,98},{3,35},{4,100},{5,37},{6,102},{7,39},{8,104},... | collective-permute-start | bytes 331784 | tf_op jit(solution)/shard_map/ppermute | solution.py:45
  11.3 9.1 %collective-permute-start.10 = (bf16[48,1152]{1,0:T(8,128)(2,1)S(1)}, bf16[48,1152]{1,0:T(8,128)(2,1)S(1)}, u32[]{:S(2)}, u32[]{:S(2)}) collective-permute-start(bf16[48,1152]{1,0:T(8,128)(2,1)S(1)} %pad_maximum_fusion.5), channel_id=1, source_target_pairs={{0,6},{1,3},{2,4},{3,1},{4,2},{5,7},{6,0},{7,5},{8,14},{9,11},{10,... | collective-permute-start | bytes 331784 | tf_op jit(solution)/shard_map/ppermute | solution.py:45
  14.2 8.5 %collective-permute-start.6 = (bf16[48,1152]{1,0:T(8,128)(2,1)S(1)}, bf16[48,1152]{1,0:T(8,128)(2,1)S(1)}, u32[]{:S(2)}, u32[]{:S(2)}) collective-permute-start(bf16[48,1152]{1,0:T(8,128)(2,1)S(1)} %pad_maximum_fusion.4), channel_id=1, source_target_pairs={{0,24},{1,9},{2,26},{3,11},{4,28},{5,13},{6,30},{7,15},{8,16},{9,1... | collective-permute-start | bytes 331784 | tf_op jit(solution)/shard_map/ppermute | solution.py:45
  20.3 6.0 %copy-start.19 = (bf16[192,1152]{1,0:T(8,128)(2,1)S(1)}, bf16[192,1152]{1,0:T(8,128)(2,1)}, u32[]{:S(2)}) copy-start(bf16[192,1152]{1,0:T(8,128)(2,1)} %get-tuple-element.92) | copy-start | bytes 1327108
  20.3 6.0 %collective-permute-start.3 = (bf16[96,1152]{1,0:T(8,128)(2,1)S(1)}, bf16[96,1152]{1,0:T(8,128)(2,1)S(1)}, u32[]{:S(2)}, u32[]{:S(2)}) collective-permute-start(bf16[96,1152]{1,0:T(8,128)(2,1)S(1)} %pad_maximum_fusion), channel_id=1, source_target_pairs={{0,8},{1,25},{2,10},{3,27},{4,12},{5,29},{6,14},{7,31},{8,0},{9,17... | collective-permute-start | bytes 663560 | tf_op jit(solution)/shard_map/ppermute | solution.py:45
  22.4 6.0 %collective-permute-start.11 = (bf16[96,1152]{1,0:T(8,128)(2,1)S(1)}, bf16[96,1152]{1,0:T(8,128)(2,1)S(1)}, u32[]{:S(2)}, u32[]{:S(2)}) collective-permute-start(bf16[96,1152]{1,0:T(8,128)(2,1)S(1)} %pad_maximum_fusion.2), channel_id=1, source_target_pairs={{0,32},{1,97},{2,34},{3,99},{4,36},{5,101},{6,38},{7,103},{8,40},{... | collective-permute-start | bytes 663560 | tf_op jit(solution)/shard_map/ppermute | solution.py:45
  22.8 7.1 %collective-permute-start.7 = (bf16[96,1152]{1,0:T(8,128)(2,1)S(1)}, bf16[96,1152]{1,0:T(8,128)(2,1)S(1)}, u32[]{:S(2)}, u32[]{:S(2)}) collective-permute-start(bf16[96,1152]{1,0:T(8,128)(2,1)S(1)} %pad_maximum_fusion.1), channel_id=1, source_target_pairs={{0,2},{1,7},{2,0},{3,5},{4,6},{5,3},{6,4},{7,1},{8,10},{9,15},{10,... | collective-permute-start | bytes 663560 | tf_op jit(solution)/shard_map/ppermute | solution.py:45
  26.4 9.6 %collective-permute-start.4 = (bf16[192,1152]{1,0:T(8,128)(2,1)S(1)}, bf16[192,1152]{1,0:T(8,128)(2,1)S(1)}, u32[]{:S(2)}, u32[]{:S(2)}) collective-permute-start(bf16[192,1152]{1,0:T(8,128)(2,1)S(1)} %constant_dynamic-update-slice_fusion), channel_id=1, source_target_pairs={{0,24},{1,9},{2,26},{3,11},{4,28},{5,13},{6,30},{7,15},{8,16},{9,1... | collective-permute-start | bytes 1327112 | tf_op jit(solution)/shard_map/ppermute | solution.py:45
  29.1 9.7 %collective-permute-start.12 = (bf16[192,1152]{1,0:T(8,128)(2,1)}, bf16[192,1152]{1,0:T(8,128)(2,1)S(1)}, u32[]{:S(2)}, u32[]{:S(2)}) collective-permute-start(bf16[192,1152]{1,0:T(8,128)(2,1)} %constant_dynamic-update-slice_fusion.18), channel_id=1, source_target_pairs={{0,96},{1,33},{2,98},{3,35},{4,100},{5,37},{6,102},{7,39},{8,104},... | collective-permute-start | bytes 1327112 | tf_op jit(solution)/shard_map/ppermute | solution.py:45
  29.9 9.6 %collective-permute-start.8 = (bf16[192,1152]{1,0:T(8,128)(2,1)S(1)}, bf16[192,1152]{1,0:T(8,128)(2,1)S(1)}, u32[]{:S(2)}, u32[]{:S(2)}) collective-permute-start(bf16[192,1152]{1,0:T(8,128)(2,1)S(1)} %constant_dynamic-update-slice_fusion.9), channel_id=1, source_target_pairs={{0,6},{1,3},{2,4},{3,1},{4,2},{5,7},{6,0},{7,5},{8,14},{9,11},{10,... | collective-permute-start | bytes 1327112 | tf_op jit(solution)/shard_map/ppermute | solution.py:45
  36.0 7.4 %copy-start.20 = (f32[1,1152]{1,0:T(1,128)S(1)}, f32[1,1152]{1,0:T(1,128)}, u32[]{:S(2)}) copy-start(f32[1,1152]{1,0:T(1,128)} %param.12) | copy-start | bytes 13828
  36.1 17.4 %copy-start.2 = (bf16[384,1152]{1,0:T(8,128)(2,1)}, bf16[384,1152]{1,0:T(8,128)(2,1)S(1)}, u32[]{:S(2)}) copy-start(bf16[384,1152]{1,0:T(8,128)(2,1)S(1)} %slice_dynamic-update-slice_fusion.2.refs_0_) | copy-start | bytes 2654212
  39.8 16.5 %copy-start = (bf16[384,1152]{1,0:T(8,128)(2,1)}, bf16[384,1152]{1,0:T(8,128)(2,1)S(1)}, u32[]{:S(2)}) copy-start(bf16[384,1152]{1,0:T(8,128)(2,1)S(1)} %slice_dynamic-update-slice_fusion.1.refs_2_) | copy-start | bytes 2654212
  39.9 17.2 %copy-start.1 = (bf16[384,1152]{1,0:T(8,128)(2,1)}, bf16[384,1152]{1,0:T(8,128)(2,1)S(1)}, u32[]{:S(2)}) copy-start(bf16[384,1152]{1,0:T(8,128)(2,1)S(1)} %slice_dynamic-update-slice_fusion.refs_4_) | copy-start | bytes 2654212
  39.9 13.2 %collective-permute-start.16 = (bf16[384,1152]{1,0:T(8,128)(2,1)S(1)}, bf16[384,1152]{1,0:T(8,128)(2,1)}, u32[]{:S(2)}, u32[]{:S(2)}) collective-permute-start(bf16[384,1152]{1,0:T(8,128)(2,1)S(1)} %slice_dynamic-update-slice_fusion.2.refs_0_), channel_id=1, source_target_pairs={{0,2},{1,7},{2,0},{3,5},{4,6},{5,3},{6,4},{7,1},{8,10},{9,15},{10,... | collective-permute-start | bytes 2654216 | tf_op jit(solution)/shard_map/ppermute | solution.py:45
  40.3 13.1 %collective-permute-start.19 = (bf16[384,1152]{1,0:T(8,128)(2,1)S(1)}, bf16[384,1152]{1,0:T(8,128)(2,1)}, u32[]{:S(2)}, u32[]{:S(2)}) collective-permute-start(bf16[384,1152]{1,0:T(8,128)(2,1)S(1)} %slice_dynamic-update-slice_fusion.1.refs_2_), channel_id=1, source_target_pairs={{0,32},{1,97},{2,34},{3,99},{4,36},{5,101},{6,38},{7,103},{8,40},{... | collective-permute-start | bytes 2654216 | tf_op jit(solution)/shard_map/ppermute | solution.py:45
  40.8 15.4 %collective-permute-start.22 = (bf16[384,1152]{1,0:T(8,128)(2,1)S(1)}, bf16[384,1152]{1,0:T(8,128)(2,1)S(1)}, u32[]{:S(2)}, u32[]{:S(2)}) collective-permute-start(bf16[384,1152]{1,0:T(8,128)(2,1)S(1)} %slice_dynamic-update-slice_fusion.refs_4_), channel_id=1, source_target_pairs={{0,8},{1,25},{2,10},{3,27},{4,12},{5,29},{6,14},{7,31},{8,0},{9,17... | collective-permute-start | bytes 2654216 | tf_op jit(solution)/shard_map/ppermute | solution.py:45
  49.5 7.6 %collective-permute-start.13 = (bf16[384,1152]{1,0:T(8,128)(2,1)S(1)}, bf16[384,1152]{1,0:T(8,128)(2,1)S(1)}, u32[]{:S(2)}, u32[]{:S(2)}) collective-permute-start(bf16[384,1152]{1,0:T(8,128)(2,1)S(1)} %slice_dynamic-update-slice_fusion.2.refs_0_), channel_id=1, source_target_pairs={{0,1},{1,0},{2,3},{3,2},{4,5},{5,4},{6,7},{7,6},{8,9},{9,8},{10,11... | collective-permute-start | bytes 2654216 | tf_op jit(solution)/shard_map/ppermute | solution.py:49
  49.5 10.1 %collective-permute-start.14 = (bf16[384,1152]{1,0:T(8,128)(2,1)S(1)}, bf16[384,1152]{1,0:T(8,128)(2,1)S(1)}, u32[]{:S(2)}, u32[]{:S(2)}) collective-permute-start(bf16[384,1152]{1,0:T(8,128)(2,1)S(1)} %slice_dynamic-update-slice_fusion.1.refs_2_), channel_id=1, source_target_pairs={{0,1},{1,0},{2,3},{3,2},{4,5},{5,4},{6,7},{7,6},{8,9},{9,8},{10,11... | collective-permute-start | bytes 2654216 | tf_op jit(solution)/shard_map/ppermute | solution.py:49
  53.1 6.5 %collective-permute-start.15 = (bf16[384,1152]{1,0:T(8,128)(2,1)S(1)}, bf16[384,1152]{1,0:T(8,128)(2,1)S(1)}, u32[]{:S(2)}, u32[]{:S(2)}) collective-permute-start(bf16[384,1152]{1,0:T(8,128)(2,1)S(1)} %slice_dynamic-update-slice_fusion.refs_4_), channel_id=1, source_target_pairs={{0,1},{1,0},{2,3},{3,2},{4,5},{5,4},{6,7},{7,6},{8,9},{9,8},{10,11... | collective-permute-start | bytes 2654216 | tf_op jit(solution)/shard_map/ppermute | solution.py:49
  53.5 17.5 %collective-permute-start.17 = (bf16[384,1152]{1,0:T(8,128)(2,1)S(1)}, bf16[384,1152]{1,0:T(8,128)(2,1)S(1)}, u32[]{:S(2)}, u32[]{:S(2)}) collective-permute-start(bf16[384,1152]{1,0:T(8,128)(2,1)S(1)} %slice_dynamic-update-slice_fusion.2.refs_0_), channel_id=1, source_target_pairs={{0,6},{1,3},{2,4},{3,1},{4,2},{5,7},{6,0},{7,5},{8,14},{9,11},{10,... | collective-permute-start | bytes 2654216 | tf_op jit(solution)/shard_map/ppermute | solution.py:45
  56.2 23.2 %copy-start.3 = (bf16[384,1152]{1,0:T(8,128)(2,1)}, bf16[384,1152]{1,0:T(8,128)(2,1)S(1)}, u32[]{:S(2)}) copy-start(bf16[384,1152]{1,0:T(8,128)(2,1)S(1)} %collective-permute-done.22.refs_4_) | copy-start | bytes 2654212
  56.2 14.9 %collective-permute-start.20 = (bf16[384,1152]{1,0:T(8,128)(2,1)S(1)}, bf16[384,1152]{1,0:T(8,128)(2,1)S(1)}, u32[]{:S(2)}, u32[]{:S(2)}) collective-permute-start(bf16[384,1152]{1,0:T(8,128)(2,1)S(1)} %slice_dynamic-update-slice_fusion.1.refs_2_), channel_id=1, source_target_pairs={{0,96},{1,33},{2,98},{3,35},{4,100},{5,37},{6,102},{7,39},{8,104},... | collective-permute-start | bytes 2654216 | tf_op jit(solution)/shard_map/ppermute | solution.py:45
  57.1 3.5 %copy-start.13 = (bf16[384,1152]{1,0:T(8,128)(2,1)}, bf16[384,1152]{1,0:T(8,128)(2,1)S(1)}, u32[]{:S(2)}) copy-start(bf16[384,1152]{1,0:T(8,128)(2,1)S(1)} %collective-permute-done.13.refs_1_) | copy-start | bytes 2654212
  57.1 14.5 %collective-permute-start.23 = (bf16[384,1152]{1,0:T(8,128)(2,1)S(1)}, bf16[384,1152]{1,0:T(8,128)(2,1)S(1)}, u32[]{:S(2)}, u32[]{:S(2)}) collective-permute-start(bf16[384,1152]{1,0:T(8,128)(2,1)S(1)} %slice_dynamic-update-slice_fusion.refs_4_), channel_id=1, source_target_pairs={{0,24},{1,9},{2,26},{3,11},{4,28},{5,13},{6,30},{7,15},{8,16},{9,1... | collective-permute-start | bytes 2654216 | tf_op jit(solution)/shard_map/ppermute | solution.py:45
  59.6 1.2 copy-start.14
  59.6 0.9 copy-start.15
  70.4 2.7 %collective-permute-start.25 = (bf16[384,1152]{1,0:T(8,128)(2,1)}, bf16[384,1152]{1,0:T(8,128)(2,1)S(1)}, u32[]{:S(2)}, u32[]{:S(2)}) collective-permute-start(bf16[384,1152]{1,0:T(8,128)(2,1)} %collective-permute-done.16.refs_0_), channel_id=1, source_target_pairs={{0,1},{1,0},{2,3},{3,2},{4,5},{5,4},{6,7},{7,6},{8,9},{9,8},{10,11... | collective-permute-start | bytes 2654216 | tf_op jit(solution)/shard_map/ppermute | solution.py:49
  70.5 5.2 %collective-permute-start.26 = (bf16[384,1152]{1,0:T(8,128)(2,1)}, bf16[384,1152]{1,0:T(8,128)(2,1)S(1)}, u32[]{:S(2)}, u32[]{:S(2)}) collective-permute-start(bf16[384,1152]{1,0:T(8,128)(2,1)} %collective-permute-done.19.refs_2_), channel_id=1, source_target_pairs={{0,1},{1,0},{2,3},{3,2},{4,5},{5,4},{6,7},{7,6},{8,9},{9,8},{10,11... | collective-permute-start | bytes 2654216 | tf_op jit(solution)/shard_map/ppermute | solution.py:49
  71.0 9.7 %copy-start.4 = (bf16[384,1152]{1,0:T(8,128)(2,1)}, bf16[384,1152]{1,0:T(8,128)(2,1)S(1)}, u32[]{:S(2)}) copy-start(bf16[384,1152]{1,0:T(8,128)(2,1)S(1)} %collective-permute-done.17.refs_6_) | copy-start | bytes 2654212
  71.0 5.8 %collective-permute-start.27 = (bf16[384,1152]{1,0:T(8,128)(2,1)S(1)}, bf16[384,1152]{1,0:T(8,128)(2,1)S(1)}, u32[]{:S(2)}, u32[]{:S(2)}) collective-permute-start(bf16[384,1152]{1,0:T(8,128)(2,1)S(1)} %collective-permute-done.22.refs_4_), channel_id=1, source_target_pairs={{0,1},{1,0},{2,3},{3,2},{4,5},{5,4},{6,7},{7,6},{8,9},{9,8},{10,11... | collective-permute-start | bytes 2654216 | tf_op jit(solution)/shard_map/ppermute | solution.py:49
  71.1 9.6 %copy-start.5 = (bf16[384,1152]{1,0:T(8,128)(2,1)}, bf16[384,1152]{1,0:T(8,128)(2,1)S(1)}, u32[]{:S(2)}) copy-start(bf16[384,1152]{1,0:T(8,128)(2,1)S(1)} %collective-permute-done.20.refs_8_) | copy-start | bytes 2654212
  71.1 8.3 %collective-permute-start.18 = (bf16[384,1152]{1,0:T(8,128)(2,1)S(1)}, bf16[384,1152]{1,0:T(8,128)(2,1)S(1)}, u32[]{:S(2)}, u32[]{:S(2)}) collective-permute-start(bf16[384,1152]{1,0:T(8,128)(2,1)S(1)} %collective-permute-done.17.refs_6_), channel_id=1, source_target_pairs={{0,1},{1,0},{2,3},{3,2},{4,5},{5,4},{6,7},{7,6},{8,9},{9,8},{10,11... | collective-permute-start | bytes 2654216 | tf_op jit(solution)/shard_map/ppermute | solution.py:49
  71.6 9.2 %copy-start.6 = (bf16[384,1152]{1,0:T(8,128)(2,1)}, bf16[384,1152]{1,0:T(8,128)(2,1)S(1)}, u32[]{:S(2)}) copy-start(bf16[384,1152]{1,0:T(8,128)(2,1)S(1)} %collective-permute-done.23.refs_10_) | copy-start | bytes 2654212
  71.6 8.2 %collective-permute-start.21 = (bf16[384,1152]{1,0:T(8,128)(2,1)S(1)}, bf16[384,1152]{1,0:T(8,128)(2,1)S(1)}, u32[]{:S(2)}, u32[]{:S(2)}) collective-permute-start(bf16[384,1152]{1,0:T(8,128)(2,1)S(1)} %collective-permute-done.20.refs_8_), channel_id=1, source_target_pairs={{0,1},{1,0},{2,3},{3,2},{4,5},{5,4},{6,7},{7,6},{8,9},{9,8},{10,11... | collective-permute-start | bytes 2654216 | tf_op jit(solution)/shard_map/ppermute | solution.py:49
  73.2 7.6 %copy-start.7 = (bf16[384,1152]{1,0:T(8,128)(2,1)}, bf16[384,1152]{1,0:T(8,128)(2,1)S(1)}, u32[]{:S(2)}) copy-start(bf16[384,1152]{1,0:T(8,128)(2,1)S(1)} %collective-permute-done.25.refs_7_) | copy-start | bytes 2654212
  73.2 6.6 %collective-permute-start.24 = (bf16[384,1152]{1,0:T(8,128)(2,1)S(1)}, bf16[384,1152]{1,0:T(8,128)(2,1)S(1)}, u32[]{:S(2)}, u32[]{:S(2)}) collective-permute-start(bf16[384,1152]{1,0:T(8,128)(2,1)S(1)} %collective-permute-done.23.refs_10_), channel_id=1, source_target_pairs={{0,1},{1,0},{2,3},{3,2},{4,5},{5,4},{6,7},{7,6},{8,9},{9,8},{10,11... | collective-permute-start | bytes 2654216 | tf_op jit(solution)/shard_map/ppermute | solution.py:49
  75.7 5.0 %copy-start.8 = (bf16[384,1152]{1,0:T(8,128)(2,1)}, bf16[384,1152]{1,0:T(8,128)(2,1)S(1)}, u32[]{:S(2)}) copy-start(bf16[384,1152]{1,0:T(8,128)(2,1)S(1)} %collective-permute-done.26.refs_9_) | copy-start | bytes 2654212
  75.7 16.0 %collective-permute-start.28 = (bf16[384,1152]{1,0:T(8,128)(2,1)}, bf16[384,1152]{1,0:T(8,128)(2,1)}, u32[]{:S(2)}, u32[]{:S(2)}) collective-permute-start(bf16[384,1152]{1,0:T(8,128)(2,1)} %collective-permute-done.16.refs_0_), channel_id=1, source_target_pairs={{0,6},{1,3},{2,4},{3,1},{4,2},{5,7},{6,0},{7,5},{8,14},{9,11},{10,... | collective-permute-start | bytes 2654216 | tf_op jit(solution)/shard_map/ppermute | solution.py:45
  76.9 3.8 %copy-start.9 = (bf16[384,1152]{1,0:T(8,128)(2,1)}, bf16[384,1152]{1,0:T(8,128)(2,1)S(1)}, u32[]{:S(2)}) copy-start(bf16[384,1152]{1,0:T(8,128)(2,1)S(1)} %collective-permute-done.27.refs_11_) | copy-start | bytes 2654212
  76.9 14.9 %collective-permute-start.30 = (bf16[384,1152]{1,0:T(8,128)(2,1)}, bf16[384,1152]{1,0:T(8,128)(2,1)}, u32[]{:S(2)}, u32[]{:S(2)}) collective-permute-start(bf16[384,1152]{1,0:T(8,128)(2,1)} %collective-permute-done.19.refs_2_), channel_id=1, source_target_pairs={{0,96},{1,33},{2,98},{3,35},{4,100},{5,37},{6,102},{7,39},{8,104},... | collective-permute-start | bytes 2654216 | tf_op jit(solution)/shard_map/ppermute | solution.py:45
  79.4 1.3 copy-start.10
  79.4 14.4 %collective-permute-start.32 = (bf16[384,1152]{1,0:T(8,128)(2,1)S(1)}, bf16[384,1152]{1,0:T(8,128)(2,1)}, u32[]{:S(2)}, u32[]{:S(2)}) collective-permute-start(bf16[384,1152]{1,0:T(8,128)(2,1)S(1)} %collective-permute-done.22.refs_4_), channel_id=1, source_target_pairs={{0,24},{1,9},{2,26},{3,11},{4,28},{5,13},{6,30},{7,15},{8,16},{9,1... | collective-permute-start | bytes 2654216 | tf_op jit(solution)/shard_map/ppermute | solution.py:45
  79.7 1.3 copy-start.11
  79.8 1.0 copy-start.12
  91.7 2.7 %collective-permute-start.29 = (bf16[384,1152]{1,0:T(8,128)(2,1)}, bf16[384,1152]{1,0:T(8,128)(2,1)S(1)}, u32[]{:S(2)}, u32[]{:S(2)}) collective-permute-start(bf16[384,1152]{1,0:T(8,128)(2,1)} %collective-permute-done.28.refs_0_), channel_id=1, source_target_pairs={{0,1},{1,0},{2,3},{3,2},{4,5},{5,4},{6,7},{7,6},{8,9},{9,8},{10,11... | collective-permute-start | bytes 2654216 | tf_op jit(solution)/shard_map/ppermute | solution.py:49
  91.8 3.9 %collective-permute-start.31 = (bf16[384,1152]{1,0:T(8,128)(2,1)}, bf16[384,1152]{1,0:T(8,128)(2,1)S(1)}, u32[]{:S(2)}, u32[]{:S(2)}) collective-permute-start(bf16[384,1152]{1,0:T(8,128)(2,1)} %collective-permute-done.30.refs_2_), channel_id=1, source_target_pairs={{0,1},{1,0},{2,3},{3,2},{4,5},{5,4},{6,7},{7,6},{8,9},{9,8},{10,11... | collective-permute-start | bytes 2654216 | tf_op jit(solution)/shard_map/ppermute | solution.py:49
  93.9 3.1 %collective-permute-start.33 = (bf16[384,1152]{1,0:T(8,128)(2,1)}, bf16[384,1152]{1,0:T(8,128)(2,1)S(1)}, u32[]{:S(2)}, u32[]{:S(2)}) collective-permute-start(bf16[384,1152]{1,0:T(8,128)(2,1)} %collective-permute-done.32.refs_4_), channel_id=1, source_target_pairs={{0,1},{1,0},{2,3},{3,2},{4,5},{5,4},{6,7},{7,6},{8,9},{9,8},{10,11... | collective-permute-start | bytes 2654216 | tf_op jit(solution)/shard_map/ppermute | solution.py:49
  94.4 2.5 %copy-start.16 = (bf16[384,1152]{1,0:T(8,128)(2,1)}, bf16[384,1152]{1,0:T(8,128)(2,1)S(1)}, u32[]{:S(2)}) copy-start(bf16[384,1152]{1,0:T(8,128)(2,1)S(1)} %collective-permute-done.29.refs_1_) | copy-start | bytes 2654212
  95.7 1.3 copy-start.17
  96.9 0.9 copy-start.18
